TPU v7x, 32 devices: a whole 2x2x4 slice. The times are simulated.
32 devices in a mesh: ctx: 8 (over y, x, core), roll: 4 (over z).
Axes of the slice: x: 2, y: 2, z: 4, core: 2. Of those that a mesh axis runs over, the one named last changes fastest.
Arguments:
- prompt_query: bfloat16 [1024, 8192], P('ctx', 'roll'), may hold values from -3 to 3
- prompt_key_rows: bfloat16 [1024, 1024], P('ctx', 'roll'), may hold values from -3 to 3
- prompt_value_rows: bfloat16 [1024, 1024], P('ctx', 'roll'), may hold values from -4 to 4
- prompt_dout: bfloat16 [1024, 8192], P('ctx', 'roll'), may hold values from -72 to 72
- prompt_out: bfloat16 [1024, 8192], P('ctx', 'roll'), may hold values from -3 to 3
- prompt_lse: bfloat16 [1024, 64], P('ctx', 'roll'), may hold values from 7.5 to 9.5
- roll_query: bfloat16 [1024, 8192], P(('ctx', 'roll')), may hold values from -3 to 3
- rollout_key_rows: bfloat16 [1024, 1024], P(('ctx', 'roll')), may hold values from -3 to 3
- rollout_value_rows: bfloat16 [1024, 1024], P(('ctx', 'roll')), may hold values from -4 to 4
- roll_dout: bfloat16 [1024, 8192], P(('ctx', 'roll')), may hold values from -72 to 72
- roll_out: bfloat16 [1024, 8192], P(('ctx', 'roll')), may hold values from -3 to 3
- roll_lse: bfloat16 [1024, 64], P(('ctx', 'roll')), may hold values from 7.5 to 9.5
Outputs:
- prompt_dq: bfloat16 [1024, 8192], P('ctx', 'roll')
- prompt_dk: bfloat16 [1024, 1024], P('ctx', 'roll')
- prompt_dv: bfloat16 [1024, 1024], P('ctx', 'roll')
- roll_dq: bfloat16 [1024, 8192], P(('ctx', 'roll'))
- roll_dk: bfloat16 [1024, 1024], P(('ctx', 'roll'))
- roll_dv: bfloat16 [1024, 1024], P(('ctx', 'roll'))
All inputs are finite; a program needn't handle non-finite values.
Results may differ from a plain program's by a relative error of at most 0.0095.
Values may be sent and summed in bfloat16 or wider, within the bound.
No kernel may reach another device: no remote copies, remote signals or barrier semaphores. Data moves between devices by JAX's collectives and lax.ppermute only.
A program may use at most 64 MiB of HBM per device.

v0:
```python
import math

import jax
import jax.numpy as jnp
from jax import lax
from jax.sharding import PartitionSpec as P

HEAD_SIZE = 128


def positions(row_ids, half_rows, cycle_count):
    block_index = row_ids // half_rows
    pair_index = block_index // 2
    offset = row_ids % half_rows
    return jnp.where(
        block_index % 2 == 0,
        pair_index * half_rows + offset,
        (2 * cycle_count - 1 - pair_index) * half_rows + offset,
    )


def head_sums(grad_out, outputs):
    product = grad_out.astype(jnp.float32) * outputs.astype(jnp.float32)
    return product.reshape(product.shape[0], -1, HEAD_SIZE).sum(axis=2)


def tile_grads(queries, grad_out, log_sums, delta_sums, query_pos, key_tile, value_tile, key_pos):
    query_rows = queries.shape[0]
    key_rows = key_tile.shape[0]
    groups = key_tile.shape[1] // HEAD_SIZE
    group_members = queries.shape[1] // (groups * HEAD_SIZE)
    scaling = 1.0 / math.sqrt(HEAD_SIZE)
    query_heads = queries.reshape(query_rows, groups, group_members, HEAD_SIZE)
    grad_heads = grad_out.reshape(query_rows, groups, group_members, HEAD_SIZE)
    key_heads = key_tile.reshape(key_rows, groups, HEAD_SIZE)
    value_heads = value_tile.reshape(key_rows, groups, HEAD_SIZE)
    scores = (
        jnp.einsum("qgmd,kgd->gmqk", query_heads, key_heads, preferred_element_type=jnp.float32)
        * scaling
    )
    lse_cols = (
        log_sums.astype(jnp.float32)
        .reshape(query_rows, groups, group_members)
        .transpose(1, 2, 0)[..., None]
    )
    delta_cols = delta_sums.reshape(query_rows, groups, group_members).transpose(1, 2, 0)[..., None]
    allowed = key_pos[None, :] <= query_pos[:, None]
    probs = jnp.where(allowed, jnp.exp(scores - lse_cols), 0.0)
    grad_probs = jnp.einsum(
        "qgmd,kgd->gmqk", grad_heads, value_heads, preferred_element_type=jnp.float32
    )
    grad_scores = (probs * (grad_probs - delta_cols)).astype(jnp.bfloat16)
    grad_query = None
    grad_key = None
    grad_value = None
    grad_query = (
        jnp.einsum(
            "gmqk,kgd->qgmd", grad_scores, key_heads, preferred_element_type=jnp.float32
        ).reshape(query_rows, -1)
        * scaling
    )
    probs_low = probs.astype(jnp.bfloat16)
    grad_key = (
        jnp.einsum(
            "gmqk,qgmd->kgd", grad_scores, query_heads, preferred_element_type=jnp.float32
        ).reshape(key_rows, -1)
        * scaling
    )
    grad_value = jnp.einsum(
        "gmqk,qgmd->kgd", probs_low, grad_heads, preferred_element_type=jnp.float32
    ).reshape(key_rows, -1)
    return (grad_query, grad_key, grad_value)


def sweep(
    queries, grad_out, log_sums, delta_sums, query_pos, key_tile, value_tile, half_rows, cycle_count
):
    key_rows = key_tile.shape[0]
    tile_rows = math.gcd(key_rows, 256)
    key_pos = positions(jnp.arange(key_rows, dtype=jnp.int32), half_rows, cycle_count)
    stacked = (
        key_tile.reshape(key_rows // tile_rows, tile_rows, -1),
        value_tile.reshape(key_rows // tile_rows, tile_rows, -1),
        key_pos.reshape(-1, tile_rows),
    )

    def key_step(running, pieces):
        grad_query, grad_key, grad_value = tile_grads(
            queries, grad_out, log_sums, delta_sums, query_pos, pieces[0], pieces[1], pieces[2]
        )
        running = running + grad_query
        return (running, (grad_key, grad_value))

    running = jnp.zeros((queries.shape[0], queries.shape[1]), jnp.float32)
    running, (grad_key, grad_value) = lax.scan(key_step, running, stacked)
    grad_key = grad_key.reshape(key_rows, -1)
    grad_value = grad_value.reshape(key_rows, -1)
    return (running, grad_key, grad_value)


def on_device(
    prompt_query,
    prompt_key_rows,
    prompt_value_rows,
    prompt_dout,
    prompt_out,
    prompt_lse,
    roll_query,
    rollout_key_rows,
    rollout_value_rows,
    roll_dout,
    roll_out,
    roll_lse,
):
    cycle_count = lax.axis_size("ctx")
    my_index = lax.axis_index("ctx")
    prompt_rows = prompt_query.shape[0]
    half_rows = prompt_rows // 2
    prompt_total = prompt_rows * cycle_count
    roll_queries, roll_keys, roll_values, roll_grads, roll_outputs, roll_sums = (
        lax.all_to_all(roll_query, "roll", split_axis=1, concat_axis=0, tiled=True),
        lax.all_to_all(rollout_key_rows, "roll", split_axis=1, concat_axis=0, tiled=True),
        lax.all_to_all(rollout_value_rows, "roll", split_axis=1, concat_axis=0, tiled=True),
        lax.all_to_all(roll_dout, "roll", split_axis=1, concat_axis=0, tiled=True),
        lax.all_to_all(roll_out, "roll", split_axis=1, concat_axis=0, tiled=True),
        lax.all_to_all(roll_lse, "roll", split_axis=1, concat_axis=0, tiled=True),
    )
    roll_rows = roll_queries.shape[0]
    prompt_pos = positions(
        my_index * prompt_rows + jnp.arange(prompt_rows, dtype=jnp.int32), half_rows, cycle_count
    )
    queries = jnp.concatenate([prompt_query, roll_queries], 0)
    grad_out = jnp.concatenate([prompt_dout, roll_grads], 0)
    log_sums = jnp.concatenate([prompt_lse, roll_sums], 0)
    delta_sums = head_sums(grad_out, jnp.concatenate([prompt_out, roll_outputs], 0))
    query_pos = jnp.concatenate([prompt_pos, jnp.full((roll_rows,), prompt_total, jnp.int32)])
    places = jnp.arange(roll_rows, dtype=jnp.int32)
    own_query, roll_keygrad, roll_valgrad = tile_grads(
        roll_queries,
        roll_grads,
        roll_sums,
        delta_sums[prompt_rows:],
        places,
        roll_keys,
        roll_values,
        places,
    )
    keys_all, values_all = (
        lax.all_gather(prompt_key_rows, "ctx", axis=0, tiled=True),
        lax.all_gather(prompt_value_rows, "ctx", axis=0, tiled=True),
    )
    query_grads, key_part, value_part = sweep(
        queries,
        grad_out,
        log_sums,
        delta_sums,
        query_pos,
        keys_all,
        values_all,
        half_rows,
        cycle_count,
    )
    key_owned, value_owned = (
        lax.psum_scatter(key_part, "ctx", scatter_dimension=0, tiled=True),
        lax.psum_scatter(value_part, "ctx", scatter_dimension=0, tiled=True),
    )
    prompt_grad = query_grads[:prompt_rows].astype(jnp.bfloat16)
    roll_total = (query_grads[prompt_rows:] + own_query).astype(jnp.bfloat16)
    back_query, back_key, back_value = (
        lax.all_to_all(roll_total, "roll", split_axis=0, concat_axis=1, tiled=True),
        lax.all_to_all(
            roll_keygrad.astype(jnp.bfloat16), "roll", split_axis=0, concat_axis=1, tiled=True
        ),
        lax.all_to_all(
            roll_valgrad.astype(jnp.bfloat16), "roll", split_axis=0, concat_axis=1, tiled=True
        ),
    )
    return (
        prompt_grad,
        key_owned.astype(jnp.bfloat16),
        value_owned.astype(jnp.bfloat16),
        back_query,
        back_key,
        back_value,
    )


def solution(mesh):
    placed = (
        P("ctx", "roll"),
        P("ctx", "roll"),
        P("ctx", "roll"),
        P("ctx", "roll"),
        P("ctx", "roll"),
        P("ctx", "roll"),
        P(("ctx", "roll"), None),
        P(("ctx", "roll"), None),
        P(("ctx", "roll"), None),
        P(("ctx", "roll"), None),
        P(("ctx", "roll"), None),
        P(("ctx", "roll"), None),
    )
    return jax.shard_map(
        on_device,
        mesh=mesh,
        in_specs=placed,
        out_specs=(
            P("ctx", "roll"),
            P("ctx", "roll"),
            P("ctx", "roll"),
            P(("ctx", "roll"), None),
            P(("ctx", "roll"), None),
            P(("ctx", "roll"), None),
        ),
        check_vma=False,
    )
```

profile of v0, /device:TPU:0, one launch (start us, length us, event | category | flops | bytes accessed | tf_op | source)
XLA Modules:
  0.0 217.3 jit_solution(15056542794766125692)
XLA Ops:
  8.7 6.3 %all-to-all-start.1 = ((bf16[4,2,256]{2,1,0:T(2,128)(2,1)}), bf16[4,2,256]{2,1,0:T(2,128)(2,1)S(1)}, u32[]{:S(2)}, u32[]{:S(2)}) async-start(bf16[4,2,256]{2,1,0:T(2,128)(2,1)} %reshape.172), calls=%async_computation.1 | async-start | bytes 8192 | tf_op jit(solution)/shard_map/all_to_all | solution.py:126
  15.0 1.9 copy.245
  17.0 3.6 %all-to-all-done.1 = bf16[4,2,256]{2,1,0:T(2,128)(2,1)S(1)} async-done(((bf16[4,2,256]{2,1,0:T(2,128)(2,1)}), bf16[4,2,256]{2,1,0:T(2,128)(2,1)S(1)}, u32[]{:S(2)}, u32[]{:S(2)}) %all-to-all-start.1) | async-done | bytes 4128 | tf_op jit(solution)/shard_map/all_to_all | solution.py:126
  20.6 3.6 %all-to-all-start.2 = ((bf16[32,4,2048]{2,0,1:T(8,128)(2,1)}), bf16[32,4,2048]{2,0,1:T(8,128)(2,1)S(1)}, u32[]{:S(2)}, u32[]{:S(2)}) async-start(bf16[32,4,2048]{2,0,1:T(8,128)(2,1)} %bitcast.187), calls=%async_computation.2 | async-start | bytes 1048576 | tf_op jit(solution)/shard_map/all_to_all | solution.py:124
  25.1 12.5 %all-to-all-done.2 = bf16[32,4,2048]{2,0,1:T(8,128)(2,1)S(1)} async-done(((bf16[32,4,2048]{2,0,1:T(8,128)(2,1)}), bf16[32,4,2048]{2,0,1:T(8,128)(2,1)S(1)}, u32[]{:S(2)}, u32[]{:S(2)}) %all-to-all-start.2) | async-done | bytes 524320 | tf_op jit(solution)/shard_map/all_to_all | solution.py:124
  37.5 3.6 %all-to-all-start.3 = ((bf16[32,4,2048]{2,0,1:T(8,128)(2,1)}), bf16[32,4,2048]{2,0,1:T(8,128)(2,1)S(1)}, u32[]{:S(2)}, u32[]{:S(2)}) async-start(bf16[32,4,2048]{2,0,1:T(8,128)(2,1)} %bitcast.186), calls=%async_computation.3 | async-start | bytes 1048576 | tf_op jit(solution)/shard_map/all_to_all | solution.py:125
  42.3 9.9 %all_gather.6 = bf16[1024,256]{1,0:T(8,128)(2,1)S(1)} all-gather(bf16[128,256]{1,0:T(8,128)(2,1)S(1)} %copy-done.27), channel_id=1, replica_groups=mesh['ctx'=8,'roll'=4] {'ctx'}, dimensions={0}, use_global_device_ids=true | all-gather | bytes 589824 | tf_op jit(solution)/shard_map/all_gather | solution.py:149
  52.2 9.8 %all_gather.7 = bf16[1024,256]{1,0:T(8,128)(2,1)S(1)} all-gather(bf16[128,256]{1,0:T(8,128)(2,1)S(1)} %copy-done.28), channel_id=1, replica_groups=mesh['ctx'=8,'roll'=4] {'ctx'}, dimensions={0}, use_global_device_ids=true | all-gather | bytes 589824 | tf_op jit(solution)/shard_map/all_gather | solution.py:150
  62.8 5.0 %all-to-all-start = ((bf16[32,4,2048]{2,0,1:T(8,128)(2,1)}), bf16[32,4,2048]{2,0,1:T(8,128)(2,1)S(1)}, u32[]{:S(2)}, u32[]{:S(2)}) async-start(bf16[32,4,2048]{2,0,1:T(8,128)(2,1)} %bitcast.260), calls=%async_computation | async-start | bytes 1048576 | tf_op jit(solution)/shard_map/all_to_all | solution.py:121
  68.2 1.3 copy.226
  71.4 1.3 copy.158
  72.7 10.1 %all-to-all-done = bf16[32,4,2048]{2,0,1:T(8,128)(2,1)S(1)} async-done(((bf16[32,4,2048]{2,0,1:T(8,128)(2,1)}), bf16[32,4,2048]{2,0,1:T(8,128)(2,1)S(1)}, u32[]{:S(2)}, u32[]{:S(2)}) %all-to-all-start) | async-done | bytes 524320 | tf_op jit(solution)/shard_map/all_to_all | solution.py:121
  84.3 51.0 %while.15 = (s32[]{:T(128)}, f32[256,2048]{0,1:T(8,128)}, f32[4,256,256]{2,1,0:T(8,128)}, f32[4,256,256]{2,1,0:T(8,128)}, bf16[4,256,256]{2,1,0:T(8,128)(2,1)S(1...) while((s32[]{:T(128)}, f32[256,2048]{0,1:T(8,128)}, ...), condition=%wide.region_2.3_spmd.clone, body=%wide.region_1.2_spmd.clone.sunk | while | flops 1354371072 | bytes 66704000 | solution.py:95
  86.0 1.7 fusion.75
  87.7 2.3 %fusion.74 = bf16[2,8,256,256]{2,3,1,0:T(8,128)(2,1)S(1)} fusion(f32[2,256,256,8]{2,1,3,0:T(8,128)S(1)} %fusion.73, bf16[256,2,128,1]{0,2,3,1:T(8,128)(2,1)S(1)} %bitcast.253, bf16[256,2,8,128]{0,3,2,1:T(8,128)(2,1)S(1)} %bitcast.264, f32[2,8,256]{2,1,0:T(8,128)} %bitcast.287, f32[2,8,256]{2,1,0:T(8,128)S(1)} %convert_bitcast_fusion.2, ...), kind=kOutput, calls=%fused_computation.2.clone.1 | convolution fusion | flops 274726912 | bytes 7569408 | tf_op jit(solution)/shard_map/while/body/eval_jaxpr/qgmd,kgd->gmqk/dot_general | solution.py:49
  91.0 1.5 fusion.76
  94.7 1.3 copy-done.1
  98.8 1.7 fusion.75
  100.4 2.3 %fusion.74 = bf16[2,8,256,256]{2,3,1,0:T(8,128)(2,1)S(1)} fusion(f32[2,256,256,8]{2,1,3,0:T(8,128)S(1)} %fusion.73, bf16[256,2,128,1]{0,2,3,1:T(8,128)(2,1)S(1)} %bitcast.253, bf16[256,2,8,128]{0,3,2,1:T(8,128)(2,1)S(1)} %bitcast.264, f32[2,8,256]{2,1,0:T(8,128)} %bitcast.287, f32[2,8,256]{2,1,0:T(8,128)S(1)} %convert_bitcast_fusion.2, ...), kind=kOutput, calls=%fused_computation.2.clone.1 | convolution fusion | flops 274726912 | bytes 7569408 | tf_op jit(solution)/shard_map/while/body/eval_jaxpr/qgmd,kgd->gmqk/dot_general | solution.py:49
  103.8 1.5 fusion.76
  107.4 1.3 copy-done.1
  111.5 1.7 fusion.75
  113.2 2.3 %fusion.74 = bf16[2,8,256,256]{2,3,1,0:T(8,128)(2,1)S(1)} fusion(f32[2,256,256,8]{2,1,3,0:T(8,128)S(1)} %fusion.73, bf16[256,2,128,1]{0,2,3,1:T(8,128)(2,1)S(1)} %bitcast.253, bf16[256,2,8,128]{0,3,2,1:T(8,128)(2,1)S(1)} %bitcast.264, f32[2,8,256]{2,1,0:T(8,128)} %bitcast.287, f32[2,8,256]{2,1,0:T(8,128)S(1)} %convert_bitcast_fusion.2, ...), kind=kOutput, calls=%fused_computation.2.clone.1 | convolution fusion | flops 274726912 | bytes 7569408 | tf_op jit(solution)/shard_map/while/body/eval_jaxpr/qgmd,kgd->gmqk/dot_general | solution.py:49
  116.5 1.5 fusion.76
  120.2 1.3 copy-done.1
  124.3 1.7 fusion.75
  125.9 2.3 %fusion.74 = bf16[2,8,256,256]{2,3,1,0:T(8,128)(2,1)S(1)} fusion(f32[2,256,256,8]{2,1,3,0:T(8,128)S(1)} %fusion.73, bf16[256,2,128,1]{0,2,3,1:T(8,128)(2,1)S(1)} %bitcast.253, bf16[256,2,8,128]{0,3,2,1:T(8,128)(2,1)S(1)} %bitcast.264, f32[2,8,256]{2,1,0:T(8,128)} %bitcast.287, f32[2,8,256]{2,1,0:T(8,128)S(1)} %convert_bitcast_fusion.2, ...), kind=kOutput, calls=%fused_computation.2.clone.1 | convolution fusion | flops 274726912 | bytes 7569408 | tf_op jit(solution)/shard_map/while/body/eval_jaxpr/qgmd,kgd->gmqk/dot_general | solution.py:49
  129.3 1.5 fusion.76
  132.9 1.3 copy-done.1
  135.4 1.6 copy.248
  136.9 3.3 %all-to-all-start.4 = ((bf16[32,4,256]{2,0,1:T(8,128)(2,1)}), bf16[32,4,256]{2,0,1:T(8,128)(2,1)S(1)}, u32[]{:S(2)}, u32[]{:S(2)}) async-start(bf16[32,4,256]{2,0,1:T(8,128)(2,1)} %bitcast.190), calls=%async_computation.6 | async-start | bytes 131072 | tf_op jit(solution)/shard_map/all_to_all | solution.py:122
  140.2 1.5 copy.247
  141.7 4.2 %all-to-all-done.4 = bf16[32,4,256]{2,0,1:T(8,128)(2,1)S(1)} async-done(((bf16[32,4,256]{2,0,1:T(8,128)(2,1)}), bf16[32,4,256]{2,0,1:T(8,128)(2,1)S(1)}, u32[]{:S(2)}, u32[]{:S(2)}) %all-to-all-start.4) | async-done | bytes 65568 | tf_op jit(solution)/shard_map/all_to_all | solution.py:122
  145.9 3.3 %all-to-all-start.5 = ((bf16[32,4,256]{2,0,1:T(8,128)(2,1)}), bf16[32,4,256]{2,0,1:T(8,128)(2,1)S(1)}, u32[]{:S(2)}, u32[]{:S(2)}) async-start(bf16[32,4,256]{2,0,1:T(8,128)(2,1)} %bitcast.189), calls=%async_computation.7 | async-start | bytes 131072 | tf_op jit(solution)/shard_map/all_to_all | solution.py:123
  150.2 4.7 %all-to-all-done.5 = bf16[32,4,256]{2,0,1:T(8,128)(2,1)S(1)} async-done(((bf16[32,4,256]{2,0,1:T(8,128)(2,1)}), bf16[32,4,256]{2,0,1:T(8,128)(2,1)S(1)}, u32[]{:S(2)}, u32[]{:S(2)}) %all-to-all-start.5) | async-done | bytes 65568 | tf_op jit(solution)/shard_map/all_to_all | solution.py:123
  156.7 3.3 %all-to-all-start.8 = ((bf16[4,32,256]{2,1,0:T(8,128)(2,1)}), bf16[4,32,256]{2,1,0:T(8,128)(2,1)S(1)}, u32[]{:S(2)}, u32[]{:S(2)}) async-start(bf16[4,32,256]{2,1,0:T(8,128)(2,1)} %convert_element_type.73), calls=%async_computation.10 | async-start | bytes 131072 | tf_op jit(solution)/shard_map/all_to_all | solution.py:174
  162.4 1.5 fusion.22
  164.6 1.6 copy.174
  166.2 1.8 copy.160
  168.1 5.0 %all-to-all-start.7 = ((bf16[4,32,256]{2,1,0:T(8,128)(2,1)}), bf16[4,32,256]{2,1,0:T(8,128)(2,1)S(1)}, u32[]{:S(2)}, u32[]{:S(2)}) async-start(bf16[4,32,256]{2,1,0:T(8,128)(2,1)} %convert_element_type.69), calls=%async_computation.9 | async-start | bytes 131072 | tf_op jit(solution)/shard_map/all_to_all | solution.py:171
  173.1 2.1 fusion.23
  175.2 3.6 %all-to-all-done.7 = bf16[4,32,256]{2,1,0:T(8,128)(2,1)S(1)} async-done(((bf16[4,32,256]{2,1,0:T(8,128)(2,1)}), bf16[4,32,256]{2,1,0:T(8,128)(2,1)S(1)}, u32[]{:S(2)}, u32[]{:S(2)}) %all-to-all-start.7) | async-done | bytes 65568 | tf_op jit(solution)/shard_map/all_to_all | solution.py:171
  178.8 3.5 %all-to-all-start.6 = ((bf16[4,32,2048]{2,1,0:T(8,128)(2,1)}), bf16[4,32,2048]{2,1,0:T(8,128)(2,1)S(1)}, u32[]{:S(2)}, u32[]{:S(2)}) async-start(bf16[4,32,2048]{2,1,0:T(8,128)(2,1)} %bitcast.23), calls=%async_computation.8 | async-start | bytes 1048576 | tf_op jit(solution)/shard_map/all_to_all | solution.py:170
  182.3 2.1 slice.20
  185.7 6.9 %all-to-all-done.6 = bf16[4,32,2048]{2,1,0:T(8,128)(2,1)S(1)} async-done(((bf16[4,32,2048]{2,1,0:T(8,128)(2,1)}), bf16[4,32,2048]{2,1,0:T(8,128)(2,1)S(1)}, u32[]{:S(2)}, u32[]{:S(2)}) %all-to-all-start.6) | async-done | bytes 524320 | tf_op jit(solution)/shard_map/all_to_all | solution.py:170
  193.4 1.5 convert_element_type.63
  194.9 14.0 %reduce-scatter.3.cloned.1.call-done = f32[128,256]{1,0:T(8,128)} async-done(((f32[1024,256]{1,0:T(8,128)}), f32[128,256]{1,0:T(8,128)}) %reduce-scatter.3.cloned.1.call-update) | async-done | bytes 131088 | tf_op jit(solution)/shard_map/reduce_scatter | solution.py:164
  208.9 1.5 convert_element_type.62
  (274 shorter events, 38.5 us)
Async XLA Ops:
  7.2 17.1 %copy-start.18 = (bf16[32,8192]{1,0:T(8,128)(2,1)S(1)}, bf16[32,8192]{1,0:T(8,128)(2,1)}, u32[]{:S(2)}) copy-start(bf16[32,8192]{1,0:T(8,128)(2,1)} %param.24) | copy-start | bytes 1572868
  8.7 11.9 %all-to-all-start.1 = ((bf16[4,2,256]{2,1,0:T(2,128)(2,1)}), bf16[4,2,256]{2,1,0:T(2,128)(2,1)S(1)}, u32[]{:S(2)}, u32[]{:S(2)}) async-start(bf16[4,2,256]{2,1,0:T(2,128)(2,1)} %reshape.172), calls=%async_computation.1 | async-start | bytes 8192 | tf_op jit(solution)/shard_map/all_to_all | solution.py:126
  15.0 26.2 %copy-start.19 = (bf16[128,2048]{1,0:T(8,128)(2,1)S(1)}, bf16[128,2048]{1,0:T(8,128)(2,1)}, u32[]{:S(2)}) copy-start(bf16[128,2048]{1,0:T(8,128)(2,1)} %param.18) | copy-start | bytes 1572868
  20.6 20.7 %copy-start.20 = (bf16[32,8192]{1,0:T(8,128)(2,1)S(1)}, bf16[32,8192]{1,0:T(8,128)(2,1)}, u32[]{:S(2)}) copy-start(bf16[32,8192]{1,0:T(8,128)(2,1)} %param.20) | copy-start | bytes 1572868
  20.6 16.9 %all-to-all-start.2 = ((bf16[32,4,2048]{2,0,1:T(8,128)(2,1)}), bf16[32,4,2048]{2,0,1:T(8,128)(2,1)S(1)}, u32[]{:S(2)}, u32[]{:S(2)}) async-start(bf16[32,4,2048]{2,0,1:T(8,128)(2,1)} %bitcast.187), calls=%async_computation.2 | async-start | bytes 1048576 | tf_op jit(solution)/shard_map/all_to_all | solution.py:124
  24.2 17.9 %copy-start.14 = (bf16[128,2048]{1,0:T(8,128)(2,1)S(1)}, bf16[128,2048]{1,0:T(8,128)(2,1)}, u32[]{:S(2)}) copy-start(bf16[128,2048]{1,0:T(8,128)(2,1)} %param.17) | copy-start | bytes 1572868
  37.5 4.8 %copy-start.27 = (bf16[128,256]{1,0:T(8,128)(2,1)S(1)}, bf16[128,256]{1,0:T(8,128)(2,1)}, u32[]{:S(2)}) copy-start(bf16[128,256]{1,0:T(8,128)(2,1)} %param.15) | copy-start | bytes 196612
  37.5 24.5 %all-to-all-start.3 = ((bf16[32,4,2048]{2,0,1:T(8,128)(2,1)}), bf16[32,4,2048]{2,0,1:T(8,128)(2,1)S(1)}, u32[]{:S(2)}, u32[]{:S(2)}) async-start(bf16[32,4,2048]{2,0,1:T(8,128)(2,1)} %bitcast.186), calls=%async_computation.3 | async-start | bytes 1048576 | tf_op jit(solution)/shard_map/all_to_all | solution.py:125
  41.1 11.1 %copy-start.28 = (bf16[128,256]{1,0:T(8,128)(2,1)S(1)}, bf16[128,256]{1,0:T(8,128)(2,1)}, u32[]{:S(2)}) copy-start(bf16[128,256]{1,0:T(8,128)(2,1)} %param.16) | copy-start | bytes 196612
  41.3 26.7 %copy-start.35 = (bf16[128,16]{0,1:T(8,128)(2,1)S(1)}, bf16[128,16]{0,1:T(8,128)(2,1)}, u32[]{:S(2)}) copy-start(bf16[128,16]{0,1:T(8,128)(2,1)} %param.19) | copy-start | bytes 12292
  62.8 20.0 %all-to-all-start = ((bf16[32,4,2048]{2,0,1:T(8,128)(2,1)}), bf16[32,4,2048]{2,0,1:T(8,128)(2,1)S(1)}, u32[]{:S(2)}, u32[]{:S(2)}) async-start(bf16[32,4,2048]{2,0,1:T(8,128)(2,1)} %bitcast.260), calls=%async_computation | async-start | bytes 1048576 | tf_op jit(solution)/shard_map/all_to_all | solution.py:121
  67.8 125.5 %reduce-scatter.5.cloned.1.call-start = ((), (), s32[]{:S(2)}) async-start(), calls=%async_computation.12 | async-start | bytes 1179648 | tf_op jit(solution)/shard_map/reduce_scatter | solution.py:165
  71.4 12.2 %copy-start.23 = (bf16[128,2048]{1,0:T(8,128)(2,1)S(1)}, bf16[128,2048]{1,0:T(8,128)(2,1)}, u32[]{:S(2)}) copy-start(bf16[128,2048]{1,0:T(8,128)(2,1)} %param.14) | copy-start | bytes 1572868
  94.2 2.8 %copy-start.9 = (bf16[4,256,256]{2,1,0:T(8,128)(2,1)S(1)}, bf16[4,256,256]{2,1,0:T(8,128)(2,1)}, u32[]{:S(2)}) copy-start(bf16[4,256,256]{2,1,0:T(8,128)(2,1)} %copy-done.8) | copy-start | bytes 1572868 | tf_op jit(solution)/shard_map/while
  94.2 2.8 %copy-start.11 = (bf16[4,256,256]{2,1,0:T(8,128)(2,1)S(1)}, bf16[4,256,256]{2,1,0:T(8,128)(2,1)}, u32[]{:S(2)}) copy-start(bf16[4,256,256]{2,1,0:T(8,128)(2,1)} %copy-done.10) | copy-start | bytes 1572868 | tf_op jit(solution)/shard_map/while
  94.2 2.8 %copy-start.25 = (bf16[256,16]{0,1:T(8,128)(2,1)S(1)}, bf16[256,16]{0,1:T(8,128)(2,1)}, u32[]{:S(2)}) copy-start(bf16[256,16]{0,1:T(8,128)(2,1)} %copy-done.24) | copy-start | bytes 24580 | tf_op jit(solution)/shard_map/while
  94.2 2.8 %copy-start.30 = (s32[256]{0:T(256)S(1)}, s32[256]{0:T(256)}, u32[]{:S(2)}) copy-start(s32[256]{0:T(256)} %copy-done.29) | copy-start | bytes 3076 | tf_op jit(solution)/shard_map/while
  94.2 2.8 %copy-start.32 = (s32[4,256]{1,0:T(4,128)S(1)}, s32[4,256]{1,0:T(4,128)}, u32[]{:S(2)}) copy-start(s32[4,256]{1,0:T(4,128)} %copy-done.31) | copy-start | bytes 12292 | tf_op jit(solution)/shard_map/while
  94.2 2.8 %copy-start.34 = (f32[256,16]{0,1:T(8,128)S(1)}, f32[256,16]{0,1:T(8,128)}, u32[]{:S(2)}) copy-start(f32[256,16]{0,1:T(8,128)} %copy-done.33) | copy-start | bytes 49156 | tf_op jit(solution)/shard_map/while
  106.9 2.8 %copy-start.9 = (bf16[4,256,256]{2,1,0:T(8,128)(2,1)S(1)}, bf16[4,256,256]{2,1,0:T(8,128)(2,1)}, u32[]{:S(2)}) copy-start(bf16[4,256,256]{2,1,0:T(8,128)(2,1)} %copy-done.8) | copy-start | bytes 1572868 | tf_op jit(solution)/shard_map/while
  106.9 2.8 %copy-start.11 = (bf16[4,256,256]{2,1,0:T(8,128)(2,1)S(1)}, bf16[4,256,256]{2,1,0:T(8,128)(2,1)}, u32[]{:S(2)}) copy-start(bf16[4,256,256]{2,1,0:T(8,128)(2,1)} %copy-done.10) | copy-start | bytes 1572868 | tf_op jit(solution)/shard_map/while
  106.9 2.8 %copy-start.25 = (bf16[256,16]{0,1:T(8,128)(2,1)S(1)}, bf16[256,16]{0,1:T(8,128)(2,1)}, u32[]{:S(2)}) copy-start(bf16[256,16]{0,1:T(8,128)(2,1)} %copy-done.24) | copy-start | bytes 24580 | tf_op jit(solution)/shard_map/while
  106.9 2.8 %copy-start.30 = (s32[256]{0:T(256)S(1)}, s32[256]{0:T(256)}, u32[]{:S(2)}) copy-start(s32[256]{0:T(256)} %copy-done.29) | copy-start | bytes 3076 | tf_op jit(solution)/shard_map/while
  106.9 2.8 %copy-start.32 = (s32[4,256]{1,0:T(4,128)S(1)}, s32[4,256]{1,0:T(4,128)}, u32[]{:S(2)}) copy-start(s32[4,256]{1,0:T(4,128)} %copy-done.31) | copy-start | bytes 12292 | tf_op jit(solution)/shard_map/while
  106.9 2.8 %copy-start.34 = (f32[256,16]{0,1:T(8,128)S(1)}, f32[256,16]{0,1:T(8,128)}, u32[]{:S(2)}) copy-start(f32[256,16]{0,1:T(8,128)} %copy-done.33) | copy-start | bytes 49156 | tf_op jit(solution)/shard_map/while
  119.7 2.8 %copy-start.9 = (bf16[4,256,256]{2,1,0:T(8,128)(2,1)S(1)}, bf16[4,256,256]{2,1,0:T(8,128)(2,1)}, u32[]{:S(2)}) copy-start(bf16[4,256,256]{2,1,0:T(8,128)(2,1)} %copy-done.8) | copy-start | bytes 1572868 | tf_op jit(solution)/shard_map/while
  119.7 2.8 %copy-start.11 = (bf16[4,256,256]{2,1,0:T(8,128)(2,1)S(1)}, bf16[4,256,256]{2,1,0:T(8,128)(2,1)}, u32[]{:S(2)}) copy-start(bf16[4,256,256]{2,1,0:T(8,128)(2,1)} %copy-done.10) | copy-start | bytes 1572868 | tf_op jit(solution)/shard_map/while
  119.7 2.8 %copy-start.25 = (bf16[256,16]{0,1:T(8,128)(2,1)S(1)}, bf16[256,16]{0,1:T(8,128)(2,1)}, u32[]{:S(2)}) copy-start(bf16[256,16]{0,1:T(8,128)(2,1)} %copy-done.24) | copy-start | bytes 24580 | tf_op jit(solution)/shard_map/while
  119.7 2.8 %copy-start.30 = (s32[256]{0:T(256)S(1)}, s32[256]{0:T(256)}, u32[]{:S(2)}) copy-start(s32[256]{0:T(256)} %copy-done.29) | copy-start | bytes 3076 | tf_op jit(solution)/shard_map/while
  119.7 2.8 %copy-start.32 = (s32[4,256]{1,0:T(4,128)S(1)}, s32[4,256]{1,0:T(4,128)}, u32[]{:S(2)}) copy-start(s32[4,256]{1,0:T(4,128)} %copy-done.31) | copy-start | bytes 12292 | tf_op jit(solution)/shard_map/while
  119.7 2.8 %copy-start.34 = (f32[256,16]{0,1:T(8,128)S(1)}, f32[256,16]{0,1:T(8,128)}, u32[]{:S(2)}) copy-start(f32[256,16]{0,1:T(8,128)} %copy-done.33) | copy-start | bytes 49156 | tf_op jit(solution)/shard_map/while
  132.4 2.9 %copy-start.9 = (bf16[4,256,256]{2,1,0:T(8,128)(2,1)S(1)}, bf16[4,256,256]{2,1,0:T(8,128)(2,1)}, u32[]{:S(2)}) copy-start(bf16[4,256,256]{2,1,0:T(8,128)(2,1)} %copy-done.8) | copy-start | bytes 1572868 | tf_op jit(solution)/shard_map/while
  132.4 2.9 %copy-start.11 = (bf16[4,256,256]{2,1,0:T(8,128)(2,1)S(1)}, bf16[4,256,256]{2,1,0:T(8,128)(2,1)}, u32[]{:S(2)}) copy-start(bf16[4,256,256]{2,1,0:T(8,128)(2,1)} %copy-done.10) | copy-start | bytes 1572868 | tf_op jit(solution)/shard_map/while
  132.4 2.9 %copy-start.25 = (bf16[256,16]{0,1:T(8,128)(2,1)S(1)}, bf16[256,16]{0,1:T(8,128)(2,1)}, u32[]{:S(2)}) copy-start(bf16[256,16]{0,1:T(8,128)(2,1)} %copy-done.24) | copy-start | bytes 24580 | tf_op jit(solution)/shard_map/while
  132.4 2.9 %copy-start.30 = (s32[256]{0:T(256)S(1)}, s32[256]{0:T(256)}, u32[]{:S(2)}) copy-start(s32[256]{0:T(256)} %copy-done.29) | copy-start | bytes 3076 | tf_op jit(solution)/shard_map/while
  132.4 2.9 %copy-start.32 = (s32[4,256]{1,0:T(4,128)S(1)}, s32[4,256]{1,0:T(4,128)}, u32[]{:S(2)}) copy-start(s32[4,256]{1,0:T(4,128)} %copy-done.31) | copy-start | bytes 12292 | tf_op jit(solution)/shard_map/while
  132.4 2.9 %copy-start.34 = (f32[256,16]{0,1:T(8,128)S(1)}, f32[256,16]{0,1:T(8,128)}, u32[]{:S(2)}) copy-start(f32[256,16]{0,1:T(8,128)} %copy-done.33) | copy-start | bytes 49156 | tf_op jit(solution)/shard_map/while
  135.3 19.6 %copy-start.7 = (bf16[32,4,2048]{2,0,1:T(8,128)(2,1)S(1)}, bf16[32,4,2048]{2,0,1:T(8,128)(2,1)}, u32[]{:S(2)}) copy-start(bf16[32,4,2048]{2,0,1:T(8,128)(2,1)} %copy-done.6) | copy-start | bytes 1572868
  135.3 19.8 %slice-start = ((f32[256,16]{1,0:T(8,128)}), f32[128,16]{1,0:T(8,128)S(1)}, s32[]{:S(2)}) async-start(f32[256,16]{1,0:T(8,128)} %copy-done.17), calls=%async_computation.13 | async-start | bytes 131072 | tf_op jit(solution)/shard_map/slice | solution.py:142
  135.4 20.2 %copy-start.5 = (bf16[16,8,16,128]{3,2,1,0:T(8,128)(2,1)S(1)}, bf16[16,8,16,128]{3,2,1,0:T(8,128)(2,1)}, u32[]{:S(2)}) copy-start(bf16[16,8,16,128]{3,2,1,0:T(8,128)(2,1)} %copy-done.4) | copy-start | bytes 1572868
  136.9 9.0 %all-to-all-start.4 = ((bf16[32,4,256]{2,0,1:T(8,128)(2,1)}), bf16[32,4,256]{2,0,1:T(8,128)(2,1)S(1)}, u32[]{:S(2)}, u32[]{:S(2)}) async-start(bf16[32,4,256]{2,0,1:T(8,128)(2,1)} %bitcast.190), calls=%async_computation.6 | async-start | bytes 131072 | tf_op jit(solution)/shard_map/all_to_all | solution.py:122
  145.9 9.0 %all-to-all-start.5 = ((bf16[32,4,256]{2,0,1:T(8,128)(2,1)}), bf16[32,4,256]{2,0,1:T(8,128)(2,1)S(1)}, u32[]{:S(2)}, u32[]{:S(2)}) async-start(bf16[32,4,256]{2,0,1:T(8,128)(2,1)} %bitcast.189), calls=%async_computation.7 | async-start | bytes 131072 | tf_op jit(solution)/shard_map/all_to_all | solution.py:123
  155.1 4.9 %copy-start.21 = (bf16[16,8,16,128]{3,2,1,0:T(8,128)(2,1)}, bf16[16,8,16,128]{3,2,1,0:T(8,128)(2,1)S(1)}, u32[]{:S(2)}) copy-start(bf16[16,8,16,128]{3,2,1,0:T(8,128)(2,1)S(1)} %copy.227) | copy-start | bytes 1572868
  156.7 11.4 %all-to-all-start.8 = ((bf16[4,32,256]{2,1,0:T(8,128)(2,1)}), bf16[4,32,256]{2,1,0:T(8,128)(2,1)S(1)}, u32[]{:S(2)}, u32[]{:S(2)}) async-start(bf16[4,32,256]{2,1,0:T(8,128)(2,1)} %convert_element_type.73), calls=%async_computation.10 | async-start | bytes 131072 | tf_op jit(solution)/shard_map/all_to_all | solution.py:174
  160.0 49.0 %reduce-scatter.3.cloned.1.call-start = ((), (), s32[]{:S(2)}) async-start(), calls=%async_computation.11 | async-start | bytes 1179648 | tf_op jit(solution)/shard_map/reduce_scatter | solution.py:164
  162.4 3.8 %copy-start.2 = (f32[256,2048]{0,1:T(8,128)S(1)}, f32[256,2048]{0,1:T(8,128)}, u32[]{:S(2)}) copy-start(f32[256,2048]{0,1:T(8,128)} %get-tuple-element.70) | copy-start | bytes 6291460
  168.1 10.7 %all-to-all-start.7 = ((bf16[4,32,256]{2,1,0:T(8,128)(2,1)}), bf16[4,32,256]{2,1,0:T(8,128)(2,1)S(1)}, u32[]{:S(2)}, u32[]{:S(2)}) async-start(bf16[4,32,256]{2,1,0:T(8,128)(2,1)} %convert_element_type.69), calls=%async_computation.9 | async-start | bytes 131072 | tf_op jit(solution)/shard_map/all_to_all | solution.py:171
  178.8 13.7 %all-to-all-start.6 = ((bf16[4,32,2048]{2,1,0:T(8,128)(2,1)}), bf16[4,32,2048]{2,1,0:T(8,128)(2,1)S(1)}, u32[]{:S(2)}, u32[]{:S(2)}) async-start(bf16[4,32,2048]{2,1,0:T(8,128)(2,1)} %bitcast.23), calls=%async_computation.8 | async-start | bytes 1048576 | tf_op jit(solution)/shard_map/all_to_all | solution.py:170
  (51 other events, 68.1 us)
Sparse Core Ops, SparseCore 0:
  135.5 34.1 reduce-scatter.4
  172.8 36.0 reduce-scatter.2
where the time goes:
time: 219 us; the launch traced here: 217 us
  waiting for transfers between devices  60 us (27%)
  local copies, waits for them, and re-layouts  44.3 us (20%)
  starting transfers between devices  36.9 us (17%)
  matrix products  30.4 us (14%)
  blocking collectives  19.7 us (9%)
  between operations  14.5 us (7%)
  other arithmetic  10.2 us (5%)
    reduce_scatter x1, waiting for transfers between devices, on_device(): lax.psum_scatter(key_part, 'ctx', scatter_dimension=0, tiled=True)  14 us
    all_to_all x1, waiting for transfers between devices, on_device(): lax.all_to_all(roll_dout, 'roll', split_axis=1, concat_axis=0, tiled=True)  12.5 us
    while x136, local copies, waits for them, and re-layouts  11.6 us
    all_to_all x1, waiting for transfers between devices, on_device(): lax.all_to_all(roll_query, 'roll', split_axis=1, concat_axis=0, tiled=True)  10.1 us
    all_gather x1, blocking collectives, on_device(): lax.all_gather(prompt_key_rows, 'ctx', axis=0, tiled=True)  9.87 us
    all_gather x1, blocking collectives, on_device(): lax.all_gather(prompt_value_rows, 'ctx', axis=0, tiled=True)  9.82 us
    dot_general x5, matrix products, tile_grads(): jnp.einsum('qgmd,kgd->gmqk', grad_heads, value_heads, preferred_element_t...  9.38 us
    dynamic_update_slice x12, local copies, waits for them, and re-layouts, sweep(): running, (grad_key, grad_value) = lax.scan(key_step, running, stacked)  8.19 us
  transfers between devices with their start and end apart: 11, of which 8 were waited for; matrix products, arithmetic and copies ran while one was open for 13% of the time, Pallas kernels for 0%

commit v1 on v0

v1 whole, which is shorter than its diff:
```python
import functools
import math

import jax
import jax.numpy as jnp
from jax import lax
from jax.experimental import pallas as pl
from jax.experimental.pallas import tpu as pltpu
from jax.sharding import PartitionSpec as P

HEAD = 128
LOG2E = math.log2(math.e)
SCALE = 1.0 / math.sqrt(HEAD)
VMEM_LIMIT = 56 * 1024 * 1024
KEY_CHUNK = 512
ROW_CHUNK = 512

BF = jnp.bfloat16
F32 = jnp.float32


def dot_nt(a, b):
    return lax.dot_general(a, b, (((1,), (1,)), ((), ())), preferred_element_type=F32)


def dot_nn(a, b):
    return lax.dot_general(a, b, (((1,), (0,)), ((), ())), preferred_element_type=F32)


def dot_tn(a, b):
    return lax.dot_general(a, b, (((0,), (0,)), ((), ())), preferred_element_type=F32)


def split_sum(product):
    high = product.astype(BF)
    low = (product - high.astype(F32)).astype(BF)
    return high, low


def tile_grads(keys, values, queries, grads, lse_row, delta_row, mask):
    scores = dot_nt(keys, queries)
    probs = jnp.exp2(scores * (SCALE * LOG2E) - lse_row)
    if mask is not None:
        probs = jnp.where(mask, probs, 0.0)
    grad_probs = dot_nt(values, grads)
    grad_scores = (probs * (grad_probs - delta_row)).astype(BF)
    grad_value = dot_nn(probs.astype(BF), grads)
    grad_key = dot_nn(grad_scores, queries)
    grad_query = dot_tn(grad_scores, keys)
    return grad_query, grad_key, grad_value


def stacked_heads(ref, low, high, base, group, members):
    first = base + group * members * HEAD
    return jnp.concatenate(
        [ref[low:high, first + h * HEAD : first + (h + 1) * HEAD] for h in range(members)], axis=0
    )


def pack_kernel(me_ref, q_ref, do_ref, o_ref, k_ref, v_ref, lse_ref, *outs):
    parts = len(outs)
    width = q_ref.shape[1] // parts
    narrow = k_ref.shape[1] // parts
    heads = width // HEAD
    rows = q_ref.shape[0]
    me = me_ref[0]
    column = lax.broadcasted_iota(jnp.int32, (width, HEAD), 0) // HEAD
    lane = lax.broadcasted_iota(jnp.int32, (width, HEAD), 1)
    pick = jnp.where((lane == column + heads) | (lane == column + 2 * heads), 1.0, 0.0).astype(BF)
    all_heads = lse_ref.shape[1]
    lse_column = lax.broadcasted_iota(jnp.int32, (all_heads, HEAD), 0)
    lse_lane = lax.broadcasted_iota(jnp.int32, (all_heads, HEAD), 1)
    out_lane = lax.broadcasted_iota(jnp.int32, (rows, HEAD), 1)
    for k, out in enumerate(outs):
        dest = me ^ k
        wide = pl.ds(pl.multiple_of(dest * width, HEAD), width)
        thin = pl.ds(pl.multiple_of(dest * narrow, HEAD), narrow)
        grads = do_ref[:, wide]
        out[:, :width] = q_ref[:, wide]
        out[:, width : 2 * width] = grads
        out[:, 2 * width : 2 * width + narrow] = k_ref[:, thin]
        out[:, 2 * width + narrow : 2 * width + 2 * narrow] = v_ref[:, thin]
        high, low = split_sum(grads.astype(F32) * o_ref[:, wide].astype(F32))
        delta = dot_nn(high, pick) + dot_nn(low, pick)
        lse_pick = jnp.where(
            (lse_column == lse_lane + dest * heads) & (lse_lane < heads), 1.0, 0.0
        ).astype(BF)
        lse = dot_nn(lse_ref[...], lse_pick)
        delta_high = delta.astype(BF).astype(F32)
        stats = jnp.where(
            out_lane < heads, lse, jnp.where(out_lane < 2 * heads, delta_high, delta - delta_high)
        )
        out[:, 2 * width + 2 * narrow :] = stats.astype(BF)


def prompt_kernel(members, me_ref, q_ref, do_ref, o_ref, lse_ref, *rest):
    kv_refs, (dq_ref, part_ref) = rest[:-2], rest[-2:]
    slots = len(kv_refs)
    rows = q_ref.shape[0]
    half = rows // 2
    narrow = kv_refs[0].shape[1] // 2
    groups = narrow // HEAD
    me = me_ref[0]
    count = members * half
    ones = jnp.ones((8, HEAD), BF)
    chunk_slots = max(1, min(slots, KEY_CHUNK // half))
    chunk = chunk_slots * half
    key_row = lax.broadcasted_iota(jnp.int32, (chunk, 1), 0)
    query_row = lax.broadcasted_iota(jnp.int32, (1, count), 1) % half
    stat_lane = lax.broadcasted_iota(jnp.int32, (half, HEAD), 1)
    for g in range(groups):
        queries, grads, lse_rows, delta_rows = [], [], [], []
        for s in range(2):
            low, high = s * half, (s + 1) * half
            queries.append(stacked_heads(q_ref, low, high, 0, g, members))
            grads.append(stacked_heads(do_ref, low, high, 0, g, members))
            outs = stacked_heads(o_ref, low, high, 0, g, members)
            up, down = split_sum(grads[s].astype(F32) * outs.astype(F32))
            delta_rows.append((dot_nt(ones, up) + dot_nt(ones, down))[0:1])
            lse = lse_ref[low:high, :]
            picked = jnp.concatenate(
                [jnp.where(stat_lane == g * members + h, lse, jnp.zeros_like(lse)) for h in range(members)],
                axis=0,
            )
            lse_rows.append(dot_nt(ones, picked)[0:1] * LOG2E)
        grad_queries = [None, None]
        for side in range(2):
            for c in range(slots // chunk_slots):
                owned = kv_refs[c * chunk_slots : (c + 1) * chunk_slots]
                span = slice(side * half, (side + 1) * half)
                keys = jnp.concatenate([r[span, g * HEAD : (g + 1) * HEAD] for r in owned], axis=0)
                values = jnp.concatenate(
                    [r[span, narrow + g * HEAD : narrow + (g + 1) * HEAD] for r in owned], axis=0
                )
                owner = me ^ (c * chunk_slots + key_row // half)
                offset = key_row % half
                grad_key = grad_value = None
                for s in (1, 0) if side == 0 else (1,):
                    mask = None
                    if s == side:
                        ahead = owner - me if side == 0 else me - owner
                        mask = ahead * half + offset <= query_row
                    dq, dk, dv = tile_grads(
                        keys, values, queries[s], grads[s], lse_rows[s], delta_rows[s], mask
                    )
                    grad_queries[s] = dq if grad_queries[s] is None else grad_queries[s] + dq
                    grad_key = dk if grad_key is None else grad_key + dk
                    grad_value = dv if grad_value is None else grad_value + dv
                grad_key = grad_key * SCALE
                for t in range(chunk_slots):
                    piece = slice(t * half, (t + 1) * half)
                    slot = c * chunk_slots + t
                    part_ref[slot, span, g * HEAD : (g + 1) * HEAD] = grad_key[piece]
                    part_ref[slot, span, narrow + g * HEAD : narrow + (g + 1) * HEAD] = grad_value[piece]
        for s in range(2):
            result = (grad_queries[s] * SCALE).astype(BF)
            for h in range(members):
                first = (g * members + h) * HEAD
                dq_ref[s * half : (s + 1) * half, first : first + HEAD] = result[h * half : (h + 1) * half]


def roll_kernel(parts, slots, members, me_ref, *rest):
    packs, rest = rest[:parts], rest[parts:]
    kv_refs, rest = rest[:slots], rest[slots:]
    part_ref, even_ref, odd_ref = rest[:3]
    backs = rest[3:]
    me = me_ref[0]
    rows = packs[0].shape[0]
    kv_rows = kv_refs[0].shape[0]
    narrow = kv_refs[0].shape[1] // 2
    groups = narrow // HEAD
    heads = groups * members
    width = heads * HEAD
    block = members * rows
    count = parts * block
    stat_row = lax.broadcasted_iota(jnp.int32, (8, HEAD), 0)
    stat_lane = lax.broadcasted_iota(jnp.int32, (8, HEAD), 1)
    pick = jnp.where(
        ((stat_row == 0) & (stat_lane < heads))
        | ((stat_row == 1) & (stat_lane >= heads) & (stat_lane < 3 * heads)),
        1.0,
        0.0,
    ).astype(BF)
    lane_head = lax.broadcasted_iota(jnp.int32, (rows, HEAD), 1) % heads
    chunk_slots = max(1, min(slots, KEY_CHUNK // kv_rows))
    row_chunk = min(count, ROW_CHUNK)
    own_key = lax.broadcasted_iota(jnp.int32, (parts * rows, 1), 0)
    own_key_pos = (me ^ (own_key // rows)) * rows + own_key % rows
    own_query = lax.broadcasted_iota(jnp.int32, (1, count), 1)
    own_query_pos = (me ^ (own_query // block)) * rows + own_query % rows
    for g in range(groups):
        queries = jnp.concatenate([stacked_heads(p, 0, rows, 0, g, members) for p in packs], axis=0)
        grads = jnp.concatenate([stacked_heads(p, 0, rows, width, g, members) for p in packs], axis=0)
        picked = []
        for p in packs:
            stats = p[:, 2 * width + 2 * narrow :]
            for h in range(members):
                picked.append(jnp.where(lane_head == g * members + h, stats, jnp.zeros_like(stats)))
        stat_rows = dot_nt(pick, jnp.concatenate(picked, axis=0))
        lse_row = stat_rows[0:1] * LOG2E
        delta_row = stat_rows[1:2]
        first = 2 * width + g * HEAD
        own_keys = jnp.concatenate([p[:, first : first + HEAD] for p in packs], axis=0)
        own_values = jnp.concatenate([p[:, first + narrow : first + narrow + HEAD] for p in packs], axis=0)
        grad_query, own_dk, own_dv = tile_grads(
            own_keys, own_values, queries, grads, lse_row, delta_row, own_key_pos <= own_query_pos
        )
        own_dk = (own_dk * SCALE).astype(BF)
        own_dv = own_dv.astype(BF)
        for k, back in enumerate(backs):
            piece = slice(k * rows, (k + 1) * rows)
            back[:, width + g * HEAD : width + (g + 1) * HEAD] = own_dk[piece]
            back[:, width + narrow + g * HEAD : width + narrow + (g + 1) * HEAD] = own_dv[piece]
        grad_rows = [grad_query[r : r + row_chunk] for r in range(0, count, row_chunk)]
        for c in range(slots // chunk_slots):
            owned = kv_refs[c * chunk_slots : (c + 1) * chunk_slots]
            keys = jnp.concatenate([r[:, g * HEAD : (g + 1) * HEAD] for r in owned], axis=0)
            values = jnp.concatenate(
                [r[:, narrow + g * HEAD : narrow + (g + 1) * HEAD] for r in owned], axis=0
            )
            grad_key = grad_value = None
            for i in range(count // row_chunk):
                piece = slice(i * row_chunk, (i + 1) * row_chunk)
                dq, dk, dv = tile_grads(
                    keys, values, queries[piece], grads[piece], lse_row[:, piece], delta_row[:, piece], None
                )
                grad_rows[i] = grad_rows[i] + dq
                grad_key = dk if grad_key is None else grad_key + dk
                grad_value = dv if grad_value is None else grad_value + dv
            grad_key = grad_key * SCALE
            for t in range(chunk_slots):
                slot = c * chunk_slots + t
                piece = slice(t * kv_rows, (t + 1) * kv_rows)
                for total, base in ((grad_key, 0), (grad_value, narrow)):
                    cols = slice(base + g * HEAD, base + (g + 1) * HEAD)
                    value = total[piece] + part_ref[slot, :, cols]
                    if slot % 2 == 0:
                        even_ref[slot // 2, :, cols] = value
                    else:
                        odd_ref[slot // 2, :, cols] = value.astype(BF)
        result = jnp.concatenate([(r * SCALE).astype(BF) for r in grad_rows], axis=0)
        for k, back in enumerate(backs):
            for h in range(members):
                start = k * block + h * rows
                first = (g * members + h) * HEAD
                back[:, first : first + HEAD] = result[start : start + rows]


def add_kernel(even_ref, got_ref, own_ref, *outs):
    own_ref[...] = even_ref[0] + got_ref[0].astype(F32)
    for t, out in enumerate(outs):
        out[...] = (even_ref[t + 1] + got_ref[t + 1].astype(F32)).astype(BF)


def final_kernel(parts, others, me_ref, own_ref, *rest):
    got, rest = rest[:others], rest[others:]
    backs, outs = rest[:parts], rest[parts:]
    pk_ref, pv_ref, rq_ref, rk_ref, rv_ref = outs
    me = me_ref[0]
    total = own_ref[...]
    for r in got:
        total = total + r[...].astype(F32)
    narrow = pk_ref.shape[1]
    pk_ref[...] = total[:, :narrow].astype(BF)
    pv_ref[...] = total[:, narrow:].astype(BF)
    width = rq_ref.shape[1] // parts
    for k, back in enumerate(backs):
        dest = me ^ k
        rq_ref[:, pl.ds(pl.multiple_of(dest * width, HEAD), width)] = back[:, :width]
        thin = pl.ds(pl.multiple_of(dest * narrow, HEAD), narrow)
        rk_ref[:, thin] = back[:, width : width + narrow]
        rv_ref[:, thin] = back[:, width + narrow :]


VMEM = pl.BlockSpec(memory_space=pltpu.VMEM)
SMEM = pl.BlockSpec(memory_space=pltpu.SMEM)


def call(kernel, name, outs, args, flops=0, scalar=True):
    moved = sum(math.prod(a.shape) * a.dtype.itemsize for a in list(args) + list(outs))
    return pl.pallas_call(
        kernel,
        name=name,
        out_shape=outs,
        in_specs=[SMEM] * scalar + [VMEM] * (len(args) - scalar),
        out_specs=[VMEM] * len(outs),
        compiler_params=pltpu.CompilerParams(vmem_limit_bytes=VMEM_LIMIT),
        cost_estimate=pl.CostEstimate(flops=flops, bytes_accessed=moved, transcendentals=0),
    )(*args)


def shape(dims, dtype):
    return jax.ShapeDtypeStruct(dims, dtype)


def swap(x, axis, k):
    n = lax.axis_size(axis)
    return lax.ppermute(x, axis, [(i, i ^ k) for i in range(n)])


def on_device(
    prompt_query,
    prompt_key_rows,
    prompt_value_rows,
    prompt_dout,
    prompt_out,
    prompt_lse,
    roll_query,
    rollout_key_rows,
    rollout_value_rows,
    roll_dout,
    roll_out,
    roll_lse,
):
    slots = lax.axis_size("ctx")
    parts = lax.axis_size("roll")
    ctx_id = lax.axis_index("ctx").astype(jnp.int32).reshape(1)
    roll_id = lax.axis_index("roll").astype(jnp.int32).reshape(1)
    prompt_rows, width = prompt_query.shape
    narrow = prompt_key_rows.shape[1]
    members = width // narrow
    heads = width // HEAD
    rows = roll_query.shape[0]
    packed = 2 * width + 2 * narrow + HEAD

    packs = call(
        pack_kernel,
        "pack",
        [shape((rows, packed), BF)] * parts,
        (roll_id, roll_query, roll_dout, roll_out, rollout_key_rows, rollout_value_rows, roll_lse),
    )
    kv = jnp.concatenate([prompt_key_rows, prompt_value_rows], axis=1)
    got = [packs[0]] + [None] * (parts - 1)
    for k in sorted(range(1, parts), key=lambda k: (k % 2 == 0, k)):
        got[k] = swap(packs[k], "roll", k)

    blocks = [None] * slots
    for s in range(0, slots, 2):
        blocks[s] = kv if s == 0 else swap(kv, "ctx", s)
    for s in range(0, slots, 2):
        blocks[s + 1] = swap(blocks[s], "ctx", 1)

    lse_padded = jnp.pad(prompt_lse, ((0, 0), (0, HEAD - heads)))
    unit = 2 * 5 * heads * HEAD * prompt_rows * slots
    prompt_dq, part = call(
        functools.partial(prompt_kernel, members),
        "prompt_grads",
        [shape((prompt_rows, width), BF), shape((slots, prompt_rows, 2 * narrow), F32)],
        (ctx_id, prompt_query, prompt_dout, prompt_out, lse_padded, *blocks),
        flops=unit * prompt_rows * 3 // 2,
    )
    even, odd, *backs = call(
        functools.partial(roll_kernel, parts, slots, members),
        "roll_grads",
        [
            shape((slots // 2, prompt_rows, 2 * narrow), F32),
            shape((slots // 2, prompt_rows, 2 * narrow), BF),
        ]
        + [shape((rows, width + 2 * narrow), BF)] * parts,
        (roll_id, *got, *blocks, part),
        flops=unit * rows * parts * 2,
    )
    returned = [backs[0]] + [None] * (parts - 1)
    for k in sorted(range(1, parts), key=lambda k: (k % 2 == 0, k)):
        returned[k] = swap(backs[k], "roll", k)
    odd_got = swap(odd, "ctx", 1)
    own, *sums = call(
        add_kernel,
        "pair_sum",
        [shape((prompt_rows, 2 * narrow), F32)] + [shape((prompt_rows, 2 * narrow), BF)] * (slots // 2 - 1),
        (even, odd_got),
        scalar=False,
    )
    sums = [swap(x, "ctx", 2 * (t + 1)) for t, x in enumerate(sums)]
    prompt_dk, prompt_dv, roll_dq, roll_dk, roll_dv = call(
        functools.partial(final_kernel, parts, len(sums)),
        "finish",
        [
            shape((prompt_rows, narrow), BF),
            shape((prompt_rows, narrow), BF),
            shape((rows, parts * width), BF),
            shape((rows, parts * narrow), BF),
            shape((rows, parts * narrow), BF),
        ],
        (roll_id, own, *sums, *returned),
    )
    return prompt_dq, prompt_dk, prompt_dv, roll_dq, roll_dk, roll_dv


def solution(mesh):
    both = P(("ctx", "roll"), None)
    split = P("ctx", "roll")
    return jax.shard_map(
        on_device,
        mesh=mesh,
        in_specs=(split,) * 6 + (both,) * 6,
        out_specs=(split,) * 3 + (both,) * 3,
        check_vma=False,
    )
```

time: 219 us -> 80.4 us (0.37)
  local copies, waits for them, and re-layouts: 44.3 us -> 6.18 us
  waiting for transfers between devices: 60 us -> 25.1 us
  matrix products: 30.4 us -> 0 us
  Pallas kernels: 0 us -> 26.5 us
  blocking collectives: 19.7 us -> 0 us
  starting transfers between devices: 36.9 us -> 21.3 us
  between operations: 14.5 us -> 0.8 us
  other arithmetic: 10.2 us -> 0 us
    all_to_all x9 -> x0, waiting for transfers between devices: 45.6 us -> none  [the longest x1 12.5 us: on_device(): lax.all_to_all(roll_dout, 'roll', split_axis=1, concat_axis=0, tiled=True)]
    all_to_all x9 -> x0, starting transfers between devices: 36.9 us -> none  [the longest x1 6.32 us: on_device(): lax.all_to_all(roll_lse, 'roll', split_axis=1, concat_axis=0, tiled=True)]
    dot_general x25 -> x0, matrix products: 30.4 us -> none  [the longest x5 9.38 us: tile_grads(): jnp.einsum('qgmd,kgd->gmqk', grad_heads, value_heads, preferred_element_t...]
    pallas_call x0 -> x5, Pallas kernels: none -> 26.5 us  [call(): pl.pallas_call(kernel, name=name, out_shape=outs, in_specs=[SMEM] * scala...]
    ppermute x0 -> x17, waiting for transfers between devices: none -> 25.1 us  [swap(): return lax.ppermute(x, axis, [(i, i ^ k) for i in range(n)])]
    ppermute x0 -> x17, starting transfers between devices: none -> 21.3 us  [swap(): return lax.ppermute(x, axis, [(i, i ^ k) for i in range(n)])]
    all_gather x2 -> x0, blocking collectives: 19.7 us -> none  [the longest x1 9.87 us: on_device(): lax.all_gather(prompt_key_rows, 'ctx', axis=0, tiled=True)]
    reduce_scatter x2 -> x0, waiting for transfers between devices: 14 us -> none  [the longest x1 14 us: on_device(): lax.psum_scatter(key_part, 'ctx', scatter_dimension=0, tiled=True)]
  transfers between devices with their start and end apart: 11 -> 17, of which waited for: 8 -> 5; matrix products, arithmetic and copies ran while one was open for 13% -> 2% of each run, Pallas kernels for 0% -> 17%
where the time goes in v1:
time: 80.4 us; the launch traced here: 79.8 us
  Pallas kernels  26.5 us (33%)
  waiting for transfers between devices  25.1 us (31%)
  starting transfers between devices  21.3 us (26%)
  local copies, waits for them, and re-layouts  6.18 us (8%)
    pallas_call x5, Pallas kernels, call(): pl.pallas_call(kernel, name=name, out_shape=outs, in_specs=[SMEM] * scala...  26.5 us
    ppermute x17, waiting for transfers between devices, swap(): return lax.ppermute(x, axis, [(i, i ^ k) for i in range(n)])  25.1 us
    ppermute x17, starting transfers between devices, swap(): return lax.ppermute(x, axis, [(i, i ^ k) for i in range(n)])  21.3 us
    unnamed x38, local copies, waits for them, and re-layouts  4.71 us
  transfers between devices with their start and end apart: 17, of which 5 were waited for; matrix products, arithmetic and copies ran while one was open for 2% of the time, Pallas kernels for 17%

profile of v1, /device:TPU:0, one launch (start us, length us, event | category | flops | bytes accessed | tf_op | source)
XLA Modules:
  0.0 79.8 jit_solution(6425058954473708552)
XLA Ops:
  0.6 0.8 %constant_dynamic-update-slice_fusion.1 = bf16[128,512]{1,0:T(8,128)(2,1)S(1)} fusion(bf16[128,256]{1,0:T(8,128)(2,1)} %param.13), kind=kLoop, calls=%fused_computation.1 | loop fusion | bytes 131072
  1.5 0.8 %constant_dynamic-update-slice_fusion.rest_0_.rest_4_ = bf16[128,512]{1,0:T(8,128)(2,1)S(1)} fusion(bf16[128,512]{1,0:T(8,128)(2,1)S(1)} %constant_dynamic-update-slice_fusion.1, bf16[128,256]{1,0:T(8,128)(2,1)} %param.14), kind=kLoop, calls=%fused_computation | loop fusion | bytes 131072 | tf_op jit(solution)/shard_map/concatenate | solution.py:332
  2.3 2.9 %collective-permute-start.1 = (bf16[128,512]{1,0:T(8,128)(2,1)S(1)}, bf16[128,512]{1,0:T(8,128)(2,1)S(1)}, u32[]{:S(2)}, u32[]{:S(2)}) collective-permute-start(bf16[128,512]{1,0:T(8,128)(2,1)S(1)} %constant_dynamic-update-slice_fusion.rest_0_.rest_4_), channel_id=1, source_target_pairs={{0,8},{4,12},{8,0},{12,4},{16,24},{20,28},{24,16},{28,20},{1,9},{5... | collective-permute-start | bytes 393224 | tf_op jit(solution)/shard_map/ppermute | solution.py:298
  5.3 1.5 %collective-permute-start.3 = (bf16[128,512]{1,0:T(8,128)(2,1)S(1)}, bf16[128,512]{1,0:T(8,128)(2,1)S(1)}, u32[]{:S(2)}, u32[]{:S(2)}) collective-permute-start(bf16[128,512]{1,0:T(8,128)(2,1)S(1)} %constant_dynamic-update-slice_fusion.rest_0_.rest_4_), channel_id=1, source_target_pairs={{0,16},{4,20},{8,24},{12,28},{16,0},{20,4},{24,8},{28,12},{1,17},{... | collective-permute-start | bytes 393224 | tf_op jit(solution)/shard_map/ppermute | solution.py:298
  6.8 0.0 collective-permute-start.5
  6.8 0.0 collective-permute-start
  6.8 2.4 %collective-permute-done.1.rest_2_.rest_6_ = bf16[128,512]{1,0:T(8,128)(2,1)S(1)} collective-permute-done((bf16[128,512]{1,0:T(8,128)(2,1)S(1)}, bf16[128,512]{1,0:T(8,128)(2,1)S(1)}, u32[]{:S(2)}, u32[]{:S(2)}) %collective-permute-start.1) | collective-permute-done | bytes 131104 | tf_op jit(solution)/shard_map/ppermute | solution.py:298
  9.2 0.0 collective-permute-start.2
  9.2 3.9 %collective-permute-done.3.rest_4_.rest_8_ = bf16[128,512]{1,0:T(8,128)(2,1)S(1)} collective-permute-done((bf16[128,512]{1,0:T(8,128)(2,1)S(1)}, bf16[128,512]{1,0:T(8,128)(2,1)S(1)}, u32[]{:S(2)}, u32[]{:S(2)}) %collective-permute-start.3) | collective-permute-done | bytes 131104 | tf_op jit(solution)/shard_map/ppermute | solution.py:298
  13.0 0.0 collective-permute-start.4
  13.0 0.0 collective-permute-done.5.rest_6_.rest_10_
  13.1 0.5 collective-permute-start.6
  13.6 3.3 %pack.1 = (bf16[32,4736]{1,0:T(8,128)(2,1)}, bf16[32,4736]{1,0:T(8,128)(2,1)}, bf16[32,4736]{1,0:T(8,128)(2,1)}, bf16[32,4736]{1,0:T(8,128)(2,1)}) custom-call(s32[1]{0:T(128)} %bitcast.1.me_ref, bf16[32,8192]{1,0:T(8,128)(2,1)} %q_ref.3, bf16[32,8192]{1,0:T(8,128)(2,1)} %do_ref.3, bf16[32,8192]{1,0:T(8,128)(2,1)} %o_ref.3, bf16[32,1024]{1,0:T(8,128)(2,1)} %k_ref.1, ...), custom_call_target="tpu_custom_call" | custom-call | bytes 2920452 | tf_op jit(solution)/shard_map/pack/pallas_call | solution.py:281
  16.8 1.6 %collective-permute-start.7 = (bf16[32,4736]{1,0:T(8,128)(2,1)}, bf16[32,4736]{1,0:T(8,128)(2,1)S(1)}, u32[]{:S(2)}, u32[]{:S(2)}) collective-permute-start(bf16[32,4736]{1,0:T(8,128)(2,1)} %get-tuple-element.29), channel_id=1, source_target_pairs={{0,1},{1,0},{2,3},{3,2},{4,5},{5,4},{6,7},{7,6},{8,9},{9,8},{10,11... | collective-permute-start | bytes 909320 | tf_op jit(solution)/shard_map/ppermute | solution.py:298
  18.4 0.8 %copy.18 = bf16[128,16]{1,0:T(8,128)(2,1)S(1)} copy(bf16[128,16]{0,1:T(8,128)(2,1)} %param.17) | data formatting | bytes 8192 | tf_op args[5]
  19.2 0.6 pad.4.lse_ref
  19.8 0.0 collective-permute-done.rest_1_.rest_5_
  19.8 2.6 %collective-permute-start.8 = (bf16[32,4736]{1,0:T(8,128)(2,1)}, bf16[32,4736]{1,0:T(8,128)(2,1)S(1)}, u32[]{:S(2)}, u32[]{:S(2)}) collective-permute-start(bf16[32,4736]{1,0:T(8,128)(2,1)} %get-tuple-element.30), channel_id=1, source_target_pairs={{0,2},{1,3},{2,0},{3,1},{4,6},{5,7},{6,4},{7,5},{8,10},{9,11},{10,... | collective-permute-start | bytes 909320 | tf_op jit(solution)/shard_map/ppermute | solution.py:298
  22.4 0.2 collective-permute-start.9
  22.7 0.4 copy-done.15
  23.1 0.2 copy-done.16
  23.3 0.1 copy-done.17
  23.4 8.1 %prompt_grads.1 = (bf16[128,2048]{1,0:T(8,128)(2,1)}, f32[8,128,512]{2,1,0:T(8,128)}) custom-call(s32[1]{0:T(128)} %bitcast.me_ref, bf16[128,2048]{1,0:T(8,128)(2,1)} %q_ref.2, bf16[128,2048]{1,0:T(8,128)(2,1)} %do_ref.2, bf16[128,2048]{1,0:T(8,128)(2,1)} %o_ref.2, bf16[128,128]{1,0:T(8,128)(2,1)} %pad.4.lse_ref, bf16[128,512]{1,0:T(8,128)(2,1)} %copy-done.7, ...), custom_call_target="tpu_custom_call" | custom-call | flops 4026531840 | bytes 5275652 | tf_op jit(solution)/shard_map/prompt_grads/pallas_call | solution.py:281
  31.4 0.0 collective-permute-done.7.rest_1_
  31.4 12.6 %collective-permute-done.8.rest_2_ = bf16[32,4736]{1,0:T(8,128)(2,1)S(1)} collective-permute-done((bf16[32,4736]{1,0:T(8,128)(2,1)}, bf16[32,4736]{1,0:T(8,128)(2,1)S(1)}, u32[]{:S(2)}, u32[]{:S(2)}) %collective-permute-start.8) | collective-permute-done | bytes 303136 | tf_op jit(solution)/shard_map/ppermute | solution.py:298
  44.0 0.7 copy-done.9
  44.7 0.1 copy-done.10
  44.8 10.7 %roll_grads.1 = (f32[4,128,512]{2,1,0:T(8,128)}, bf16[4,128,512]{2,1,0:T(8,128)(2,1)}, bf16[32,2560]{1,0:T(8,128)(2,1)}, bf16[32,2560]{1,0:T(8,128)(2,1)}, bf16[...) custom-call(s32[1]{0:T(128)} %bitcast.1.me_ref, bf16[32,4736]{1,0:T(8,128)(2,1)} %get-tuple-element.28.rest_0_, ...), custom_call_target="tpu_custom_call" | custom-call | flops 5368709120 | bytes 6586372 | tf_op jit(solution)/shard_map/roll_grads/pallas_call | solution.py:281
  55.5 0.0 collective-permute-start.10
  55.5 5.9 %collective-permute-start.14 = (bf16[32,2560]{1,0:T(8,128)(2,1)}, bf16[32,2560]{1,0:T(8,128)(2,1)S(1)}, u32[]{:S(2)}, u32[]{:S(2)}) collective-permute-start(bf16[32,2560]{1,0:T(8,128)(2,1)} %get-tuple-element.40), channel_id=1, source_target_pairs={{0,1},{1,0},{2,3},{3,2},{4,5},{5,4},{6,7},{7,6},{8,9},{9,8},{10,11... | collective-permute-start | bytes 491528 | tf_op jit(solution)/shard_map/ppermute | solution.py:298
  61.4 1.1 %collective-permute-start.15 = (bf16[32,2560]{1,0:T(8,128)(2,1)}, bf16[32,2560]{1,0:T(8,128)(2,1)S(1)}, u32[]{:S(2)}, u32[]{:S(2)}) collective-permute-start(bf16[32,2560]{1,0:T(8,128)(2,1)} %get-tuple-element.41), channel_id=1, source_target_pairs={{0,2},{1,3},{2,0},{3,1},{4,6},{5,7},{6,4},{7,5},{8,10},{9,11},{10,... | collective-permute-start | bytes 491528 | tf_op jit(solution)/shard_map/ppermute | solution.py:298
  62.5 1.4 %collective-permute-start.16 = (bf16[32,2560]{1,0:T(8,128)(2,1)}, bf16[32,2560]{1,0:T(8,128)(2,1)S(1)}, u32[]{:S(2)}, u32[]{:S(2)}) collective-permute-start(bf16[32,2560]{1,0:T(8,128)(2,1)} %get-tuple-element.42), channel_id=1, source_target_pairs={{0,3},{1,2},{2,1},{3,0},{4,7},{5,6},{6,5},{7,4},{8,11},{9,10},{10,... | collective-permute-start | bytes 491528 | tf_op jit(solution)/shard_map/ppermute | solution.py:298
  63.9 0.0 collective-permute-done.10.got_ref
  63.9 0.8 copy-done
  64.7 2.2 %pair_sum.1 = (f32[128,512]{1,0:T(8,128)}, bf16[128,512]{1,0:T(8,128)(2,1)}, bf16[128,512]{1,0:T(8,128)(2,1)}, bf16[128,512]{1,0:T(8,128)(2,1)}) custom-call(f32[4,128,512]{2,1,0:T(8,128)} %get-tuple-element.33.even_ref, bf16[4,128,512]{2,1,0:T(8,128)(2,1)} %copy-done), custom_call_target="tpu_custom_call" | custom-call | bytes 2228224 | tf_op jit(solution)/shard_map/pair_sum/pallas_call | solution.py:281
  66.9 1.1 %collective-permute-start.11 = (bf16[128,512]{1,0:T(8,128)(2,1)}, bf16[128,512]{1,0:T(8,128)(2,1)S(1)}, u32[]{:S(2)}, u32[]{:S(2)}) collective-permute-start(bf16[128,512]{1,0:T(8,128)(2,1)} %get-tuple-element.36), channel_id=1, source_target_pairs={{0,8},{4,12},{8,0},{12,4},{16,24},{20,28},{24,16},{28,20},{1,9},{5... | collective-permute-start | bytes 393224 | tf_op jit(solution)/shard_map/ppermute | solution.py:298
  68.0 0.9 %collective-permute-start.12 = (bf16[128,512]{1,0:T(8,128)(2,1)}, bf16[128,512]{1,0:T(8,128)(2,1)S(1)}, u32[]{:S(2)}, u32[]{:S(2)}) collective-permute-start(bf16[128,512]{1,0:T(8,128)(2,1)} %get-tuple-element.37), channel_id=1, source_target_pairs={{0,16},{4,20},{8,24},{12,28},{16,0},{20,4},{24,8},{28,12},{1,17},{... | collective-permute-start | bytes 393224 | tf_op jit(solution)/shard_map/ppermute | solution.py:298
  69.0 0.5 collective-permute-done.14.rest_4_
  69.5 1.5 %collective-permute-start.13 = (bf16[128,512]{1,0:T(8,128)(2,1)}, bf16[128,512]{1,0:T(8,128)(2,1)S(1)}, u32[]{:S(2)}, u32[]{:S(2)}) collective-permute-start(bf16[128,512]{1,0:T(8,128)(2,1)} %get-tuple-element.38), channel_id=1, source_target_pairs={{0,24},{4,28},{8,16},{12,20},{16,8},{20,12},{24,0},{28,4},{1,25},{... | collective-permute-start | bytes 393224 | tf_op jit(solution)/shard_map/ppermute | solution.py:298
  71.0 5.7 %collective-permute-done.15.rest_5_ = bf16[32,2560]{1,0:T(8,128)(2,1)S(1)} collective-permute-done((bf16[32,2560]{1,0:T(8,128)(2,1)}, bf16[32,2560]{1,0:T(8,128)(2,1)S(1)}, u32[]{:S(2)}, u32[]{:S(2)}) %collective-permute-start.15) | collective-permute-done | bytes 163872 | tf_op jit(solution)/shard_map/ppermute | solution.py:298
  76.7 0.0 collective-permute-done.11.rest_0_
  76.7 0.0 collective-permute-done.13.rest_2_
  76.7 0.6 copy-done.2
  77.3 0.1 copy-done.3
  77.4 0.1 copy-done.4
  77.4 0.1 copy-done.5
  77.5 0.0 copy-done.6
  77.5 2.3 %finish.1 = (bf16[128,256]{1,0:T(8,128)(2,1)}, bf16[128,256]{1,0:T(8,128)(2,1)}, bf16[32,8192]{1,0:T(8,128)(2,1)}, bf16[32,1024]{1,0:T(8,128)(2,1)}, bf16[32,1024]{1,0:T(8,128)(2,1)}) custom-call(s32[1]{0:T(128)} %bitcast.1.me_ref, f32[128,512]{1,0:T(8,128)} %get-tuple-element.35.own_ref, bf16[128,512]{1,0:T(8,128)(2,1)} %copy-done.4, ...), custom_call_target="tpu_custom_call" | custom-call | bytes 2097156 | tf_op jit(solution)/shard_map/finish/pallas_call | solution.py:281
  (31 shorter events, 0.1 us)
Async XLA Ops:
  2.3 20.4 %copy-start.7 = (bf16[128,512]{1,0:T(8,128)(2,1)}, bf16[128,512]{1,0:T(8,128)(2,1)S(1)}, u32[]{:S(2)}) copy-start(bf16[128,512]{1,0:T(8,128)(2,1)S(1)} %constant_dynamic-update-slice_fusion.rest_0_.rest_4_) | copy-start | bytes 393220
  2.3 6.8 %collective-permute-start.1 = (bf16[128,512]{1,0:T(8,128)(2,1)S(1)}, bf16[128,512]{1,0:T(8,128)(2,1)S(1)}, u32[]{:S(2)}, u32[]{:S(2)}) collective-permute-start(bf16[128,512]{1,0:T(8,128)(2,1)S(1)} %constant_dynamic-update-slice_fusion.rest_0_.rest_4_), channel_id=1, source_target_pairs={{0,8},{4,12},{8,0},{12,4},{16,24},{20,28},{24,16},{28,20},{1,9},{5... | collective-permute-start | bytes 393224 | tf_op jit(solution)/shard_map/ppermute | solution.py:298
  5.3 7.8 %collective-permute-start.3 = (bf16[128,512]{1,0:T(8,128)(2,1)S(1)}, bf16[128,512]{1,0:T(8,128)(2,1)S(1)}, u32[]{:S(2)}, u32[]{:S(2)}) collective-permute-start(bf16[128,512]{1,0:T(8,128)(2,1)S(1)} %constant_dynamic-update-slice_fusion.rest_0_.rest_4_), channel_id=1, source_target_pairs={{0,16},{4,20},{8,24},{12,28},{16,0},{20,4},{24,8},{28,12},{1,17},{... | collective-permute-start | bytes 393224 | tf_op jit(solution)/shard_map/ppermute | solution.py:298
  6.8 6.3 %collective-permute-start.5 = (bf16[128,512]{1,0:T(8,128)(2,1)S(1)}, bf16[128,512]{1,0:T(8,128)(2,1)S(1)}, u32[]{:S(2)}, u32[]{:S(2)}) collective-permute-start(bf16[128,512]{1,0:T(8,128)(2,1)S(1)} %constant_dynamic-update-slice_fusion.rest_0_.rest_4_), channel_id=1, source_target_pairs={{0,24},{4,28},{8,16},{12,20},{16,8},{20,12},{24,0},{28,4},{1,25},{... | collective-permute-start | bytes 393224 | tf_op jit(solution)/shard_map/ppermute | solution.py:298
  6.8 13.0 %collective-permute-start = (bf16[128,512]{1,0:T(8,128)(2,1)S(1)}, bf16[128,512]{1,0:T(8,128)(2,1)S(1)}, u32[]{:S(2)}, u32[]{:S(2)}) collective-permute-start(bf16[128,512]{1,0:T(8,128)(2,1)S(1)} %constant_dynamic-update-slice_fusion.rest_0_.rest_4_), channel_id=1, source_target_pairs={{0,4},{4,0},{8,12},{12,8},{16,20},{20,16},{24,28},{28,24},{1,5},{5... | collective-permute-start | bytes 393224 | tf_op jit(solution)/shard_map/ppermute | solution.py:298
  9.2 13.5 %copy-start.11 = (bf16[128,512]{1,0:T(8,128)(2,1)}, bf16[128,512]{1,0:T(8,128)(2,1)S(1)}, u32[]{:S(2)}) copy-start(bf16[128,512]{1,0:T(8,128)(2,1)S(1)} %collective-permute-done.1.rest_2_.rest_6_) | copy-start | bytes 393220
  9.2 13.3 %collective-permute-start.2 = (bf16[128,512]{1,0:T(8,128)(2,1)S(1)}, bf16[128,512]{1,0:T(8,128)(2,1)S(1)}, u32[]{:S(2)}, u32[]{:S(2)}) collective-permute-start(bf16[128,512]{1,0:T(8,128)(2,1)S(1)} %collective-permute-done.1.rest_2_.rest_6_), channel_id=1, source_target_pairs={{0,4},{4,0},{8,12},{12,8},{16,20},{20,16},{24,28},{28,24},{1,5},{5... | collective-permute-start | bytes 393224 | tf_op jit(solution)/shard_map/ppermute | solution.py:298
  13.0 9.7 %copy-start.12 = (bf16[128,512]{1,0:T(8,128)(2,1)}, bf16[128,512]{1,0:T(8,128)(2,1)S(1)}, u32[]{:S(2)}) copy-start(bf16[128,512]{1,0:T(8,128)(2,1)S(1)} %collective-permute-done.3.rest_4_.rest_8_) | copy-start | bytes 393220
  13.0 9.6 %collective-permute-start.4 = (bf16[128,512]{1,0:T(8,128)(2,1)S(1)}, bf16[128,512]{1,0:T(8,128)(2,1)S(1)}, u32[]{:S(2)}, u32[]{:S(2)}) collective-permute-start(bf16[128,512]{1,0:T(8,128)(2,1)S(1)} %collective-permute-done.3.rest_4_.rest_8_), channel_id=1, source_target_pairs={{0,4},{4,0},{8,12},{12,8},{16,20},{20,16},{24,28},{28,24},{1,5},{5... | collective-permute-start | bytes 393224 | tf_op jit(solution)/shard_map/ppermute | solution.py:298
  13.1 9.7 %copy-start.13 = (bf16[128,512]{1,0:T(8,128)(2,1)}, bf16[128,512]{1,0:T(8,128)(2,1)S(1)}, u32[]{:S(2)}) copy-start(bf16[128,512]{1,0:T(8,128)(2,1)S(1)} %collective-permute-done.5.rest_6_.rest_10_) | copy-start | bytes 393220
  13.1 9.6 %collective-permute-start.6 = (bf16[128,512]{1,0:T(8,128)(2,1)S(1)}, bf16[128,512]{1,0:T(8,128)(2,1)S(1)}, u32[]{:S(2)}, u32[]{:S(2)}) collective-permute-start(bf16[128,512]{1,0:T(8,128)(2,1)S(1)} %collective-permute-done.5.rest_6_.rest_10_), channel_id=1, source_target_pairs={{0,4},{4,0},{8,12},{12,8},{16,20},{20,16},{24,28},{28,24},{1,5},{5... | collective-permute-start | bytes 393224 | tf_op jit(solution)/shard_map/ppermute | solution.py:298
  16.8 14.6 %collective-permute-start.7 = (bf16[32,4736]{1,0:T(8,128)(2,1)}, bf16[32,4736]{1,0:T(8,128)(2,1)S(1)}, u32[]{:S(2)}, u32[]{:S(2)}) collective-permute-start(bf16[32,4736]{1,0:T(8,128)(2,1)} %get-tuple-element.29), channel_id=1, source_target_pairs={{0,1},{1,0},{2,3},{3,2},{4,5},{5,4},{6,7},{7,6},{8,9},{9,8},{10,11... | collective-permute-start | bytes 909320 | tf_op jit(solution)/shard_map/ppermute | solution.py:298
  19.8 2.9 %copy-start.14 = (bf16[128,512]{1,0:T(8,128)(2,1)}, bf16[128,512]{1,0:T(8,128)(2,1)S(1)}, u32[]{:S(2)}) copy-start(bf16[128,512]{1,0:T(8,128)(2,1)S(1)} %collective-permute-done.rest_1_.rest_5_) | copy-start | bytes 393220
  19.8 24.2 %collective-permute-start.8 = (bf16[32,4736]{1,0:T(8,128)(2,1)}, bf16[32,4736]{1,0:T(8,128)(2,1)S(1)}, u32[]{:S(2)}, u32[]{:S(2)}) collective-permute-start(bf16[32,4736]{1,0:T(8,128)(2,1)} %get-tuple-element.30), channel_id=1, source_target_pairs={{0,2},{1,3},{2,0},{3,1},{4,6},{5,7},{6,4},{7,5},{8,10},{9,11},{10,... | collective-permute-start | bytes 909320 | tf_op jit(solution)/shard_map/ppermute | solution.py:298
  22.4 0.7 copy-start.15
  22.4 21.6 %collective-permute-start.9 = (bf16[32,4736]{1,0:T(8,128)(2,1)}, bf16[32,4736]{1,0:T(8,128)(2,1)S(1)}, u32[]{:S(2)}, u32[]{:S(2)}) collective-permute-start(bf16[32,4736]{1,0:T(8,128)(2,1)} %get-tuple-element.31), channel_id=1, source_target_pairs={{0,3},{1,2},{2,1},{3,0},{4,7},{5,6},{6,5},{7,4},{8,11},{9,10},{10,... | collective-permute-start | bytes 909320 | tf_op jit(solution)/shard_map/ppermute | solution.py:298
  22.7 0.6 copy-start.16
  22.7 0.7 copy-start.17
  31.4 12.6 %copy-start.8 = (bf16[32,4736]{1,0:T(8,128)(2,1)}, bf16[32,4736]{1,0:T(8,128)(2,1)S(1)}, u32[]{:S(2)}) copy-start(bf16[32,4736]{1,0:T(8,128)(2,1)S(1)} %collective-permute-done.7.rest_1_) | copy-start | bytes 909316
  44.0 0.7 copy-start.9
  44.0 0.8 %copy-start.10 = (bf16[32,4736]{1,0:T(8,128)(2,1)}, bf16[32,4736]{1,0:T(8,128)(2,1)S(1)}, u32[]{:S(2)}) copy-start(bf16[32,4736]{1,0:T(8,128)(2,1)S(1)} %collective-permute-done.9.rest_3_) | copy-start | bytes 909316
  55.5 8.4 %collective-permute-start.10 = (bf16[4,128,512]{2,1,0:T(8,128)(2,1)}, bf16[4,128,512]{2,1,0:T(8,128)(2,1)S(1)}, u32[]{:S(2)}, u32[]{:S(2)}) collective-permute-start(bf16[4,128,512]{2,1,0:T(8,128)(2,1)} %get-tuple-element.34), channel_id=1, source_target_pairs={{0,4},{4,0},{8,12},{12,8},{16,20},{20,16},{24,28},{28,24},{1,5},{5... | collective-permute-start | bytes 1572872 | tf_op jit(solution)/shard_map/ppermute | solution.py:298
  55.5 13.9 %collective-permute-start.14 = (bf16[32,2560]{1,0:T(8,128)(2,1)}, bf16[32,2560]{1,0:T(8,128)(2,1)S(1)}, u32[]{:S(2)}, u32[]{:S(2)}) collective-permute-start(bf16[32,2560]{1,0:T(8,128)(2,1)} %get-tuple-element.40), channel_id=1, source_target_pairs={{0,1},{1,0},{2,3},{3,2},{4,5},{5,4},{6,7},{7,6},{8,9},{9,8},{10,11... | collective-permute-start | bytes 491528 | tf_op jit(solution)/shard_map/ppermute | solution.py:298
  61.4 15.2 %collective-permute-start.15 = (bf16[32,2560]{1,0:T(8,128)(2,1)}, bf16[32,2560]{1,0:T(8,128)(2,1)S(1)}, u32[]{:S(2)}, u32[]{:S(2)}) collective-permute-start(bf16[32,2560]{1,0:T(8,128)(2,1)} %get-tuple-element.41), channel_id=1, source_target_pairs={{0,2},{1,3},{2,0},{3,1},{4,6},{5,7},{6,4},{7,5},{8,10},{9,11},{10,... | collective-permute-start | bytes 491528 | tf_op jit(solution)/shard_map/ppermute | solution.py:298
  62.5 14.1 %collective-permute-start.16 = (bf16[32,2560]{1,0:T(8,128)(2,1)}, bf16[32,2560]{1,0:T(8,128)(2,1)S(1)}, u32[]{:S(2)}, u32[]{:S(2)}) collective-permute-start(bf16[32,2560]{1,0:T(8,128)(2,1)} %get-tuple-element.42), channel_id=1, source_target_pairs={{0,3},{1,2},{2,1},{3,0},{4,7},{5,6},{6,5},{7,4},{8,11},{9,10},{10,... | collective-permute-start | bytes 491528 | tf_op jit(solution)/shard_map/ppermute | solution.py:298
  63.9 0.8 copy-start
  66.9 9.7 %collective-permute-start.11 = (bf16[128,512]{1,0:T(8,128)(2,1)}, bf16[128,512]{1,0:T(8,128)(2,1)S(1)}, u32[]{:S(2)}, u32[]{:S(2)}) collective-permute-start(bf16[128,512]{1,0:T(8,128)(2,1)} %get-tuple-element.36), channel_id=1, source_target_pairs={{0,8},{4,12},{8,0},{12,4},{16,24},{20,28},{24,16},{28,20},{1,9},{5... | collective-permute-start | bytes 393224 | tf_op jit(solution)/shard_map/ppermute | solution.py:298
  68.0 8.6 %collective-permute-start.12 = (bf16[128,512]{1,0:T(8,128)(2,1)}, bf16[128,512]{1,0:T(8,128)(2,1)S(1)}, u32[]{:S(2)}, u32[]{:S(2)}) collective-permute-start(bf16[128,512]{1,0:T(8,128)(2,1)} %get-tuple-element.37), channel_id=1, source_target_pairs={{0,16},{4,20},{8,24},{12,28},{16,0},{20,4},{24,8},{28,12},{1,17},{... | collective-permute-start | bytes 393224 | tf_op jit(solution)/shard_map/ppermute | solution.py:298
  69.5 7.2 %copy-start.1 = (bf16[32,2560]{1,0:T(8,128)(2,1)}, bf16[32,2560]{1,0:T(8,128)(2,1)S(1)}, u32[]{:S(2)}) copy-start(bf16[32,2560]{1,0:T(8,128)(2,1)S(1)} %collective-permute-done.14.rest_4_) | copy-start | bytes 491524
  69.5 7.2 %collective-permute-start.13 = (bf16[128,512]{1,0:T(8,128)(2,1)}, bf16[128,512]{1,0:T(8,128)(2,1)S(1)}, u32[]{:S(2)}, u32[]{:S(2)}) collective-permute-start(bf16[128,512]{1,0:T(8,128)(2,1)} %get-tuple-element.38), channel_id=1, source_target_pairs={{0,24},{4,28},{8,16},{12,20},{16,8},{20,12},{24,0},{28,4},{1,25},{... | collective-permute-start | bytes 393224 | tf_op jit(solution)/shard_map/ppermute | solution.py:298
  76.6 0.7 copy-start.2
  76.7 0.7 copy-start.3
  76.7 0.8 copy-start.4
  76.7 0.8 %copy-start.5 = (bf16[128,512]{1,0:T(8,128)(2,1)}, bf16[128,512]{1,0:T(8,128)(2,1)S(1)}, u32[]{:S(2)}) copy-start(bf16[128,512]{1,0:T(8,128)(2,1)S(1)} %collective-permute-done.12.rest_1_) | copy-start | bytes 393220
  76.7 0.8 %copy-start.6 = (bf16[128,512]{1,0:T(8,128)(2,1)}, bf16[128,512]{1,0:T(8,128)(2,1)S(1)}, u32[]{:S(2)}) copy-start(bf16[128,512]{1,0:T(8,128)(2,1)S(1)} %collective-permute-done.13.rest_2_) | copy-start | bytes 393220

commit v2 on v1

--- a/solution.py
+++ b/solution.py
@@ -57,40 +57,44 @@
     )
 
 
-def pack_kernel(me_ref, q_ref, do_ref, o_ref, k_ref, v_ref, lse_ref, *outs):
+def pack_rows(dest, heads, q_ref, do_ref, o_ref, lse_ref, out):
+    rows, width = q_ref.shape
+    all_heads = lse_ref.shape[1]
+    lse_column = lax.broadcasted_iota(jnp.int32, (all_heads, HEAD), 0)
+    lse_lane = lax.broadcasted_iota(jnp.int32, (all_heads, HEAD), 1)
+    lane = lax.broadcasted_iota(jnp.int32, (rows, HEAD), 1)
+    delta = jnp.zeros((rows, HEAD), F32)
+    for h in range(heads):
+        cols = slice(h * HEAD, (h + 1) * HEAD)
+        product = do_ref[:, cols].astype(F32) * o_ref[:, cols].astype(F32)
+        here = (lane == heads + h) | (lane == 2 * heads + h)
+        delta = jnp.where(here, jnp.sum(product, axis=1, keepdims=True), delta)
+    out[:, :width] = q_ref[...]
+    out[:, width : 2 * width] = do_ref[...]
+    lse_pick = jnp.where((lse_column == lse_lane + dest * heads) & (lse_lane < heads), 1.0, 0.0)
+    lse = dot_nn(lse_ref[...], lse_pick.astype(BF))
+    delta_high = delta.astype(BF).astype(F32)
+    stats = jnp.where(lane < heads, lse, jnp.where(lane < 2 * heads, delta_high, delta - delta_high))
+    out[:, 2 * width : 2 * width + HEAD] = stats.astype(BF)
+
+
+def pack_kernel(me_ref, q_ref, do_ref, o_ref, lse_ref, k_ref, v_ref, pk_ref, pv_ref, kv_out, *outs):
     parts = len(outs)
     width = q_ref.shape[1] // parts
     narrow = k_ref.shape[1] // parts
-    heads = width // HEAD
-    rows = q_ref.shape[0]
+    start = 2 * width + HEAD
     me = me_ref[0]
-    column = lax.broadcasted_iota(jnp.int32, (width, HEAD), 0) // HEAD
-    lane = lax.broadcasted_iota(jnp.int32, (width, HEAD), 1)
-    pick = jnp.where((lane == column + heads) | (lane == column + 2 * heads), 1.0, 0.0).astype(BF)
-    all_heads = lse_ref.shape[1]
-    lse_column = lax.broadcasted_iota(jnp.int32, (all_heads, HEAD), 0)
-    lse_lane = lax.broadcasted_iota(jnp.int32, (all_heads, HEAD), 1)
-    out_lane = lax.broadcasted_iota(jnp.int32, (rows, HEAD), 1)
+    kv_out[:, :narrow] = pk_ref[...]
+    kv_out[:, narrow:] = pv_ref[...]
     for k, out in enumerate(outs):
         dest = me ^ k
         wide = pl.ds(pl.multiple_of(dest * width, HEAD), width)
         thin = pl.ds(pl.multiple_of(dest * narrow, HEAD), narrow)
-        grads = do_ref[:, wide]
-        out[:, :width] = q_ref[:, wide]
-        out[:, width : 2 * width] = grads
-        out[:, 2 * width : 2 * width + narrow] = k_ref[:, thin]
-        out[:, 2 * width + narrow : 2 * width + 2 * narrow] = v_ref[:, thin]
-        high, low = split_sum(grads.astype(F32) * o_ref[:, wide].astype(F32))
-        delta = dot_nn(high, pick) + dot_nn(low, pick)
-        lse_pick = jnp.where(
-            (lse_column == lse_lane + dest * heads) & (lse_lane < heads), 1.0, 0.0
-        ).astype(BF)
-        lse = dot_nn(lse_ref[...], lse_pick)
-        delta_high = delta.astype(BF).astype(F32)
-        stats = jnp.where(
-            out_lane < heads, lse, jnp.where(out_lane < 2 * heads, delta_high, delta - delta_high)
+        pack_rows(
+            dest, width // HEAD, q_ref.at[:, wide], do_ref.at[:, wide], o_ref.at[:, wide], lse_ref, out
         )
-        out[:, 2 * width + 2 * narrow :] = stats.astype(BF)
+        out[:, start : start + narrow] = k_ref[:, thin]
+        out[:, start + narrow :] = v_ref[:, thin]
 
 
 def prompt_kernel(members, me_ref, q_ref, do_ref, o_ref, lse_ref, *rest):
@@ -100,6 +104,7 @@
     half = rows // 2
     narrow = kv_refs[0].shape[1] // 2
     groups = narrow // HEAD
+    heads = lse_ref.shape[0]
     me = me_ref[0]
     count = members * half
     ones = jnp.ones((8, HEAD), BF)
@@ -108,6 +113,10 @@
     key_row = lax.broadcasted_iota(jnp.int32, (chunk, 1), 0)
     query_row = lax.broadcasted_iota(jnp.int32, (1, count), 1) % half
     stat_lane = lax.broadcasted_iota(jnp.int32, (half, HEAD), 1)
+    spread = (
+        lax.broadcasted_iota(jnp.int32, (heads, HEAD), 0) == lax.broadcasted_iota(jnp.int32, (heads, HEAD), 1)
+    )
+    all_lse = dot_tn(lse_ref[...], jnp.where(spread, 1.0, 0.0).astype(BF))
     for g in range(groups):
         queries, grads, lse_rows, delta_rows = [], [], [], []
         for s in range(2):
@@ -117,12 +126,11 @@
             outs = stacked_heads(o_ref, low, high, 0, g, members)
             up, down = split_sum(grads[s].astype(F32) * outs.astype(F32))
             delta_rows.append((dot_nt(ones, up) + dot_nt(ones, down))[0:1])
-            lse = lse_ref[low:high, :]
+            lse = all_lse[low:high]
             picked = jnp.concatenate(
-                [jnp.where(stat_lane == g * members + h, lse, jnp.zeros_like(lse)) for h in range(members)],
-                axis=0,
+                [jnp.where(stat_lane == g * members + h, lse, 0.0) for h in range(members)], axis=0
             )
-            lse_rows.append(dot_nt(ones, picked)[0:1] * LOG2E)
+            lse_rows.append(dot_nt(ones, picked.astype(BF))[0:1] * LOG2E)
         grad_queries = [None, None]
         for side in range(2):
             for c in range(slots // chunk_slots):
@@ -150,8 +158,9 @@
                 for t in range(chunk_slots):
                     piece = slice(t * half, (t + 1) * half)
                     slot = c * chunk_slots + t
-                    part_ref[slot, span, g * HEAD : (g + 1) * HEAD] = grad_key[piece]
-                    part_ref[slot, span, narrow + g * HEAD : narrow + (g + 1) * HEAD] = grad_value[piece]
+                    for total, at in ((grad_key, g * HEAD), (grad_value, narrow + g * HEAD)):
+                        cols = slice(at, at + HEAD)
+                        part_ref[slot, span, cols] = total[piece]
         for s in range(2):
             result = (grad_queries[s] * SCALE).astype(BF)
             for h in range(members):
@@ -193,13 +202,13 @@
         grads = jnp.concatenate([stacked_heads(p, 0, rows, width, g, members) for p in packs], axis=0)
         picked = []
         for p in packs:
-            stats = p[:, 2 * width + 2 * narrow :]
+            stats = p[:, 2 * width : 2 * width + HEAD]
             for h in range(members):
                 picked.append(jnp.where(lane_head == g * members + h, stats, jnp.zeros_like(stats)))
         stat_rows = dot_nt(pick, jnp.concatenate(picked, axis=0))
         lse_row = stat_rows[0:1] * LOG2E
         delta_row = stat_rows[1:2]
-        first = 2 * width + g * HEAD
+        first = 2 * width + HEAD + g * HEAD
         own_keys = jnp.concatenate([p[:, first : first + HEAD] for p in packs], axis=0)
         own_values = jnp.concatenate([p[:, first + narrow : first + narrow + HEAD] for p in packs], axis=0)
         grad_query, own_dk, own_dv = tile_grads(
@@ -276,8 +285,7 @@
 SMEM = pl.BlockSpec(memory_space=pltpu.SMEM)
 
 
-def call(kernel, name, outs, args, flops=0, scalar=True):
-    moved = sum(math.prod(a.shape) * a.dtype.itemsize for a in list(args) + list(outs))
+def call(kernel, name, outs, args, scalar=True):
     return pl.pallas_call(
         kernel,
         name=name,
@@ -285,7 +293,7 @@
         in_specs=[SMEM] * scalar + [VMEM] * (len(args) - scalar),
         out_specs=[VMEM] * len(outs),
         compiler_params=pltpu.CompilerParams(vmem_limit_bytes=VMEM_LIMIT),
-        cost_estimate=pl.CostEstimate(flops=flops, bytes_accessed=moved, transcendentals=0),
+        cost_estimate=pl.CostEstimate(flops=0, bytes_accessed=0, transcendentals=0),
     )(*args)
 
 
@@ -321,33 +329,35 @@
     members = width // narrow
     heads = width // HEAD
     rows = roll_query.shape[0]
-    packed = 2 * width + 2 * narrow + HEAD
-
-    packs = call(
+    packed = 2 * width + HEAD + 2 * narrow
+
+    kv, *packs = call(
         pack_kernel,
         "pack",
-        [shape((rows, packed), BF)] * parts,
-        (roll_id, roll_query, roll_dout, roll_out, rollout_key_rows, rollout_value_rows, roll_lse),
-    )
-    kv = jnp.concatenate([prompt_key_rows, prompt_value_rows], axis=1)
-    got = [packs[0]] + [None] * (parts - 1)
-    for k in sorted(range(1, parts), key=lambda k: (k % 2 == 0, k)):
-        got[k] = swap(packs[k], "roll", k)
-
+        [shape((prompt_rows, 2 * narrow), BF)] + [shape((rows, packed), BF)] * parts,
+        (
+            roll_id,
+            roll_query,
+            roll_dout,
+            roll_out,
+            roll_lse,
+            rollout_key_rows,
+            rollout_value_rows,
+            prompt_key_rows,
+            prompt_value_rows,
+        ),
+    )
+    got = [swap(x, "roll", k) if k else x for k, x in enumerate(packs)]
     blocks = [None] * slots
     for s in range(0, slots, 2):
-        blocks[s] = kv if s == 0 else swap(kv, "ctx", s)
-    for s in range(0, slots, 2):
+        blocks[s] = swap(kv, "ctx", s) if s else kv
         blocks[s + 1] = swap(blocks[s], "ctx", 1)
 
-    lse_padded = jnp.pad(prompt_lse, ((0, 0), (0, HEAD - heads)))
-    unit = 2 * 5 * heads * HEAD * prompt_rows * slots
     prompt_dq, part = call(
         functools.partial(prompt_kernel, members),
         "prompt_grads",
         [shape((prompt_rows, width), BF), shape((slots, prompt_rows, 2 * narrow), F32)],
-        (ctx_id, prompt_query, prompt_dout, prompt_out, lse_padded, *blocks),
-        flops=unit * prompt_rows * 3 // 2,
+        (ctx_id, prompt_query, prompt_dout, prompt_out, prompt_lse.T, *blocks),
     )
     even, odd, *backs = call(
         functools.partial(roll_kernel, parts, slots, members),
@@ -358,12 +368,9 @@
         ]
         + [shape((rows, width + 2 * narrow), BF)] * parts,
         (roll_id, *got, *blocks, part),
-        flops=unit * rows * parts * 2,
-    )
-    returned = [backs[0]] + [None] * (parts - 1)
-    for k in sorted(range(1, parts), key=lambda k: (k % 2 == 0, k)):
-        returned[k] = swap(backs[k], "roll", k)
+    )
     odd_got = swap(odd, "ctx", 1)
+    backs = [swap(x, "roll", k) if k else x for k, x in enumerate(backs)]
     own, *sums = call(
         add_kernel,
         "pair_sum",
@@ -382,7 +389,7 @@
             shape((rows, parts * narrow), BF),
             shape((rows, parts * narrow), BF),
         ],
-        (roll_id, own, *sums, *returned),
+        (roll_id, own, *sums, *backs),
     )
     return prompt_dq, prompt_dk, prompt_dv, roll_dq, roll_dk, roll_dv
 

time: 80.4 us -> 69.5 us (0.86)
  waiting for transfers between devices: 25.1 us -> 18.7 us
  local copies, waits for them, and re-layouts: 6.18 us -> 3.07 us
    ppermute x17, waiting for transfers between devices: 25.1 us -> 18.7 us  [swap(): return lax.ppermute(x, axis, [(i, i ^ k) for i in range(n)])]
    unnamed x38 -> x34, local copies, waits for them, and re-layouts: 4.71 us -> 3.07 us
    concatenate x1 -> x0, local copies, waits for them, and re-layouts: 0.84 us -> none  [on_device(): kv = jnp.concatenate([prompt_key_rows, prompt_value_rows], axis=1)]
  transfers between devices with their start and end apart: 17 -> 17, of which waited for: 5 -> 6; matrix products, arithmetic and copies ran while one was open for 2% -> 0% of each run, Pallas kernels for 17% -> 15%
where the time goes in v2:
time: 69.5 us; the launch traced here: 69.1 us
  Pallas kernels  25.9 us (37%)
  starting transfers between devices  20.7 us (30%)
  waiting for transfers between devices  18.7 us (27%)
  local copies, waits for them, and re-layouts  3.07 us (4%)
  between operations  0.78 us (1%)
    pallas_call x5, Pallas kernels, call(): pl.pallas_call(kernel, name=name, out_shape=outs, in_specs=[SMEM] * scala...  25.9 us
    ppermute x17, starting transfers between devices, swap(): return lax.ppermute(x, axis, [(i, i ^ k) for i in range(n)])  20.7 us
    ppermute x17, waiting for transfers between devices, swap(): return lax.ppermute(x, axis, [(i, i ^ k) for i in range(n)])  18.7 us
    unnamed x34, local copies, waits for them, and re-layouts  3.07 us
  transfers between devices with their start and end apart: 17, of which 6 were waited for; matrix products, arithmetic and copies ran while one was open for 0% of the time, Pallas kernels for 15%

profile of v2, /device:TPU:0, one launch (start us, length us, event | category | flops | bytes accessed | tf_op | source)
XLA Modules:
  0.0 69.1 jit_solution(15474457742539788440)
XLA Ops:
  0.6 2.8 %pack.1 = (bf16[128,512]{1,0:T(8,128)(2,1)}, bf16[32,4736]{1,0:T(8,128)(2,1)}, bf16[32,4736]{1,0:T(8,128)(2,1)}, bf16[32,4736]{1,0:T(8,128)(2,1)}, bf16[32,4736]{1,0:T(8,128)(2,1)}) custom-call(s32[1]{0:T(128)} %bitcast.2.me_ref, bf16[32,8192]{1,0:T(8,128)(2,1)} %q_ref.2, bf16[32,8192]{1,0:T(8,128)(2,1)} %do_ref.2, bf16[32,8192]{1,0:T(8,128)(2,1)} %o_ref.2, ...), custom_call_target="tpu_custom_call" | custom-call | tf_op jit(solution)/shard_map/pack/pallas_call | solution.py:289
  3.4 0.5 collective-permute-start
  3.9 2.5 %collective-permute-start.1 = (bf16[128,512]{1,0:T(8,128)(2,1)}, bf16[128,512]{1,0:T(8,128)(2,1)S(1)}, u32[]{:S(2)}, u32[]{:S(2)}) collective-permute-start(bf16[128,512]{1,0:T(8,128)(2,1)} %get-tuple-element.28.rest_0_.rest_4_), channel_id=1, source_target_pairs={{0,8},{4,12},{8,0},{12,4},{16,24},{20,28},{24,16},{28,20},{1,9},{5... | collective-permute-start | bytes 393224 | tf_op jit(solution)/shard_map/ppermute | solution.py:306
  6.4 1.5 %collective-permute-start.3 = (bf16[128,512]{1,0:T(8,128)(2,1)}, bf16[128,512]{1,0:T(8,128)(2,1)S(1)}, u32[]{:S(2)}, u32[]{:S(2)}) collective-permute-start(bf16[128,512]{1,0:T(8,128)(2,1)} %get-tuple-element.28.rest_0_.rest_4_), channel_id=1, source_target_pairs={{0,16},{4,20},{8,24},{12,28},{16,0},{20,4},{24,8},{28,12},{1,17},{... | collective-permute-start | bytes 393224 | tf_op jit(solution)/shard_map/ppermute | solution.py:306
  7.9 1.6 %collective-permute-start.7 = (bf16[32,4736]{1,0:T(8,128)(2,1)}, bf16[32,4736]{1,0:T(8,128)(2,1)S(1)}, u32[]{:S(2)}, u32[]{:S(2)}) collective-permute-start(bf16[32,4736]{1,0:T(8,128)(2,1)} %get-tuple-element.31), channel_id=1, source_target_pairs={{0,1},{1,0},{2,3},{3,2},{4,5},{5,4},{6,7},{7,6},{8,9},{9,8},{10,11... | collective-permute-start | bytes 909320 | tf_op jit(solution)/shard_map/ppermute | solution.py:306
  9.5 2.6 %collective-permute-start.8 = (bf16[32,4736]{1,0:T(8,128)(2,1)}, bf16[32,4736]{1,0:T(8,128)(2,1)S(1)}, u32[]{:S(2)}, u32[]{:S(2)}) collective-permute-start(bf16[32,4736]{1,0:T(8,128)(2,1)} %get-tuple-element.32), channel_id=1, source_target_pairs={{0,2},{1,3},{2,0},{3,1},{4,6},{5,7},{6,4},{7,5},{8,10},{9,11},{10,... | collective-permute-start | bytes 909320 | tf_op jit(solution)/shard_map/ppermute | solution.py:306
  12.1 0.0 collective-permute-done.rest_1_.rest_5_
  12.1 0.2 collective-permute-start.9
  12.3 0.0 collective-permute-done.1.rest_2_.rest_6_
  12.3 1.2 %collective-permute-start.5 = (bf16[128,512]{1,0:T(8,128)(2,1)}, bf16[128,512]{1,0:T(8,128)(2,1)S(1)}, u32[]{:S(2)}, u32[]{:S(2)}) collective-permute-start(bf16[128,512]{1,0:T(8,128)(2,1)} %get-tuple-element.28.rest_0_.rest_4_), channel_id=1, source_target_pairs={{0,24},{4,28},{8,16},{12,20},{16,8},{20,12},{24,0},{28,4},{1,25},{... | collective-permute-start | bytes 393224 | tf_op jit(solution)/shard_map/ppermute | solution.py:306
  13.4 0.0 collective-permute-done.3.rest_4_.rest_8_
  13.5 0.0 collective-permute-start.2
  13.5 4.9 %collective-permute-done.5.rest_6_.rest_10_ = bf16[128,512]{1,0:T(8,128)(2,1)S(1)} collective-permute-done((bf16[128,512]{1,0:T(8,128)(2,1)}, bf16[128,512]{1,0:T(8,128)(2,1)S(1)}, u32[]{:S(2)}, u32[]{:S(2)}) %collective-permute-start.5) | collective-permute-done | bytes 131104 | tf_op jit(solution)/shard_map/ppermute | solution.py:306
  18.4 0.0 collective-permute-start.4
  18.4 0.0 collective-permute-done.2.rest_3_.rest_7_
  18.4 0.5 collective-permute-start.6
  18.9 0.8 %collective-permute-done.4.rest_5_.rest_9_ = bf16[128,512]{1,0:T(8,128)(2,1)S(1)} collective-permute-done((bf16[128,512]{1,0:T(8,128)(2,1)S(1)}, bf16[128,512]{1,0:T(8,128)(2,1)S(1)}, u32[]{:S(2)}, u32[]{:S(2)}) %collective-permute-start.4) | collective-permute-done | bytes 131104 | tf_op jit(solution)/shard_map/ppermute | solution.py:306
  19.7 0.2 collective-permute-done.6.rest_7_.rest_11_
  19.9 0.4 copy-done.6
  20.4 0.2 copy-done.7
  20.6 8.1 %prompt_grads.1 = (bf16[128,2048]{1,0:T(8,128)(2,1)}, f32[8,128,512]{2,1,0:T(8,128)}) custom-call(s32[1]{0:T(128)} %bitcast.me_ref, bf16[128,2048]{1,0:T(8,128)(2,1)} %q_ref.3, bf16[128,2048]{1,0:T(8,128)(2,1)} %do_ref.3, bf16[128,2048]{1,0:T(8,128)(2,1)} %o_ref.3, bf16[16,128]{1,0:T(8,128)(2,1)} %bitcast.3, ...), custom_call_target="tpu_custom_call" | custom-call | tf_op jit(solution)/shard_map/prompt_grads/pallas_call | solution.py:289
  28.7 0.0 collective-permute-done.7.rest_1_
  28.7 5.0 %collective-permute-done.8.rest_2_ = bf16[32,4736]{1,0:T(8,128)(2,1)S(1)} collective-permute-done((bf16[32,4736]{1,0:T(8,128)(2,1)}, bf16[32,4736]{1,0:T(8,128)(2,1)S(1)}, u32[]{:S(2)}, u32[]{:S(2)}) %collective-permute-start.8) | collective-permute-done | bytes 303136 | tf_op jit(solution)/shard_map/ppermute | solution.py:306
  33.7 0.0 collective-permute-done.9.rest_3_
  33.7 0.7 %copy-done.9 = bf16[32,4736]{1,0:T(8,128)(2,1)} copy-done((bf16[32,4736]{1,0:T(8,128)(2,1)}, bf16[32,4736]{1,0:T(8,128)(2,1)S(1)}, u32[]{:S(2)}) %copy-start.9) | copy-done | bytes 303128
  34.4 0.1 copy-done.10
  34.5 10.5 %roll_grads.1 = (f32[4,128,512]{2,1,0:T(8,128)}, bf16[4,128,512]{2,1,0:T(8,128)(2,1)}, bf16[32,2560]{1,0:T(8,128)(2,1)}, bf16[32,2560]{1,0:T(8,128)(2,1)}, bf16[...) custom-call(s32[1]{0:T(128)} %bitcast.2.me_ref, bf16[32,4736]{1,0:T(8,128)(2,1)} %get-tuple-element.30.rest_0_, ...), custom_call_target="tpu_custom_call" | custom-call | tf_op jit(solution)/shard_map/roll_grads/pallas_call | solution.py:289
  45.0 0.0 collective-permute-start.10
  45.0 5.7 %collective-permute-start.14 = (bf16[32,2560]{1,0:T(8,128)(2,1)}, bf16[32,2560]{1,0:T(8,128)(2,1)S(1)}, u32[]{:S(2)}, u32[]{:S(2)}) collective-permute-start(bf16[32,2560]{1,0:T(8,128)(2,1)} %get-tuple-element.42), channel_id=1, source_target_pairs={{0,1},{1,0},{2,3},{3,2},{4,5},{5,4},{6,7},{7,6},{8,9},{9,8},{10,11... | collective-permute-start | bytes 491528 | tf_op jit(solution)/shard_map/ppermute | solution.py:306
  50.7 1.1 %collective-permute-start.15 = (bf16[32,2560]{1,0:T(8,128)(2,1)}, bf16[32,2560]{1,0:T(8,128)(2,1)S(1)}, u32[]{:S(2)}, u32[]{:S(2)}) collective-permute-start(bf16[32,2560]{1,0:T(8,128)(2,1)} %get-tuple-element.43), channel_id=1, source_target_pairs={{0,2},{1,3},{2,0},{3,1},{4,6},{5,7},{6,4},{7,5},{8,10},{9,11},{10,... | collective-permute-start | bytes 491528 | tf_op jit(solution)/shard_map/ppermute | solution.py:306
  51.8 1.4 %collective-permute-start.16 = (bf16[32,2560]{1,0:T(8,128)(2,1)}, bf16[32,2560]{1,0:T(8,128)(2,1)S(1)}, u32[]{:S(2)}, u32[]{:S(2)}) collective-permute-start(bf16[32,2560]{1,0:T(8,128)(2,1)} %get-tuple-element.44), channel_id=1, source_target_pairs={{0,3},{1,2},{2,1},{3,0},{4,7},{5,6},{6,5},{7,4},{8,11},{9,10},{10,... | collective-permute-start | bytes 491528 | tf_op jit(solution)/shard_map/ppermute | solution.py:306
  53.2 0.0 collective-permute-done.10.got_ref
  53.2 0.8 %copy-done = bf16[4,128,512]{2,1,0:T(8,128)(2,1)} copy-done((bf16[4,128,512]{2,1,0:T(8,128)(2,1)}, bf16[4,128,512]{2,1,0:T(8,128)(2,1)S(1)}, u32[]{:S(2)}) %copy-start) | copy-done | bytes 524312
  54.0 2.2 %pair_sum.1 = (f32[128,512]{1,0:T(8,128)}, bf16[128,512]{1,0:T(8,128)(2,1)}, bf16[128,512]{1,0:T(8,128)(2,1)}, bf16[128,512]{1,0:T(8,128)(2,1)}) custom-call(f32[4,128,512]{2,1,0:T(8,128)} %get-tuple-element.35.even_ref, bf16[4,128,512]{2,1,0:T(8,128)(2,1)} %copy-done), custom_call_target="tpu_custom_call" | custom-call | tf_op jit(solution)/shard_map/pair_sum/pallas_call | solution.py:289
  56.2 0.5 collective-permute-start.11
  56.7 0.5 collective-permute-start.12
  57.2 1.5 %collective-permute-done.14.rest_4_ = bf16[32,2560]{1,0:T(8,128)(2,1)S(1)} collective-permute-done((bf16[32,2560]{1,0:T(8,128)(2,1)}, bf16[32,2560]{1,0:T(8,128)(2,1)S(1)}, u32[]{:S(2)}, u32[]{:S(2)}) %collective-permute-start.14) | collective-permute-done | bytes 163872 | tf_op jit(solution)/shard_map/ppermute | solution.py:306
  58.8 0.9 %collective-permute-start.13 = (bf16[128,512]{1,0:T(8,128)(2,1)}, bf16[128,512]{1,0:T(8,128)(2,1)S(1)}, u32[]{:S(2)}, u32[]{:S(2)}) collective-permute-start(bf16[128,512]{1,0:T(8,128)(2,1)} %get-tuple-element.40), channel_id=1, source_target_pairs={{0,24},{4,28},{8,16},{12,20},{16,8},{20,12},{24,0},{28,4},{1,25},{... | collective-permute-start | bytes 393224 | tf_op jit(solution)/shard_map/ppermute | solution.py:306
  59.7 6.3 %collective-permute-done.15.rest_5_ = bf16[32,2560]{1,0:T(8,128)(2,1)S(1)} collective-permute-done((bf16[32,2560]{1,0:T(8,128)(2,1)}, bf16[32,2560]{1,0:T(8,128)(2,1)S(1)}, u32[]{:S(2)}, u32[]{:S(2)}) %collective-permute-start.15) | collective-permute-done | bytes 163872 | tf_op jit(solution)/shard_map/ppermute | solution.py:306
  65.9 0.0 collective-permute-done.16.rest_6_
  66.0 0.0 collective-permute-done.11.rest_0_
  66.0 0.0 collective-permute-done.12.rest_1_
  66.0 0.6 copy-done.12
  66.6 0.1 copy-done.13
  66.7 0.1 copy-done.14
  66.7 0.1 copy-done.15
  66.8 0.0 copy-done.16
  66.8 2.3 %finish.1 = (bf16[128,256]{1,0:T(8,128)(2,1)}, bf16[128,256]{1,0:T(8,128)(2,1)}, bf16[32,8192]{1,0:T(8,128)(2,1)}, bf16[32,1024]{1,0:T(8,128)(2,1)}, bf16[32,1024]{1,0:T(8,128)(2,1)}) custom-call(s32[1]{0:T(128)} %bitcast.2.me_ref, f32[128,512]{1,0:T(8,128)} %get-tuple-element.37.own_ref, bf16[128,512]{1,0:T(8,128)(2,1)} %copy-done.14, ...), custom_call_target="tpu_custom_call" | custom-call | tf_op jit(solution)/shard_map/finish/pallas_call | solution.py:289
  (25 shorter events, 0.0 us)
Async XLA Ops:
  3.4 8.6 %collective-permute-start = (bf16[128,512]{1,0:T(8,128)(2,1)}, bf16[128,512]{1,0:T(8,128)(2,1)S(1)}, u32[]{:S(2)}, u32[]{:S(2)}) collective-permute-start(bf16[128,512]{1,0:T(8,128)(2,1)} %get-tuple-element.28.rest_0_.rest_4_), channel_id=1, source_target_pairs={{0,4},{4,0},{8,12},{12,8},{16,20},{20,16},{24,28},{28,24},{1,5},{5... | collective-permute-start | bytes 393224 | tf_op jit(solution)/shard_map/ppermute | solution.py:306
  3.9 8.4 %collective-permute-start.1 = (bf16[128,512]{1,0:T(8,128)(2,1)}, bf16[128,512]{1,0:T(8,128)(2,1)S(1)}, u32[]{:S(2)}, u32[]{:S(2)}) collective-permute-start(bf16[128,512]{1,0:T(8,128)(2,1)} %get-tuple-element.28.rest_0_.rest_4_), channel_id=1, source_target_pairs={{0,8},{4,12},{8,0},{12,4},{16,24},{20,28},{24,16},{28,20},{1,9},{5... | collective-permute-start | bytes 393224 | tf_op jit(solution)/shard_map/ppermute | solution.py:306
  6.4 7.1 %collective-permute-start.3 = (bf16[128,512]{1,0:T(8,128)(2,1)}, bf16[128,512]{1,0:T(8,128)(2,1)S(1)}, u32[]{:S(2)}, u32[]{:S(2)}) collective-permute-start(bf16[128,512]{1,0:T(8,128)(2,1)} %get-tuple-element.28.rest_0_.rest_4_), channel_id=1, source_target_pairs={{0,16},{4,20},{8,24},{12,28},{16,0},{20,4},{24,8},{28,12},{1,17},{... | collective-permute-start | bytes 393224 | tf_op jit(solution)/shard_map/ppermute | solution.py:306
  7.9 20.8 %collective-permute-start.7 = (bf16[32,4736]{1,0:T(8,128)(2,1)}, bf16[32,4736]{1,0:T(8,128)(2,1)S(1)}, u32[]{:S(2)}, u32[]{:S(2)}) collective-permute-start(bf16[32,4736]{1,0:T(8,128)(2,1)} %get-tuple-element.31), channel_id=1, source_target_pairs={{0,1},{1,0},{2,3},{3,2},{4,5},{5,4},{6,7},{7,6},{8,9},{9,8},{10,11... | collective-permute-start | bytes 909320 | tf_op jit(solution)/shard_map/ppermute | solution.py:306
  9.5 24.2 %collective-permute-start.8 = (bf16[32,4736]{1,0:T(8,128)(2,1)}, bf16[32,4736]{1,0:T(8,128)(2,1)S(1)}, u32[]{:S(2)}, u32[]{:S(2)}) collective-permute-start(bf16[32,4736]{1,0:T(8,128)(2,1)} %get-tuple-element.32), channel_id=1, source_target_pairs={{0,2},{1,3},{2,0},{3,1},{4,6},{5,7},{6,4},{7,5},{8,10},{9,11},{10,... | collective-permute-start | bytes 909320 | tf_op jit(solution)/shard_map/ppermute | solution.py:306
  12.1 7.9 %copy-start.1 = (bf16[128,512]{1,0:T(8,128)(2,1)}, bf16[128,512]{1,0:T(8,128)(2,1)S(1)}, u32[]{:S(2)}) copy-start(bf16[128,512]{1,0:T(8,128)(2,1)S(1)} %collective-permute-done.rest_1_.rest_5_) | copy-start | bytes 393220
  12.1 21.6 %collective-permute-start.9 = (bf16[32,4736]{1,0:T(8,128)(2,1)}, bf16[32,4736]{1,0:T(8,128)(2,1)S(1)}, u32[]{:S(2)}, u32[]{:S(2)}) collective-permute-start(bf16[32,4736]{1,0:T(8,128)(2,1)} %get-tuple-element.33), channel_id=1, source_target_pairs={{0,3},{1,2},{2,1},{3,0},{4,7},{5,6},{6,5},{7,4},{8,11},{9,10},{10,... | collective-permute-start | bytes 909320 | tf_op jit(solution)/shard_map/ppermute | solution.py:306
  12.3 7.6 %copy-start.2 = (bf16[128,512]{1,0:T(8,128)(2,1)}, bf16[128,512]{1,0:T(8,128)(2,1)S(1)}, u32[]{:S(2)}) copy-start(bf16[128,512]{1,0:T(8,128)(2,1)S(1)} %collective-permute-done.1.rest_2_.rest_6_) | copy-start | bytes 393220
  12.3 6.1 %collective-permute-start.5 = (bf16[128,512]{1,0:T(8,128)(2,1)}, bf16[128,512]{1,0:T(8,128)(2,1)S(1)}, u32[]{:S(2)}, u32[]{:S(2)}) collective-permute-start(bf16[128,512]{1,0:T(8,128)(2,1)} %get-tuple-element.28.rest_0_.rest_4_), channel_id=1, source_target_pairs={{0,24},{4,28},{8,16},{12,20},{16,8},{20,12},{24,0},{28,4},{1,25},{... | collective-permute-start | bytes 393224 | tf_op jit(solution)/shard_map/ppermute | solution.py:306
  13.5 6.5 %copy-start.3 = (bf16[128,512]{1,0:T(8,128)(2,1)}, bf16[128,512]{1,0:T(8,128)(2,1)S(1)}, u32[]{:S(2)}) copy-start(bf16[128,512]{1,0:T(8,128)(2,1)S(1)} %collective-permute-done.3.rest_4_.rest_8_) | copy-start | bytes 393220
  13.5 4.9 %collective-permute-start.2 = (bf16[128,512]{1,0:T(8,128)(2,1)S(1)}, bf16[128,512]{1,0:T(8,128)(2,1)S(1)}, u32[]{:S(2)}, u32[]{:S(2)}) collective-permute-start(bf16[128,512]{1,0:T(8,128)(2,1)S(1)} %collective-permute-done.1.rest_2_.rest_6_), channel_id=1, source_target_pairs={{0,4},{4,0},{8,12},{12,8},{16,20},{20,16},{24,28},{28,24},{1,5},{5... | collective-permute-start | bytes 393224 | tf_op jit(solution)/shard_map/ppermute | solution.py:306
  18.4 1.6 %copy-start.4 = (bf16[128,512]{1,0:T(8,128)(2,1)}, bf16[128,512]{1,0:T(8,128)(2,1)S(1)}, u32[]{:S(2)}) copy-start(bf16[128,512]{1,0:T(8,128)(2,1)S(1)} %collective-permute-done.5.rest_6_.rest_10_) | copy-start | bytes 393220
  18.4 1.3 %collective-permute-start.4 = (bf16[128,512]{1,0:T(8,128)(2,1)S(1)}, bf16[128,512]{1,0:T(8,128)(2,1)S(1)}, u32[]{:S(2)}, u32[]{:S(2)}) collective-permute-start(bf16[128,512]{1,0:T(8,128)(2,1)S(1)} %collective-permute-done.3.rest_4_.rest_8_), channel_id=1, source_target_pairs={{0,4},{4,0},{8,12},{12,8},{16,20},{20,16},{24,28},{28,24},{1,5},{5... | collective-permute-start | bytes 393224 | tf_op jit(solution)/shard_map/ppermute | solution.py:306
  18.4 1.6 %copy-start.5 = (bf16[128,512]{1,0:T(8,128)(2,1)}, bf16[128,512]{1,0:T(8,128)(2,1)S(1)}, u32[]{:S(2)}) copy-start(bf16[128,512]{1,0:T(8,128)(2,1)S(1)} %collective-permute-done.2.rest_3_.rest_7_) | copy-start | bytes 393220
  18.4 1.5 %collective-permute-start.6 = (bf16[128,512]{1,0:T(8,128)(2,1)S(1)}, bf16[128,512]{1,0:T(8,128)(2,1)S(1)}, u32[]{:S(2)}, u32[]{:S(2)}) collective-permute-start(bf16[128,512]{1,0:T(8,128)(2,1)S(1)} %collective-permute-done.5.rest_6_.rest_10_), channel_id=1, source_target_pairs={{0,4},{4,0},{8,12},{12,8},{16,20},{20,16},{24,28},{28,24},{1,5},{5... | collective-permute-start | bytes 393224 | tf_op jit(solution)/shard_map/ppermute | solution.py:306
  19.7 0.7 copy-start.6
  19.9 0.7 copy-start.7
  28.7 5.0 %copy-start.8 = (bf16[32,4736]{1,0:T(8,128)(2,1)}, bf16[32,4736]{1,0:T(8,128)(2,1)S(1)}, u32[]{:S(2)}) copy-start(bf16[32,4736]{1,0:T(8,128)(2,1)S(1)} %collective-permute-done.7.rest_1_) | copy-start | bytes 909316
  33.7 0.7 %copy-start.9 = (bf16[32,4736]{1,0:T(8,128)(2,1)}, bf16[32,4736]{1,0:T(8,128)(2,1)S(1)}, u32[]{:S(2)}) copy-start(bf16[32,4736]{1,0:T(8,128)(2,1)S(1)} %collective-permute-done.8.rest_2_) | copy-start | bytes 909316
  33.7 0.8 %copy-start.10 = (bf16[32,4736]{1,0:T(8,128)(2,1)}, bf16[32,4736]{1,0:T(8,128)(2,1)S(1)}, u32[]{:S(2)}) copy-start(bf16[32,4736]{1,0:T(8,128)(2,1)S(1)} %collective-permute-done.9.rest_3_) | copy-start | bytes 909316
  45.0 8.2 %collective-permute-start.10 = (bf16[4,128,512]{2,1,0:T(8,128)(2,1)}, bf16[4,128,512]{2,1,0:T(8,128)(2,1)S(1)}, u32[]{:S(2)}, u32[]{:S(2)}) collective-permute-start(bf16[4,128,512]{2,1,0:T(8,128)(2,1)} %get-tuple-element.36), channel_id=1, source_target_pairs={{0,4},{4,0},{8,12},{12,8},{16,20},{20,16},{24,28},{28,24},{1,5},{5... | collective-permute-start | bytes 1572872 | tf_op jit(solution)/shard_map/ppermute | solution.py:306
  45.0 13.8 %collective-permute-start.14 = (bf16[32,2560]{1,0:T(8,128)(2,1)}, bf16[32,2560]{1,0:T(8,128)(2,1)S(1)}, u32[]{:S(2)}, u32[]{:S(2)}) collective-permute-start(bf16[32,2560]{1,0:T(8,128)(2,1)} %get-tuple-element.42), channel_id=1, source_target_pairs={{0,1},{1,0},{2,3},{3,2},{4,5},{5,4},{6,7},{7,6},{8,9},{9,8},{10,11... | collective-permute-start | bytes 491528 | tf_op jit(solution)/shard_map/ppermute | solution.py:306
  50.7 15.2 %collective-permute-start.15 = (bf16[32,2560]{1,0:T(8,128)(2,1)}, bf16[32,2560]{1,0:T(8,128)(2,1)S(1)}, u32[]{:S(2)}, u32[]{:S(2)}) collective-permute-start(bf16[32,2560]{1,0:T(8,128)(2,1)} %get-tuple-element.43), channel_id=1, source_target_pairs={{0,2},{1,3},{2,0},{3,1},{4,6},{5,7},{6,4},{7,5},{8,10},{9,11},{10,... | collective-permute-start | bytes 491528 | tf_op jit(solution)/shard_map/ppermute | solution.py:306
  51.8 14.1 %collective-permute-start.16 = (bf16[32,2560]{1,0:T(8,128)(2,1)}, bf16[32,2560]{1,0:T(8,128)(2,1)S(1)}, u32[]{:S(2)}, u32[]{:S(2)}) collective-permute-start(bf16[32,2560]{1,0:T(8,128)(2,1)} %get-tuple-element.44), channel_id=1, source_target_pairs={{0,3},{1,2},{2,1},{3,0},{4,7},{5,6},{6,5},{7,4},{8,11},{9,10},{10,... | collective-permute-start | bytes 491528 | tf_op jit(solution)/shard_map/ppermute | solution.py:306
  53.2 0.8 %copy-start = (bf16[4,128,512]{2,1,0:T(8,128)(2,1)}, bf16[4,128,512]{2,1,0:T(8,128)(2,1)S(1)}, u32[]{:S(2)}) copy-start(bf16[4,128,512]{2,1,0:T(8,128)(2,1)S(1)} %collective-permute-done.10.got_ref) | copy-start | bytes 1572868
  56.2 9.8 %collective-permute-start.11 = (bf16[128,512]{1,0:T(8,128)(2,1)}, bf16[128,512]{1,0:T(8,128)(2,1)S(1)}, u32[]{:S(2)}, u32[]{:S(2)}) collective-permute-start(bf16[128,512]{1,0:T(8,128)(2,1)} %get-tuple-element.38), channel_id=1, source_target_pairs={{0,8},{4,12},{8,0},{12,4},{16,24},{20,28},{24,16},{28,20},{1,9},{5... | collective-permute-start | bytes 393224 | tf_op jit(solution)/shard_map/ppermute | solution.py:306
  56.7 9.2 %collective-permute-start.12 = (bf16[128,512]{1,0:T(8,128)(2,1)}, bf16[128,512]{1,0:T(8,128)(2,1)S(1)}, u32[]{:S(2)}, u32[]{:S(2)}) collective-permute-start(bf16[128,512]{1,0:T(8,128)(2,1)} %get-tuple-element.39), channel_id=1, source_target_pairs={{0,16},{4,20},{8,24},{12,28},{16,0},{20,4},{24,8},{28,12},{1,17},{... | collective-permute-start | bytes 393224 | tf_op jit(solution)/shard_map/ppermute | solution.py:306
  58.8 7.2 %copy-start.11 = (bf16[32,2560]{1,0:T(8,128)(2,1)}, bf16[32,2560]{1,0:T(8,128)(2,1)S(1)}, u32[]{:S(2)}) copy-start(bf16[32,2560]{1,0:T(8,128)(2,1)S(1)} %collective-permute-done.14.rest_4_) | copy-start | bytes 491524
  58.8 7.2 %collective-permute-start.13 = (bf16[128,512]{1,0:T(8,128)(2,1)}, bf16[128,512]{1,0:T(8,128)(2,1)S(1)}, u32[]{:S(2)}, u32[]{:S(2)}) collective-permute-start(bf16[128,512]{1,0:T(8,128)(2,1)} %get-tuple-element.40), channel_id=1, source_target_pairs={{0,24},{4,28},{8,16},{12,20},{16,8},{20,12},{24,0},{28,4},{1,25},{... | collective-permute-start | bytes 393224 | tf_op jit(solution)/shard_map/ppermute | solution.py:306
  65.9 0.7 copy-start.12
  65.9 0.7 %copy-start.13 = (bf16[32,2560]{1,0:T(8,128)(2,1)}, bf16[32,2560]{1,0:T(8,128)(2,1)S(1)}, u32[]{:S(2)}) copy-start(bf16[32,2560]{1,0:T(8,128)(2,1)S(1)} %collective-permute-done.16.rest_6_) | copy-start | bytes 491524
  66.0 0.8 %copy-start.14 = (bf16[128,512]{1,0:T(8,128)(2,1)}, bf16[128,512]{1,0:T(8,128)(2,1)S(1)}, u32[]{:S(2)}) copy-start(bf16[128,512]{1,0:T(8,128)(2,1)S(1)} %collective-permute-done.11.rest_0_) | copy-start | bytes 393220
  66.0 0.8 %copy-start.15 = (bf16[128,512]{1,0:T(8,128)(2,1)}, bf16[128,512]{1,0:T(8,128)(2,1)S(1)}, u32[]{:S(2)}) copy-start(bf16[128,512]{1,0:T(8,128)(2,1)S(1)} %collective-permute-done.12.rest_1_) | copy-start | bytes 393220
  66.0 0.8 %copy-start.16 = (bf16[128,512]{1,0:T(8,128)(2,1)}, bf16[128,512]{1,0:T(8,128)(2,1)S(1)}, u32[]{:S(2)}) copy-start(bf16[128,512]{1,0:T(8,128)(2,1)S(1)} %collective-permute-done.13.rest_2_) | copy-start | bytes 393220

commit v3 on v2

--- a/solution.py
+++ b/solution.py
@@ -11,9 +11,8 @@
 HEAD = 128
 LOG2E = math.log2(math.e)
 SCALE = 1.0 / math.sqrt(HEAD)
-VMEM_LIMIT = 56 * 1024 * 1024
+VMEM_LIMIT = 28 * 1024 * 1024
 KEY_CHUNK = 512
-ROW_CHUNK = 512
 
 BF = jnp.bfloat16
 F32 = jnp.float32
@@ -46,7 +45,7 @@
     grad_scores = (probs * (grad_probs - delta_row)).astype(BF)
     grad_value = dot_nn(probs.astype(BF), grads)
     grad_key = dot_nn(grad_scores, queries)
-    grad_query = dot_tn(grad_scores, keys)
+    grad_query = dot_nn(keys.T, grad_scores)
     return grad_query, grad_key, grad_value
 
 
@@ -55,6 +54,26 @@
     return jnp.concatenate(
         [ref[low:high, first + h * HEAD : first + (h + 1) * HEAD] for h in range(members)], axis=0
     )
+
+
+def stat_rows(packs, group, members, heads, width):
+    rows = packs[0].shape[0]
+    stat_row = lax.broadcasted_iota(jnp.int32, (8, HEAD), 0)
+    stat_lane = lax.broadcasted_iota(jnp.int32, (8, HEAD), 1)
+    pick = jnp.where(
+        ((stat_row == 0) & (stat_lane < heads))
+        | ((stat_row == 1) & (stat_lane >= heads) & (stat_lane < 3 * heads)),
+        1.0,
+        0.0,
+    ).astype(BF)
+    lane_head = lax.broadcasted_iota(jnp.int32, (rows, HEAD), 1) % heads
+    picked = []
+    for p in packs:
+        stats = p[:, 2 * width : 2 * width + HEAD]
+        for h in range(members):
+            picked.append(jnp.where(lane_head == group * members + h, stats, jnp.zeros_like(stats)))
+    both = dot_nt(pick, jnp.concatenate(picked, axis=0))
+    return both[0:1] * LOG2E, both[1:2]
 
 
 def pack_rows(dest, heads, q_ref, do_ref, o_ref, lse_ref, out):
@@ -97,14 +116,15 @@
         out[:, start + narrow :] = v_ref[:, thin]
 
 
-def prompt_kernel(members, me_ref, q_ref, do_ref, o_ref, lse_ref, *rest):
-    kv_refs, (dq_ref, part_ref) = rest[:-2], rest[-2:]
+def prompt_kernel(members, me_ref, q_ref, do_ref, o_ref, lse_ref, roll_ref, *rest):
+    kv_refs, (dq_ref, part_ref, roll_dq_ref) = rest[:-3], rest[-3:]
     slots = len(kv_refs)
     rows = q_ref.shape[0]
     half = rows // 2
     narrow = kv_refs[0].shape[1] // 2
     groups = narrow // HEAD
     heads = lse_ref.shape[0]
+    width = q_ref.shape[1]
     me = me_ref[0]
     count = members * half
     ones = jnp.ones((8, HEAD), BF)
@@ -131,7 +151,12 @@
                 [jnp.where(stat_lane == g * members + h, lse, 0.0) for h in range(members)], axis=0
             )
             lse_rows.append(dot_nt(ones, picked.astype(BF))[0:1] * LOG2E)
-        grad_queries = [None, None]
+        queries.append(stacked_heads(roll_ref, 0, roll_ref.shape[0], 0, g, members))
+        grads.append(stacked_heads(roll_ref, 0, roll_ref.shape[0], width, g, members))
+        lse_row, delta_row = stat_rows([roll_ref], g, members, heads, width)
+        lse_rows.append(lse_row)
+        delta_rows.append(delta_row)
+        grad_queries = [None, None, None]
         for side in range(2):
             for c in range(slots // chunk_slots):
                 owned = kv_refs[c * chunk_slots : (c + 1) * chunk_slots]
@@ -143,7 +168,7 @@
                 owner = me ^ (c * chunk_slots + key_row // half)
                 offset = key_row % half
                 grad_key = grad_value = None
-                for s in (1, 0) if side == 0 else (1,):
+                for s in (1, 0, 2) if side == 0 else (1, 2):
                     mask = None
                     if s == side:
                         ahead = owner - me if side == 0 else me - owner
@@ -162,17 +187,18 @@
                         cols = slice(at, at + HEAD)
                         part_ref[slot, span, cols] = total[piece]
         for s in range(2):
-            result = (grad_queries[s] * SCALE).astype(BF)
+            result = (grad_queries[s] * SCALE).T.astype(BF)
             for h in range(members):
                 first = (g * members + h) * HEAD
                 dq_ref[s * half : (s + 1) * half, first : first + HEAD] = result[h * half : (h + 1) * half]
+        roll_dq_ref[g] = grad_queries[2]
 
 
 def roll_kernel(parts, slots, members, me_ref, *rest):
     packs, rest = rest[:parts], rest[parts:]
     kv_refs, rest = rest[:slots], rest[slots:]
-    part_ref, even_ref, odd_ref = rest[:3]
-    backs = rest[3:]
+    part_ref, roll_dq_ref, even_ref, odd_ref = rest[:4]
+    backs = rest[4:]
     me = me_ref[0]
     rows = packs[0].shape[0]
     kv_rows = kv_refs[0].shape[0]
@@ -182,17 +208,7 @@
     width = heads * HEAD
     block = members * rows
     count = parts * block
-    stat_row = lax.broadcasted_iota(jnp.int32, (8, HEAD), 0)
-    stat_lane = lax.broadcasted_iota(jnp.int32, (8, HEAD), 1)
-    pick = jnp.where(
-        ((stat_row == 0) & (stat_lane < heads))
-        | ((stat_row == 1) & (stat_lane >= heads) & (stat_lane < 3 * heads)),
-        1.0,
-        0.0,
-    ).astype(BF)
-    lane_head = lax.broadcasted_iota(jnp.int32, (rows, HEAD), 1) % heads
     chunk_slots = max(1, min(slots, KEY_CHUNK // kv_rows))
-    row_chunk = min(count, ROW_CHUNK)
     own_key = lax.broadcasted_iota(jnp.int32, (parts * rows, 1), 0)
     own_key_pos = (me ^ (own_key // rows)) * rows + own_key % rows
     own_query = lax.broadcasted_iota(jnp.int32, (1, count), 1)
@@ -200,14 +216,7 @@
     for g in range(groups):
         queries = jnp.concatenate([stacked_heads(p, 0, rows, 0, g, members) for p in packs], axis=0)
         grads = jnp.concatenate([stacked_heads(p, 0, rows, width, g, members) for p in packs], axis=0)
-        picked = []
-        for p in packs:
-            stats = p[:, 2 * width : 2 * width + HEAD]
-            for h in range(members):
-                picked.append(jnp.where(lane_head == g * members + h, stats, jnp.zeros_like(stats)))
-        stat_rows = dot_nt(pick, jnp.concatenate(picked, axis=0))
-        lse_row = stat_rows[0:1] * LOG2E
-        delta_row = stat_rows[1:2]
+        lse_row, delta_row = stat_rows(packs, g, members, heads, width)
         first = 2 * width + HEAD + g * HEAD
         own_keys = jnp.concatenate([p[:, first : first + HEAD] for p in packs], axis=0)
         own_values = jnp.concatenate([p[:, first + narrow : first + narrow + HEAD] for p in packs], axis=0)
@@ -220,22 +229,19 @@
             piece = slice(k * rows, (k + 1) * rows)
             back[:, width + g * HEAD : width + (g + 1) * HEAD] = own_dk[piece]
             back[:, width + narrow + g * HEAD : width + narrow + (g + 1) * HEAD] = own_dv[piece]
-        grad_rows = [grad_query[r : r + row_chunk] for r in range(0, count, row_chunk)]
+        own_grad = grad_query[:, :block] + roll_dq_ref[g]
+        others = slice(block, count)
+        other_grad = grad_query[:, others]
         for c in range(slots // chunk_slots):
             owned = kv_refs[c * chunk_slots : (c + 1) * chunk_slots]
             keys = jnp.concatenate([r[:, g * HEAD : (g + 1) * HEAD] for r in owned], axis=0)
             values = jnp.concatenate(
                 [r[:, narrow + g * HEAD : narrow + (g + 1) * HEAD] for r in owned], axis=0
             )
-            grad_key = grad_value = None
-            for i in range(count // row_chunk):
-                piece = slice(i * row_chunk, (i + 1) * row_chunk)
-                dq, dk, dv = tile_grads(
-                    keys, values, queries[piece], grads[piece], lse_row[:, piece], delta_row[:, piece], None
-                )
-                grad_rows[i] = grad_rows[i] + dq
-                grad_key = dk if grad_key is None else grad_key + dk
-                grad_value = dv if grad_value is None else grad_value + dv
+            dq, grad_key, grad_value = tile_grads(
+                keys, values, queries[others], grads[others], lse_row[:, others], delta_row[:, others], None
+            )
+            other_grad = other_grad + dq
             grad_key = grad_key * SCALE
             for t in range(chunk_slots):
                 slot = c * chunk_slots + t
@@ -247,7 +253,7 @@
                         even_ref[slot // 2, :, cols] = value
                     else:
                         odd_ref[slot // 2, :, cols] = value.astype(BF)
-        result = jnp.concatenate([(r * SCALE).astype(BF) for r in grad_rows], axis=0)
+        result = jnp.concatenate([(r * SCALE).T.astype(BF) for r in (own_grad, other_grad)], axis=0)
         for k, back in enumerate(backs):
             for h in range(members):
                 start = k * block + h * rows
@@ -255,24 +261,11 @@
                 back[:, first : first + HEAD] = result[start : start + rows]
 
 
-def add_kernel(even_ref, got_ref, own_ref, *outs):
-    own_ref[...] = even_ref[0] + got_ref[0].astype(F32)
-    for t, out in enumerate(outs):
-        out[...] = (even_ref[t + 1] + got_ref[t + 1].astype(F32)).astype(BF)
-
-
-def final_kernel(parts, others, me_ref, own_ref, *rest):
-    got, rest = rest[:others], rest[others:]
-    backs, outs = rest[:parts], rest[parts:]
-    pk_ref, pv_ref, rq_ref, rk_ref, rv_ref = outs
+def unpack_kernel(me_ref, *rest):
+    backs, (rq_ref, rk_ref, rv_ref) = rest[:-3], rest[-3:]
     me = me_ref[0]
-    total = own_ref[...]
-    for r in got:
-        total = total + r[...].astype(F32)
-    narrow = pk_ref.shape[1]
-    pk_ref[...] = total[:, :narrow].astype(BF)
-    pv_ref[...] = total[:, narrow:].astype(BF)
-    width = rq_ref.shape[1] // parts
+    width = rq_ref.shape[1] // len(backs)
+    narrow = rk_ref.shape[1] // len(backs)
     for k, back in enumerate(backs):
         dest = me ^ k
         rq_ref[:, pl.ds(pl.multiple_of(dest * width, HEAD), width)] = back[:, :width]
@@ -285,12 +278,14 @@
 SMEM = pl.BlockSpec(memory_space=pltpu.SMEM)
 
 
-def call(kernel, name, outs, args, scalar=True):
+def call(kernel, name, outs, args, scalar=True, unread=0):
     return pl.pallas_call(
         kernel,
         name=name,
         out_shape=outs,
-        in_specs=[SMEM] * scalar + [VMEM] * (len(args) - scalar),
+        in_specs=[SMEM] * scalar
+        + [VMEM] * (len(args) - scalar - unread)
+        + [pl.BlockSpec(memory_space=pl.ANY)] * unread,
         out_specs=[VMEM] * len(outs),
         compiler_params=pltpu.CompilerParams(vmem_limit_bytes=VMEM_LIMIT),
         cost_estimate=pl.CostEstimate(flops=0, bytes_accessed=0, transcendentals=0),
@@ -301,9 +296,21 @@
     return jax.ShapeDtypeStruct(dims, dtype)
 
 
+def vmem_shape(dims, dtype):
+    return pltpu.VMEM(dims, dtype)
+
+
 def swap(x, axis, k):
     n = lax.axis_size(axis)
     return lax.ppermute(x, axis, [(i, i ^ k) for i in range(n)])
+
+
+def in_hbm(x):
+    return pltpu.with_memory_space_constraint(x, pltpu.HBM)
+
+
+def in_vmem(x):
+    return pltpu.with_memory_space_constraint(x, pltpu.VMEM)
 
 
 def on_device(
@@ -334,17 +341,22 @@
     kv, *packs = call(
         pack_kernel,
         "pack",
-        [shape((prompt_rows, 2 * narrow), BF)] + [shape((rows, packed), BF)] * parts,
+        [vmem_shape((prompt_rows, 2 * narrow), BF)] + [vmem_shape((rows, packed), BF)] * parts,
         (
             roll_id,
-            roll_query,
-            roll_dout,
-            roll_out,
-            roll_lse,
-            rollout_key_rows,
-            rollout_value_rows,
-            prompt_key_rows,
-            prompt_value_rows,
+            *map(
+                in_hbm,
+                (
+                    roll_query,
+                    roll_dout,
+                    roll_out,
+                    roll_lse,
+                    rollout_key_rows,
+                    rollout_value_rows,
+                    prompt_key_rows,
+                    prompt_value_rows,
+                ),
+            ),
         ),
     )
     got = [swap(x, "roll", k) if k else x for k, x in enumerate(packs)]
@@ -352,44 +364,44 @@
     for s in range(0, slots, 2):
         blocks[s] = swap(kv, "ctx", s) if s else kv
         blocks[s + 1] = swap(blocks[s], "ctx", 1)
-
-    prompt_dq, part = call(
+    blocks = [in_vmem(x) for x in blocks]
+
+    prompt_dq, part, roll_own_dq = call(
         functools.partial(prompt_kernel, members),
         "prompt_grads",
-        [shape((prompt_rows, width), BF), shape((slots, prompt_rows, 2 * narrow), F32)],
-        (ctx_id, prompt_query, prompt_dout, prompt_out, prompt_lse.T, *blocks),
+        [
+            shape((prompt_rows, width), BF),
+            vmem_shape((slots, prompt_rows, 2 * narrow), F32),
+            vmem_shape((narrow // HEAD, HEAD, members * rows), F32),
+        ],
+        (ctx_id, prompt_query, prompt_dout, prompt_out, prompt_lse.T, in_vmem(packs[0]), *blocks),
     )
     even, odd, *backs = call(
         functools.partial(roll_kernel, parts, slots, members),
         "roll_grads",
         [
-            shape((slots // 2, prompt_rows, 2 * narrow), F32),
-            shape((slots // 2, prompt_rows, 2 * narrow), BF),
+            vmem_shape((slots // 2, prompt_rows, 2 * narrow), F32),
+            vmem_shape((slots // 2, prompt_rows, 2 * narrow), BF),
         ]
-        + [shape((rows, width + 2 * narrow), BF)] * parts,
-        (roll_id, *got, *blocks, part),
+        + [vmem_shape((rows, width + 2 * narrow), BF)] * parts,
+        (roll_id, *[in_vmem(x) for x in got], *blocks, in_vmem(part), in_vmem(roll_own_dq)),
     )
     odd_got = swap(odd, "ctx", 1)
-    backs = [swap(x, "roll", k) if k else x for k, x in enumerate(backs)]
-    own, *sums = call(
-        add_kernel,
-        "pair_sum",
-        [shape((prompt_rows, 2 * narrow), F32)] + [shape((prompt_rows, 2 * narrow), BF)] * (slots // 2 - 1),
-        (even, odd_got),
-        scalar=False,
-    )
-    sums = [swap(x, "ctx", 2 * (t + 1)) for t, x in enumerate(sums)]
-    prompt_dk, prompt_dv, roll_dq, roll_dk, roll_dv = call(
-        functools.partial(final_kernel, parts, len(sums)),
-        "finish",
+    backs = [in_vmem(swap(x, "roll", k) if k else x) for k, x in enumerate(backs)]
+    pair = [even[t] + odd_got[t].astype(F32) for t in range(slots // 2)]
+    total = pair[0]
+    for t in range(1, slots // 2):
+        total = total + swap(pair[t].astype(BF), "ctx", 2 * t).astype(F32)
+    prompt_dk, prompt_dv = total[:, :narrow].astype(BF), total[:, narrow:].astype(BF)
+    roll_dq, roll_dk, roll_dv = call(
+        unpack_kernel,
+        "unpack",
         [
-            shape((prompt_rows, narrow), BF),
-            shape((prompt_rows, narrow), BF),
             shape((rows, parts * width), BF),
             shape((rows, parts * narrow), BF),
             shape((rows, parts * narrow), BF),
         ],
-        (roll_id, own, *sums, *backs),
+        (roll_id, *backs),
     )
     return prompt_dq, prompt_dk, prompt_dv, roll_dq, roll_dk, roll_dv
 

time: 69.5 us -> 63.1 us (0.908)
  Pallas kernels: 25.9 us -> 16.8 us
  waiting for transfers between devices: 18.7 us -> 22.1 us
  local copies, waits for them, and re-layouts: 3.07 us -> 1.36 us
  starting transfers between devices: 20.7 us -> 21.4 us
    pallas_call x5 -> x4, Pallas kernels: 25.9 us -> 16.8 us  [call(): pl.pallas_call(kernel, name=name, out_shape=outs, in_specs=[SMEM] * scala...]
    ppermute x17, waiting for transfers between devices: 18.7 us -> 22.1 us  [swap(): return lax.ppermute(x, axis, [(i, i ^ k) for i in range(n)])]
    unnamed x34 -> x8, local copies, waits for them, and re-layouts: 3.07 us -> 0.69 us
    ppermute x17, starting transfers between devices: 20.7 us -> 21.4 us  [swap(): return lax.ppermute(x, axis, [(i, i ^ k) for i in range(n)])]
  transfers between devices with their start and end apart: 17 -> 17, of which waited for: 6 -> 6; matrix products, arithmetic and copies ran while one was open for 0% -> 0% of each run, Pallas kernels for 15% -> 12%
where the time goes in v3:
time: 63.1 us; the launch traced here: 62.6 us
  waiting for transfers between devices  22.1 us (35%)
  starting transfers between devices  21.4 us (34%)
  Pallas kernels  16.8 us (27%)
  local copies, waits for them, and re-layouts  1.36 us (2%)
  between operations  0.72 us (1%)
    ppermute x17, waiting for transfers between devices, swap(): return lax.ppermute(x, axis, [(i, i ^ k) for i in range(n)])  22.1 us
    ppermute x17, starting transfers between devices, swap(): return lax.ppermute(x, axis, [(i, i ^ k) for i in range(n)])  21.4 us
    pallas_call x4, Pallas kernels, call(): pl.pallas_call(kernel, name=name, out_shape=outs, in_specs=[SMEM] * scala...  16.8 us
  transfers between devices with their start and end apart: 17, of which 6 were waited for; matrix products, arithmetic and copies ran while one was open for 0% of the time, Pallas kernels for 12%

profile of v3, /device:TPU:0, one launch (start us, length us, event | category | flops | bytes accessed | tf_op | source)
XLA Modules:
  0.0 62.6 jit_solution(13347670413522296416)
XLA Ops:
  0.6 0.0 copy-start
  0.6 0.0 copy-start.1
  0.7 0.0 copy-start.2
  0.7 2.8 %pack.1 = (bf16[128,512]{1,0:T(8,128)(2,1)S(1)}, bf16[32,4736]{1,0:T(8,128)(2,1)S(1)}, bf16[32,4736]{1,0:T(8,128)(2,1)}, bf16[32,4736]{1,0:T(8,128)(2,1)}, bf16[32,4736]{1,0:T(8,128)(2,1)}) custom-call(s32[1]{0:T(128)} %bitcast.2.me_ref, bf16[32,8192]{1,0:T(8,128)(2,1)} %q_ref.2, bf16[32,8192]{1,0:T(8,128)(2,1)} %do_ref.2, bf16[32,8192]{1,0:T(8,128)(2,1)} %o_ref.2, ...), custom_call_target="tpu_custom_call" | custom-call | tf_op jit(solution)/shard_map/pack/pallas_call | solution.py:282
  3.4 0.5 collective-permute-start
  3.9 2.5 %collective-permute-start.1 = (bf16[128,512]{1,0:T(8,128)(2,1)S(1)}, bf16[128,512]{1,0:T(8,128)(2,1)S(1)}, u32[]{:S(2)}, u32[]{:S(2)}) collective-permute-start(bf16[128,512]{1,0:T(8,128)(2,1)S(1)} %get-tuple-element.24.rest_0_.rest_4_), channel_id=1, source_target_pairs={{0,8},{4,12},{8,0},{12,4},{16,24},{20,28},{24,16},{28,20},{1,9},{5... | collective-permute-start | bytes 393224 | tf_op jit(solution)/shard_map/ppermute | solution.py:305
  6.4 1.5 %collective-permute-start.3 = (bf16[128,512]{1,0:T(8,128)(2,1)S(1)}, bf16[128,512]{1,0:T(8,128)(2,1)S(1)}, u32[]{:S(2)}, u32[]{:S(2)}) collective-permute-start(bf16[128,512]{1,0:T(8,128)(2,1)S(1)} %get-tuple-element.24.rest_0_.rest_4_), channel_id=1, source_target_pairs={{0,16},{4,20},{8,24},{12,28},{16,0},{20,4},{24,8},{28,12},{1,17},{... | collective-permute-start | bytes 393224 | tf_op jit(solution)/shard_map/ppermute | solution.py:305
  7.9 1.6 %collective-permute-start.7 = (bf16[32,4736]{1,0:T(8,128)(2,1)}, bf16[32,4736]{1,0:T(8,128)(2,1)S(1)}, u32[]{:S(2)}, u32[]{:S(2)}) collective-permute-start(bf16[32,4736]{1,0:T(8,128)(2,1)} %get-tuple-element.26), channel_id=1, source_target_pairs={{0,1},{1,0},{2,3},{3,2},{4,5},{5,4},{6,7},{7,6},{8,9},{9,8},{10,11... | collective-permute-start | bytes 909320 | tf_op jit(solution)/shard_map/ppermute | solution.py:305
  9.5 2.6 %collective-permute-start.8 = (bf16[32,4736]{1,0:T(8,128)(2,1)}, bf16[32,4736]{1,0:T(8,128)(2,1)S(1)}, u32[]{:S(2)}, u32[]{:S(2)}) collective-permute-start(bf16[32,4736]{1,0:T(8,128)(2,1)} %get-tuple-element.27), channel_id=1, source_target_pairs={{0,2},{1,3},{2,0},{3,1},{4,6},{5,7},{6,4},{7,5},{8,10},{9,11},{10,... | collective-permute-start | bytes 909320 | tf_op jit(solution)/shard_map/ppermute | solution.py:305
  12.1 0.0 collective-permute-done.rest_1_.rest_5_
  12.1 0.2 collective-permute-start.9
  12.3 0.0 collective-permute-done.1.rest_2_.rest_6_
  12.3 0.9 %collective-permute-start.5 = (bf16[128,512]{1,0:T(8,128)(2,1)S(1)}, bf16[128,512]{1,0:T(8,128)(2,1)S(1)}, u32[]{:S(2)}, u32[]{:S(2)}) collective-permute-start(bf16[128,512]{1,0:T(8,128)(2,1)S(1)} %get-tuple-element.24.rest_0_.rest_4_), channel_id=1, source_target_pairs={{0,24},{4,28},{8,16},{12,20},{16,8},{20,12},{24,0},{28,4},{1,25},{... | collective-permute-start | bytes 393224 | tf_op jit(solution)/shard_map/ppermute | solution.py:305
  13.2 0.0 collective-permute-done.3.rest_4_.rest_8_
  13.3 0.0 collective-permute-start.2
  13.3 4.9 %collective-permute-done.5.rest_6_.rest_10_ = bf16[128,512]{1,0:T(8,128)(2,1)S(1)} collective-permute-done((bf16[128,512]{1,0:T(8,128)(2,1)S(1)}, bf16[128,512]{1,0:T(8,128)(2,1)S(1)}, u32[]{:S(2)}, u32[]{:S(2)}) %collective-permute-start.5) | collective-permute-done | bytes 131104 | tf_op jit(solution)/shard_map/ppermute | solution.py:305
  18.2 0.0 collective-permute-start.4
  18.2 0.0 collective-permute-done.2.rest_3_.rest_7_
  18.2 0.5 collective-permute-start.6
  18.7 0.8 %collective-permute-done.4.rest_5_.rest_9_ = bf16[128,512]{1,0:T(8,128)(2,1)S(1)} collective-permute-done((bf16[128,512]{1,0:T(8,128)(2,1)S(1)}, bf16[128,512]{1,0:T(8,128)(2,1)S(1)}, u32[]{:S(2)}, u32[]{:S(2)}) %collective-permute-start.4) | collective-permute-done | bytes 131104 | tf_op jit(solution)/shard_map/ppermute | solution.py:305
  19.5 0.2 collective-permute-done.6.rest_7_.rest_11_
  19.7 0.0 copy-done
  19.7 0.0 copy-done.2
  19.7 0.0 copy-start.3
  19.7 0.7 %copy-done.3 = bf16[128,16]{0,1:T(8,128)(2,1)S(1)} copy-done((bf16[128,16]{0,1:T(8,128)(2,1)S(1)}, bf16[128,16]{0,1:T(8,128)(2,1)}, u32[]{:S(2)}) %copy-start.3) | copy-done | bytes 4120
  20.4 6.9 %prompt_grads.1 = (bf16[128,2048]{1,0:T(8,128)(2,1)}, f32[8,128,512]{2,1,0:T(8,128)S(1)}, f32[2,128,256]{2,1,0:T(8,128)S(1)}) custom-call(s32[1]{0:T(128)} %bitcast.me_ref, bf16[128,2048]{1,0:T(8,128)(2,1)S(1)} %copy-done, bf16[128,2048]{1,0:T(8,128)(2,1)S(1)} %copy-done.1, bf16[128,2048]{1,0:T(8,128)(2,1)S(1)} %copy-done.2, bf16[16,128]{1,0:T(8,128)(2,1)S(1)} %bitcast.17, ...), custom_call_target="tpu_custom_call" | custom-call | tf_op jit(solution)/shard_map/prompt_grads/pallas_call | solution.py:282
  27.3 0.0 collective-permute-done.7.rest_1_
  27.3 6.4 %collective-permute-done.8.rest_2_ = bf16[32,4736]{1,0:T(8,128)(2,1)S(1)} collective-permute-done((bf16[32,4736]{1,0:T(8,128)(2,1)}, bf16[32,4736]{1,0:T(8,128)(2,1)S(1)}, u32[]{:S(2)}, u32[]{:S(2)}) %collective-permute-start.8) | collective-permute-done | bytes 303136 | tf_op jit(solution)/shard_map/ppermute | solution.py:305
  33.7 0.0 collective-permute-done.9.rest_3_
  33.7 6.3 %roll_grads.1 = (f32[4,128,512]{2,1,0:T(8,128)S(1)}, bf16[4,128,512]{2,1,0:T(8,128)(2,1)S(1)}, bf16[32,2560]{1,0:T(8,128)(2,1)S(1)}, bf16[32,2560]{1,0:T(8,128)(...) custom-call(s32[1]{0:T(128)} %bitcast.2.me_ref, ...), custom_call_target="tpu_custom_call" | custom-call | tf_op jit(solution)/shard_map/roll_grads/pallas_call | solution.py:282
  40.0 0.1 collective-permute-start.10
  40.0 5.9 %collective-permute-start.14 = (bf16[32,2560]{1,0:T(8,128)(2,1)S(1)}, bf16[32,2560]{1,0:T(8,128)(2,1)S(1)}, u32[]{:S(2)}, u32[]{:S(2)}) collective-permute-start(bf16[32,2560]{1,0:T(8,128)(2,1)S(1)} %get-tuple-element.34), channel_id=1, source_target_pairs={{0,1},{1,0},{2,3},{3,2},{4,5},{5,4},{6,7},{7,6},{8,9},{9,8},{10,11... | collective-permute-start | bytes 491528 | tf_op jit(solution)/shard_map/ppermute | solution.py:305
  46.0 1.1 %collective-permute-start.15 = (bf16[32,2560]{1,0:T(8,128)(2,1)S(1)}, bf16[32,2560]{1,0:T(8,128)(2,1)S(1)}, u32[]{:S(2)}, u32[]{:S(2)}) collective-permute-start(bf16[32,2560]{1,0:T(8,128)(2,1)S(1)} %get-tuple-element.35), channel_id=1, source_target_pairs={{0,2},{1,3},{2,0},{3,1},{4,6},{5,7},{6,4},{7,5},{8,10},{9,11},{10,... | collective-permute-start | bytes 491528 | tf_op jit(solution)/shard_map/ppermute | solution.py:305
  47.0 1.4 %collective-permute-start.16 = (bf16[32,2560]{1,0:T(8,128)(2,1)S(1)}, bf16[32,2560]{1,0:T(8,128)(2,1)S(1)}, u32[]{:S(2)}, u32[]{:S(2)}) collective-permute-start(bf16[32,2560]{1,0:T(8,128)(2,1)S(1)} %get-tuple-element.36), channel_id=1, source_target_pairs={{0,3},{1,2},{2,1},{3,0},{4,7},{5,6},{6,5},{7,4},{8,11},{9,10},{10,... | collective-permute-start | bytes 491528 | tf_op jit(solution)/shard_map/ppermute | solution.py:305
  48.4 0.0 collective-permute-done.10
  48.4 0.1 fusion.3
  48.6 0.5 collective-permute-start.13
  49.1 1.5 %collective-permute-start.12 = (bf16[128,512]{1,0:T(8,128)(2,1)S(1)}, bf16[128,512]{1,0:T(8,128)(2,1)S(1)}, u32[]{:S(2)}, u32[]{:S(2)}) collective-permute-start(bf16[128,512]{1,0:T(8,128)(2,1)S(1)} %get-tuple-element.42), channel_id=1, source_target_pairs={{0,16},{4,20},{8,24},{12,28},{16,0},{20,4},{24,8},{28,12},{1,17},{... | collective-permute-start | bytes 393224 | tf_op jit(solution)/shard_map/ppermute | solution.py:305
  50.6 3.2 %collective-permute-done.14.rest_1_ = bf16[32,2560]{1,0:T(8,128)(2,1)S(1)} collective-permute-done((bf16[32,2560]{1,0:T(8,128)(2,1)S(1)}, bf16[32,2560]{1,0:T(8,128)(2,1)S(1)}, u32[]{:S(2)}, u32[]{:S(2)}) %collective-permute-start.14) | collective-permute-done | bytes 163872 | tf_op jit(solution)/shard_map/ppermute | solution.py:305
  53.8 0.5 collective-permute-start.11
  54.4 6.6 %collective-permute-done.15.rest_2_ = bf16[32,2560]{1,0:T(8,128)(2,1)S(1)} collective-permute-done((bf16[32,2560]{1,0:T(8,128)(2,1)S(1)}, bf16[32,2560]{1,0:T(8,128)(2,1)S(1)}, u32[]{:S(2)}, u32[]{:S(2)}) %collective-permute-start.15) | collective-permute-done | bytes 163872 | tf_op jit(solution)/shard_map/ppermute | solution.py:305
  61.0 0.0 collective-permute-done.16.rest_3_
  61.0 0.9 %unpack.1 = (bf16[32,8192]{1,0:T(8,128)(2,1)}, bf16[32,1024]{1,0:T(8,128)(2,1)}, bf16[32,1024]{1,0:T(8,128)(2,1)}) custom-call(s32[1]{0:T(128)} %bitcast.2.me_ref, bf16[32,2560]{1,0:T(8,128)(2,1)S(1)} %get-tuple-element.33.rest_0_, bf16[32,2560]{1,0:T(8,128)(2,1)S(1)} %collective-permute-done.14.rest_1_, ...), custom_call_target="tpu_custom_call" | custom-call | tf_op jit(solution)/shard_map/unpack/pallas_call | solution.py:282
  61.8 0.0 collective-permute-done.13
  61.9 0.0 collective-permute-done.12
  61.9 0.0 collective-permute-done.11
  61.9 0.1 fusion.2
  62.0 0.7 %fusion.6 = (bf16[128,256]{1,0:T(8,128)(2,1)}, bf16[128,256]{1,0:T(8,128)(2,1)}) fusion(bf16[128,512]{1,0:T(8,128)(2,1)S(1)} %fusion.2), kind=kLoop, calls=%fused_computation.10 | loop fusion | bytes 262144 | tf_op jit(solution)/shard_map/slice | solution.py:395
  (1 shorter events, 0.0 us)
Async XLA Ops:
  0.6 19.1 %copy-start = (bf16[128,2048]{1,0:T(8,128)(2,1)S(1)}, bf16[128,2048]{1,0:T(8,128)(2,1)}, u32[]{:S(2)}) copy-start(bf16[128,2048]{1,0:T(8,128)(2,1)} %q_ref.3) | copy-start | bytes 1572868
  0.6 19.1 %copy-start.1 = (bf16[128,2048]{1,0:T(8,128)(2,1)S(1)}, bf16[128,2048]{1,0:T(8,128)(2,1)}, u32[]{:S(2)}) copy-start(bf16[128,2048]{1,0:T(8,128)(2,1)} %do_ref.3) | copy-start | bytes 1572868
  0.7 19.1 %copy-start.2 = (bf16[128,2048]{1,0:T(8,128)(2,1)S(1)}, bf16[128,2048]{1,0:T(8,128)(2,1)}, u32[]{:S(2)}) copy-start(bf16[128,2048]{1,0:T(8,128)(2,1)} %o_ref.3) | copy-start | bytes 1572868
  3.4 8.6 %collective-permute-start = (bf16[128,512]{1,0:T(8,128)(2,1)S(1)}, bf16[128,512]{1,0:T(8,128)(2,1)S(1)}, u32[]{:S(2)}, u32[]{:S(2)}) collective-permute-start(bf16[128,512]{1,0:T(8,128)(2,1)S(1)} %get-tuple-element.24.rest_0_.rest_4_), channel_id=1, source_target_pairs={{0,4},{4,0},{8,12},{12,8},{16,20},{20,16},{24,28},{28,24},{1,5},{5... | collective-permute-start | bytes 393224 | tf_op jit(solution)/shard_map/ppermute | solution.py:305
  3.9 8.4 %collective-permute-start.1 = (bf16[128,512]{1,0:T(8,128)(2,1)S(1)}, bf16[128,512]{1,0:T(8,128)(2,1)S(1)}, u32[]{:S(2)}, u32[]{:S(2)}) collective-permute-start(bf16[128,512]{1,0:T(8,128)(2,1)S(1)} %get-tuple-element.24.rest_0_.rest_4_), channel_id=1, source_target_pairs={{0,8},{4,12},{8,0},{12,4},{16,24},{20,28},{24,16},{28,20},{1,9},{5... | collective-permute-start | bytes 393224 | tf_op jit(solution)/shard_map/ppermute | solution.py:305
  6.4 6.9 %collective-permute-start.3 = (bf16[128,512]{1,0:T(8,128)(2,1)S(1)}, bf16[128,512]{1,0:T(8,128)(2,1)S(1)}, u32[]{:S(2)}, u32[]{:S(2)}) collective-permute-start(bf16[128,512]{1,0:T(8,128)(2,1)S(1)} %get-tuple-element.24.rest_0_.rest_4_), channel_id=1, source_target_pairs={{0,16},{4,20},{8,24},{12,28},{16,0},{20,4},{24,8},{28,12},{1,17},{... | collective-permute-start | bytes 393224 | tf_op jit(solution)/shard_map/ppermute | solution.py:305
  7.9 19.4 %collective-permute-start.7 = (bf16[32,4736]{1,0:T(8,128)(2,1)}, bf16[32,4736]{1,0:T(8,128)(2,1)S(1)}, u32[]{:S(2)}, u32[]{:S(2)}) collective-permute-start(bf16[32,4736]{1,0:T(8,128)(2,1)} %get-tuple-element.26), channel_id=1, source_target_pairs={{0,1},{1,0},{2,3},{3,2},{4,5},{5,4},{6,7},{7,6},{8,9},{9,8},{10,11... | collective-permute-start | bytes 909320 | tf_op jit(solution)/shard_map/ppermute | solution.py:305
  9.5 24.2 %collective-permute-start.8 = (bf16[32,4736]{1,0:T(8,128)(2,1)}, bf16[32,4736]{1,0:T(8,128)(2,1)S(1)}, u32[]{:S(2)}, u32[]{:S(2)}) collective-permute-start(bf16[32,4736]{1,0:T(8,128)(2,1)} %get-tuple-element.27), channel_id=1, source_target_pairs={{0,2},{1,3},{2,0},{3,1},{4,6},{5,7},{6,4},{7,5},{8,10},{9,11},{10,... | collective-permute-start | bytes 909320 | tf_op jit(solution)/shard_map/ppermute | solution.py:305
  12.1 21.6 %collective-permute-start.9 = (bf16[32,4736]{1,0:T(8,128)(2,1)}, bf16[32,4736]{1,0:T(8,128)(2,1)}, u32[]{:S(2)}, u32[]{:S(2)}) collective-permute-start(bf16[32,4736]{1,0:T(8,128)(2,1)} %get-tuple-element.28), channel_id=1, source_target_pairs={{0,3},{1,2},{2,1},{3,0},{4,7},{5,6},{6,5},{7,4},{8,11},{9,10},{10,... | collective-permute-start | bytes 909320 | tf_op jit(solution)/shard_map/ppermute | solution.py:305
  12.3 5.9 %collective-permute-start.5 = (bf16[128,512]{1,0:T(8,128)(2,1)S(1)}, bf16[128,512]{1,0:T(8,128)(2,1)S(1)}, u32[]{:S(2)}, u32[]{:S(2)}) collective-permute-start(bf16[128,512]{1,0:T(8,128)(2,1)S(1)} %get-tuple-element.24.rest_0_.rest_4_), channel_id=1, source_target_pairs={{0,24},{4,28},{8,16},{12,20},{16,8},{20,12},{24,0},{28,4},{1,25},{... | collective-permute-start | bytes 393224 | tf_op jit(solution)/shard_map/ppermute | solution.py:305
  13.3 4.9 %collective-permute-start.2 = (bf16[128,512]{1,0:T(8,128)(2,1)S(1)}, bf16[128,512]{1,0:T(8,128)(2,1)S(1)}, u32[]{:S(2)}, u32[]{:S(2)}) collective-permute-start(bf16[128,512]{1,0:T(8,128)(2,1)S(1)} %collective-permute-done.1.rest_2_.rest_6_), channel_id=1, source_target_pairs={{0,4},{4,0},{8,12},{12,8},{16,20},{20,16},{24,28},{28,24},{1,5},{5... | collective-permute-start | bytes 393224 | tf_op jit(solution)/shard_map/ppermute | solution.py:305
  18.2 1.3 %collective-permute-start.4 = (bf16[128,512]{1,0:T(8,128)(2,1)S(1)}, bf16[128,512]{1,0:T(8,128)(2,1)S(1)}, u32[]{:S(2)}, u32[]{:S(2)}) collective-permute-start(bf16[128,512]{1,0:T(8,128)(2,1)S(1)} %collective-permute-done.3.rest_4_.rest_8_), channel_id=1, source_target_pairs={{0,4},{4,0},{8,12},{12,8},{16,20},{20,16},{24,28},{28,24},{1,5},{5... | collective-permute-start | bytes 393224 | tf_op jit(solution)/shard_map/ppermute | solution.py:305
  18.2 1.5 %collective-permute-start.6 = (bf16[128,512]{1,0:T(8,128)(2,1)S(1)}, bf16[128,512]{1,0:T(8,128)(2,1)S(1)}, u32[]{:S(2)}, u32[]{:S(2)}) collective-permute-start(bf16[128,512]{1,0:T(8,128)(2,1)S(1)} %collective-permute-done.5.rest_6_.rest_10_), channel_id=1, source_target_pairs={{0,4},{4,0},{8,12},{12,8},{16,20},{20,16},{24,28},{28,24},{1,5},{5... | collective-permute-start | bytes 393224 | tf_op jit(solution)/shard_map/ppermute | solution.py:305
  19.7 0.7 %copy-start.3 = (bf16[128,16]{0,1:T(8,128)(2,1)S(1)}, bf16[128,16]{0,1:T(8,128)(2,1)}, u32[]{:S(2)}) copy-start(bf16[128,16]{0,1:T(8,128)(2,1)} %param.17) | copy-start | bytes 12292
  40.0 8.5 %collective-permute-start.10 = (bf16[4,128,512]{2,1,0:T(8,128)(2,1)S(1)}, bf16[4,128,512]{2,1,0:T(8,128)(2,1)S(1)}, u32[]{:S(2)}, u32[]{:S(2)}) collective-permute-start(bf16[4,128,512]{2,1,0:T(8,128)(2,1)S(1)} %get-tuple-element.32), channel_id=1, source_target_pairs={{0,4},{4,0},{8,12},{12,8},{16,20},{20,16},{24,28},{28,24},{1,5},{5... | collective-permute-start | bytes 1572872 | tf_op jit(solution)/shard_map/ppermute | solution.py:305
  40.0 13.8 %collective-permute-start.14 = (bf16[32,2560]{1,0:T(8,128)(2,1)S(1)}, bf16[32,2560]{1,0:T(8,128)(2,1)S(1)}, u32[]{:S(2)}, u32[]{:S(2)}) collective-permute-start(bf16[32,2560]{1,0:T(8,128)(2,1)S(1)} %get-tuple-element.34), channel_id=1, source_target_pairs={{0,1},{1,0},{2,3},{3,2},{4,5},{5,4},{6,7},{7,6},{8,9},{9,8},{10,11... | collective-permute-start | bytes 491528 | tf_op jit(solution)/shard_map/ppermute | solution.py:305
  46.0 15.0 %collective-permute-start.15 = (bf16[32,2560]{1,0:T(8,128)(2,1)S(1)}, bf16[32,2560]{1,0:T(8,128)(2,1)S(1)}, u32[]{:S(2)}, u32[]{:S(2)}) collective-permute-start(bf16[32,2560]{1,0:T(8,128)(2,1)S(1)} %get-tuple-element.35), channel_id=1, source_target_pairs={{0,2},{1,3},{2,0},{3,1},{4,6},{5,7},{6,4},{7,5},{8,10},{9,11},{10,... | collective-permute-start | bytes 491528 | tf_op jit(solution)/shard_map/ppermute | solution.py:305
  47.0 13.9 %collective-permute-start.16 = (bf16[32,2560]{1,0:T(8,128)(2,1)S(1)}, bf16[32,2560]{1,0:T(8,128)(2,1)S(1)}, u32[]{:S(2)}, u32[]{:S(2)}) collective-permute-start(bf16[32,2560]{1,0:T(8,128)(2,1)S(1)} %get-tuple-element.36), channel_id=1, source_target_pairs={{0,3},{1,2},{2,1},{3,0},{4,7},{5,6},{6,5},{7,4},{8,11},{9,10},{10,... | collective-permute-start | bytes 491528 | tf_op jit(solution)/shard_map/ppermute | solution.py:305
  48.6 13.3 %collective-permute-start.13 = (bf16[128,512]{1,0:T(8,128)(2,1)S(1)}, bf16[128,512]{1,0:T(8,128)(2,1)S(1)}, u32[]{:S(2)}, u32[]{:S(2)}) collective-permute-start(bf16[128,512]{1,0:T(8,128)(2,1)S(1)} %get-tuple-element.41), channel_id=1, source_target_pairs={{0,24},{4,28},{8,16},{12,20},{16,8},{20,12},{24,0},{28,4},{1,25},{... | collective-permute-start | bytes 393224 | tf_op jit(solution)/shard_map/ppermute | solution.py:305
  49.1 12.7 %collective-permute-start.12 = (bf16[128,512]{1,0:T(8,128)(2,1)S(1)}, bf16[128,512]{1,0:T(8,128)(2,1)S(1)}, u32[]{:S(2)}, u32[]{:S(2)}) collective-permute-start(bf16[128,512]{1,0:T(8,128)(2,1)S(1)} %get-tuple-element.42), channel_id=1, source_target_pairs={{0,16},{4,20},{8,24},{12,28},{16,0},{20,4},{24,8},{28,12},{1,17},{... | collective-permute-start | bytes 393224 | tf_op jit(solution)/shard_map/ppermute | solution.py:305
  53.8 8.0 %collective-permute-start.11 = (bf16[128,512]{1,0:T(8,128)(2,1)S(1)}, bf16[128,512]{1,0:T(8,128)(2,1)S(1)}, u32[]{:S(2)}, u32[]{:S(2)}) collective-permute-start(bf16[128,512]{1,0:T(8,128)(2,1)S(1)} %get-tuple-element.40), channel_id=1, source_target_pairs={{0,8},{4,12},{8,0},{12,4},{16,24},{20,28},{24,16},{28,20},{1,9},{5... | collective-permute-start | bytes 393224 | tf_op jit(solution)/shard_map/ppermute | solution.py:305

commit v4 on v3

--- a/solution.py
+++ b/solution.py
@@ -54,6 +54,15 @@
     return jnp.concatenate(
         [ref[low:high, first + h * HEAD : first + (h + 1) * HEAD] for h in range(members)], axis=0
     )
+
+
+def send_order(parts):
+    return sorted(range(parts), key=lambda k: (k % 2, k))
+
+
+def by_partner(refs):
+    order = send_order(len(refs))
+    return [refs[order.index(k)] for k in range(len(refs))]
 
 
 def stat_rows(packs, group, members, heads, width):
@@ -195,7 +204,7 @@
 
 
 def roll_kernel(parts, slots, members, me_ref, *rest):
-    packs, rest = rest[:parts], rest[parts:]
+    packs, rest = by_partner(rest[:parts]), rest[parts:]
     kv_refs, rest = rest[:slots], rest[slots:]
     part_ref, roll_dq_ref, even_ref, odd_ref = rest[:4]
     backs = rest[4:]
@@ -262,7 +271,7 @@
 
 
 def unpack_kernel(me_ref, *rest):
-    backs, (rq_ref, rk_ref, rv_ref) = rest[:-3], rest[-3:]
+    backs, (rq_ref, rk_ref, rv_ref) = by_partner(rest[:-3]), rest[-3:]
     me = me_ref[0]
     width = rq_ref.shape[1] // len(backs)
     narrow = rk_ref.shape[1] // len(backs)
@@ -360,11 +369,7 @@
         ),
     )
     got = [swap(x, "roll", k) if k else x for k, x in enumerate(packs)]
-    blocks = [None] * slots
-    for s in range(0, slots, 2):
-        blocks[s] = swap(kv, "ctx", s) if s else kv
-        blocks[s + 1] = swap(blocks[s], "ctx", 1)
-    blocks = [in_vmem(x) for x in blocks]
+    blocks = [in_vmem(swap(kv, "ctx", s) if s else kv) for s in range(slots)]
 
     prompt_dq, part, roll_own_dq = call(
         functools.partial(prompt_kernel, members),
@@ -374,7 +379,7 @@
             vmem_shape((slots, prompt_rows, 2 * narrow), F32),
             vmem_shape((narrow // HEAD, HEAD, members * rows), F32),
         ],
-        (ctx_id, prompt_query, prompt_dout, prompt_out, prompt_lse.T, in_vmem(packs[0]), *blocks),
+        (ctx_id, *map(in_hbm, (prompt_query, prompt_dout, prompt_out, prompt_lse.T)), in_vmem(packs[0]), *blocks),
     )
     even, odd, *backs = call(
         functools.partial(roll_kernel, parts, slots, members),
@@ -384,7 +389,7 @@
             vmem_shape((slots // 2, prompt_rows, 2 * narrow), BF),
         ]
         + [vmem_shape((rows, width + 2 * narrow), BF)] * parts,
-        (roll_id, *[in_vmem(x) for x in got], *blocks, in_vmem(part), in_vmem(roll_own_dq)),
+        (roll_id, *[in_vmem(got[k]) for k in send_order(parts)], *blocks, in_vmem(part), in_vmem(roll_own_dq)),
     )
     odd_got = swap(odd, "ctx", 1)
     backs = [in_vmem(swap(x, "roll", k) if k else x) for k, x in enumerate(backs)]
@@ -401,7 +406,7 @@
             shape((rows, parts * narrow), BF),
             shape((rows, parts * narrow), BF),
         ],
-        (roll_id, *backs),
+        (roll_id, *[backs[k] for k in send_order(parts)]),
     )
     return prompt_dq, prompt_dk, prompt_dv, roll_dq, roll_dk, roll_dv
 

time: 63.1 us -> 58.7 us (0.930)
  waiting for transfers between devices: 22.1 us -> 12.8 us
  starting transfers between devices: 21.4 us -> 27.9 us
  local copies, waits for them, and re-layouts: 1.36 us -> 0.66 us
    ppermute x17, waiting for transfers between devices: 22.1 us -> 12.8 us  [swap(): return lax.ppermute(x, axis, [(i, i ^ k) for i in range(n)])]
    ppermute x17, starting transfers between devices: 21.4 us -> 27.9 us  [swap(): return lax.ppermute(x, axis, [(i, i ^ k) for i in range(n)])]
    unnamed x8 -> x0, local copies, waits for them, and re-layouts: 0.69 us -> none
  transfers between devices with their start and end apart: 17 -> 17, of which waited for: 6 -> 7; matrix products, arithmetic and copies ran while one was open for 0% -> 0% of each run, Pallas kernels for 12% -> 16%
where the time goes in v4:
time: 58.7 us; the launch traced here: 58.5 us
  starting transfers between devices  27.9 us (48%)
  Pallas kernels  16.2 us (28%)
  waiting for transfers between devices  12.8 us (22%)
  between operations  0.68 us (1%)
  local copies, waits for them, and re-layouts  0.66 us (1%)
    ppermute x17, starting transfers between devices, swap(): return lax.ppermute(x, axis, [(i, i ^ k) for i in range(n)])  27.9 us
    pallas_call x4, Pallas kernels, call(): pl.pallas_call(kernel, name=name, out_shape=outs, in_specs=[SMEM] * scala...  16.2 us
    ppermute x17, waiting for transfers between devices, swap(): return lax.ppermute(x, axis, [(i, i ^ k) for i in range(n)])  12.8 us
  transfers between devices with their start and end apart: 17, of which 7 were waited for; matrix products, arithmetic and copies ran while one was open for 0% of the time, Pallas kernels for 16%

profile of v4, /device:TPU:0, one launch (start us, length us, event | category | flops | bytes accessed | tf_op | source)
XLA Modules:
  0.0 58.5 jit_solution(10883427439484635198)
XLA Ops:
  0.6 1.8 %pack.1 = (bf16[128,512]{1,0:T(8,128)(2,1)S(1)}, bf16[32,4736]{1,0:T(8,128)(2,1)S(1)}, bf16[32,4736]{1,0:T(8,128)(2,1)S(1)}, bf16[32,4736]{1,0:T(8,128)(2,1)S(1)}, bf16[32,4736]{1,0:T(8,128)(2,1)S(1)}) custom-call(s32[1]{0:T(128)} %bitcast.2.me_ref, bf16[32,8192]{1,0:T(8,128)(2,1)} %q_ref.2, bf16[32,8192]{1,0:T(8,128)(2,1)} %do_ref.2, ...), custom_call_target="tpu_custom_call" | custom-call | tf_op jit(solution)/shard_map/pack/pallas_call | solution.py:291
  2.5 0.5 collective-permute-start
  3.0 2.6 %collective-permute-start.1 = (bf16[128,512]{1,0:T(8,128)(2,1)S(1)}, bf16[128,512]{1,0:T(8,128)(2,1)S(1)}, u32[]{:S(2)}, u32[]{:S(2)}) collective-permute-start(bf16[128,512]{1,0:T(8,128)(2,1)S(1)} %get-tuple-element.24.rest_0_.rest_4_), channel_id=1, source_target_pairs={{0,8},{4,12},{8,0},{12,4},{16,24},{20,28},{24,16},{28,20},{1,9},{5... | collective-permute-start | bytes 393224 | tf_op jit(solution)/shard_map/ppermute | solution.py:314
  5.5 0.1 collective-permute-start.2
  5.6 2.8 %collective-permute-start.7 = (bf16[32,4736]{1,0:T(8,128)(2,1)S(1)}, bf16[32,4736]{1,0:T(8,128)(2,1)S(1)}, u32[]{:S(2)}, u32[]{:S(2)}) collective-permute-start(bf16[32,4736]{1,0:T(8,128)(2,1)S(1)} %get-tuple-element.26), channel_id=1, source_target_pairs={{0,2},{1,3},{2,0},{3,1},{4,6},{5,7},{6,4},{7,5},{8,10},{9,11},{10,... | collective-permute-start | bytes 909320 | tf_op jit(solution)/shard_map/ppermute | solution.py:314
  8.4 1.6 %collective-permute-start.8 = (bf16[32,4736]{1,0:T(8,128)(2,1)S(1)}, bf16[32,4736]{1,0:T(8,128)(2,1)S(1)}, u32[]{:S(2)}, u32[]{:S(2)}) collective-permute-start(bf16[32,4736]{1,0:T(8,128)(2,1)S(1)} %get-tuple-element.27), channel_id=1, source_target_pairs={{0,1},{1,0},{2,3},{3,2},{4,5},{5,4},{6,7},{7,6},{8,9},{9,8},{10,11... | collective-permute-start | bytes 909320 | tf_op jit(solution)/shard_map/ppermute | solution.py:314
  10.0 0.0 collective-permute-done.rest_1_.rest_5_
  10.0 0.0 collective-permute-start.9
  10.0 0.0 collective-permute-done.1.rest_2_.rest_6_
  10.0 1.8 %collective-permute-start.3 = (bf16[128,512]{1,0:T(8,128)(2,1)S(1)}, bf16[128,512]{1,0:T(8,128)(2,1)S(1)}, u32[]{:S(2)}, u32[]{:S(2)}) collective-permute-start(bf16[128,512]{1,0:T(8,128)(2,1)S(1)} %get-tuple-element.24.rest_0_.rest_4_), channel_id=1, source_target_pairs={{0,16},{4,20},{8,24},{12,28},{16,0},{20,4},{24,8},{28,12},{1,17},{... | collective-permute-start | bytes 393224 | tf_op jit(solution)/shard_map/ppermute | solution.py:314
  11.9 0.3 collective-permute-done.2.rest_3_.rest_7_
  12.2 1.8 %collective-permute-start.4 = (bf16[128,512]{1,0:T(8,128)(2,1)S(1)}, bf16[128,512]{1,0:T(8,128)(2,1)S(1)}, u32[]{:S(2)}, u32[]{:S(2)}) collective-permute-start(bf16[128,512]{1,0:T(8,128)(2,1)S(1)} %get-tuple-element.24.rest_0_.rest_4_), channel_id=1, source_target_pairs={{0,20},{4,16},{8,28},{12,24},{16,4},{20,0},{24,12},{28,8},{1,21},{... | collective-permute-start | bytes 393224 | tf_op jit(solution)/shard_map/ppermute | solution.py:314
  14.0 1.3 %collective-permute-done.3.rest_4_.rest_8_ = bf16[128,512]{1,0:T(8,128)(2,1)S(1)} collective-permute-done((bf16[128,512]{1,0:T(8,128)(2,1)S(1)}, bf16[128,512]{1,0:T(8,128)(2,1)S(1)}, u32[]{:S(2)}, u32[]{:S(2)}) %collective-permute-start.3) | collective-permute-done | bytes 131104 | tf_op jit(solution)/shard_map/ppermute | solution.py:314
  15.3 2.5 %collective-permute-start.5 = (bf16[128,512]{1,0:T(8,128)(2,1)S(1)}, bf16[128,512]{1,0:T(8,128)(2,1)S(1)}, u32[]{:S(2)}, u32[]{:S(2)}) collective-permute-start(bf16[128,512]{1,0:T(8,128)(2,1)S(1)} %get-tuple-element.24.rest_0_.rest_4_), channel_id=1, source_target_pairs={{0,24},{4,28},{8,16},{12,20},{16,8},{20,12},{24,0},{28,4},{1,25},{... | collective-permute-start | bytes 393224 | tf_op jit(solution)/shard_map/ppermute | solution.py:314
  17.8 0.8 %collective-permute-done.4.rest_5_.rest_9_ = bf16[128,512]{1,0:T(8,128)(2,1)S(1)} collective-permute-done((bf16[128,512]{1,0:T(8,128)(2,1)S(1)}, bf16[128,512]{1,0:T(8,128)(2,1)S(1)}, u32[]{:S(2)}, u32[]{:S(2)}) %collective-permute-start.4) | collective-permute-done | bytes 131104 | tf_op jit(solution)/shard_map/ppermute | solution.py:314
  18.6 3.1 %collective-permute-start.6 = (bf16[128,512]{1,0:T(8,128)(2,1)S(1)}, bf16[128,512]{1,0:T(8,128)(2,1)S(1)}, u32[]{:S(2)}, u32[]{:S(2)}) collective-permute-start(bf16[128,512]{1,0:T(8,128)(2,1)S(1)} %get-tuple-element.24.rest_0_.rest_4_), channel_id=1, source_target_pairs={{0,28},{4,24},{8,20},{12,16},{16,12},{20,8},{24,4},{28,0},{1,29},{... | collective-permute-start | bytes 393224 | tf_op jit(solution)/shard_map/ppermute | solution.py:314
  21.7 0.0 collective-permute-done.5.rest_6_.rest_10_
  21.7 3.4 %collective-permute-done.6.rest_7_.rest_11_ = bf16[128,512]{1,0:T(8,128)(2,1)S(1)} collective-permute-done((bf16[128,512]{1,0:T(8,128)(2,1)S(1)}, bf16[128,512]{1,0:T(8,128)(2,1)S(1)}, u32[]{:S(2)}, u32[]{:S(2)}) %collective-permute-start.6) | collective-permute-done | bytes 131104 | tf_op jit(solution)/shard_map/ppermute | solution.py:314
  25.1 8.2 %prompt_grads.1 = (bf16[128,2048]{1,0:T(8,128)(2,1)}, f32[8,128,512]{2,1,0:T(8,128)S(1)}, f32[2,128,256]{2,1,0:T(8,128)S(1)}) custom-call(s32[1]{0:T(128)} %bitcast.me_ref, bf16[128,2048]{1,0:T(8,128)(2,1)} %q_ref.3, bf16[128,2048]{1,0:T(8,128)(2,1)} %do_ref.3, bf16[128,2048]{1,0:T(8,128)(2,1)} %o_ref.3, bf16[16,128]{1,0:T(8,128)(2,1)} %bitcast.17, ...), custom_call_target="tpu_custom_call" | custom-call | tf_op jit(solution)/shard_map/prompt_grads/pallas_call | solution.py:291
  33.3 0.0 collective-permute-done.7.rest_1_
  33.3 0.0 collective-permute-done.8.rest_2_
  33.3 0.0 collective-permute-done.9.rest_3_
  33.3 5.3 %roll_grads.1 = (f32[4,128,512]{2,1,0:T(8,128)S(1)}, bf16[4,128,512]{2,1,0:T(8,128)(2,1)S(1)}, bf16[32,2560]{1,0:T(8,128)(2,1)S(1)}, bf16[32,2560]{1,0:T(8,128)(...) custom-call(s32[1]{0:T(128)} %bitcast.2.me_ref, ...), custom_call_target="tpu_custom_call" | custom-call | tf_op jit(solution)/shard_map/roll_grads/pallas_call | solution.py:291
  38.6 0.9 %collective-permute-start.10 = (bf16[4,128,512]{2,1,0:T(8,128)(2,1)S(1)}, bf16[4,128,512]{2,1,0:T(8,128)(2,1)S(1)}, u32[]{:S(2)}, u32[]{:S(2)}) collective-permute-start(bf16[4,128,512]{2,1,0:T(8,128)(2,1)S(1)} %get-tuple-element.32), channel_id=1, source_target_pairs={{0,4},{4,0},{8,12},{12,8},{16,20},{20,16},{24,28},{28,24},{1,5},{5... | collective-permute-start | bytes 1572872 | tf_op jit(solution)/shard_map/ppermute | solution.py:314
  39.5 4.2 %collective-permute-start.14 = (bf16[32,2560]{1,0:T(8,128)(2,1)S(1)}, bf16[32,2560]{1,0:T(8,128)(2,1)S(1)}, u32[]{:S(2)}, u32[]{:S(2)}) collective-permute-start(bf16[32,2560]{1,0:T(8,128)(2,1)S(1)} %get-tuple-element.34), channel_id=1, source_target_pairs={{0,2},{1,3},{2,0},{3,1},{4,6},{5,7},{6,4},{7,5},{8,10},{9,11},{10,... | collective-permute-start | bytes 491528 | tf_op jit(solution)/shard_map/ppermute | solution.py:314
  43.7 0.0 collective-permute-start.15
  43.7 1.5 %collective-permute-start.16 = (bf16[32,2560]{1,0:T(8,128)(2,1)S(1)}, bf16[32,2560]{1,0:T(8,128)(2,1)S(1)}, u32[]{:S(2)}, u32[]{:S(2)}) collective-permute-start(bf16[32,2560]{1,0:T(8,128)(2,1)S(1)} %get-tuple-element.36), channel_id=1, source_target_pairs={{0,3},{1,2},{2,1},{3,0},{4,7},{5,6},{6,5},{7,4},{8,11},{9,10},{10,... | collective-permute-start | bytes 491528 | tf_op jit(solution)/shard_map/ppermute | solution.py:314
  45.3 0.0 collective-permute-done.10
  45.3 0.1 fusion.3
  45.4 2.5 %collective-permute-start.13 = (bf16[128,512]{1,0:T(8,128)(2,1)S(1)}, bf16[128,512]{1,0:T(8,128)(2,1)S(1)}, u32[]{:S(2)}, u32[]{:S(2)}) collective-permute-start(bf16[128,512]{1,0:T(8,128)(2,1)S(1)} %get-tuple-element.41), channel_id=1, source_target_pairs={{0,24},{4,28},{8,16},{12,20},{16,8},{20,12},{24,0},{28,4},{1,25},{... | collective-permute-start | bytes 393224 | tf_op jit(solution)/shard_map/ppermute | solution.py:314
  47.9 0.5 collective-permute-start.12
  48.4 4.4 %collective-permute-done.14.rest_1_ = bf16[32,2560]{1,0:T(8,128)(2,1)S(1)} collective-permute-done((bf16[32,2560]{1,0:T(8,128)(2,1)S(1)}, bf16[32,2560]{1,0:T(8,128)(2,1)S(1)}, u32[]{:S(2)}, u32[]{:S(2)}) %collective-permute-start.14) | collective-permute-done | bytes 163872 | tf_op jit(solution)/shard_map/ppermute | solution.py:314
  52.8 1.5 %collective-permute-start.11 = (bf16[128,512]{1,0:T(8,128)(2,1)S(1)}, bf16[128,512]{1,0:T(8,128)(2,1)S(1)}, u32[]{:S(2)}, u32[]{:S(2)}) collective-permute-start(bf16[128,512]{1,0:T(8,128)(2,1)S(1)} %get-tuple-element.40), channel_id=1, source_target_pairs={{0,8},{4,12},{8,0},{12,4},{16,24},{20,28},{24,16},{28,20},{1,9},{5... | collective-permute-start | bytes 393224 | tf_op jit(solution)/shard_map/ppermute | solution.py:314
  54.3 2.4 %collective-permute-done.15.rest_2_ = bf16[32,2560]{1,0:T(8,128)(2,1)S(1)} collective-permute-done((bf16[32,2560]{1,0:T(8,128)(2,1)S(1)}, bf16[32,2560]{1,0:T(8,128)(2,1)S(1)}, u32[]{:S(2)}, u32[]{:S(2)}) %collective-permute-start.15) | collective-permute-done | bytes 163872 | tf_op jit(solution)/shard_map/ppermute | solution.py:314
  56.7 0.0 collective-permute-done.16.rest_3_
  56.7 0.9 %unpack.1 = (bf16[32,8192]{1,0:T(8,128)(2,1)}, bf16[32,1024]{1,0:T(8,128)(2,1)}, bf16[32,1024]{1,0:T(8,128)(2,1)}) custom-call(s32[1]{0:T(128)} %bitcast.2.me_ref, bf16[32,2560]{1,0:T(8,128)(2,1)S(1)} %get-tuple-element.33.rest_0_, bf16[32,2560]{1,0:T(8,128)(2,1)S(1)} %collective-permute-done.14.rest_1_, ...), custom_call_target="tpu_custom_call" | custom-call | tf_op jit(solution)/shard_map/unpack/pallas_call | solution.py:291
  57.6 0.0 collective-permute-done.13
  57.6 0.0 collective-permute-done.12
  57.6 0.2 collective-permute-done.11
  57.8 0.1 fusion.2
  57.8 0.7 %fusion.6 = (bf16[128,256]{1,0:T(8,128)(2,1)}, bf16[128,256]{1,0:T(8,128)(2,1)}) fusion(bf16[128,512]{1,0:T(8,128)(2,1)S(1)} %fusion.2), kind=kLoop, calls=%fused_computation.10 | loop fusion | bytes 262144 | tf_op jit(solution)/shard_map/slice | solution.py:400
Async XLA Ops:
  2.5 7.6 %collective-permute-start = (bf16[128,512]{1,0:T(8,128)(2,1)S(1)}, bf16[128,512]{1,0:T(8,128)(2,1)S(1)}, u32[]{:S(2)}, u32[]{:S(2)}) collective-permute-start(bf16[128,512]{1,0:T(8,128)(2,1)S(1)} %get-tuple-element.24.rest_0_.rest_4_), channel_id=1, source_target_pairs={{0,4},{4,0},{8,12},{12,8},{16,20},{20,16},{24,28},{28,24},{1,5},{5... | collective-permute-start | bytes 393224 | tf_op jit(solution)/shard_map/ppermute | solution.py:314
  3.0 7.0 %collective-permute-start.1 = (bf16[128,512]{1,0:T(8,128)(2,1)S(1)}, bf16[128,512]{1,0:T(8,128)(2,1)S(1)}, u32[]{:S(2)}, u32[]{:S(2)}) collective-permute-start(bf16[128,512]{1,0:T(8,128)(2,1)S(1)} %get-tuple-element.24.rest_0_.rest_4_), channel_id=1, source_target_pairs={{0,8},{4,12},{8,0},{12,4},{16,24},{20,28},{24,16},{28,20},{1,9},{5... | collective-permute-start | bytes 393224 | tf_op jit(solution)/shard_map/ppermute | solution.py:314
  5.5 6.6 %collective-permute-start.2 = (bf16[128,512]{1,0:T(8,128)(2,1)S(1)}, bf16[128,512]{1,0:T(8,128)(2,1)S(1)}, u32[]{:S(2)}, u32[]{:S(2)}) collective-permute-start(bf16[128,512]{1,0:T(8,128)(2,1)S(1)} %get-tuple-element.24.rest_0_.rest_4_), channel_id=1, source_target_pairs={{0,12},{4,8},{8,4},{12,0},{16,28},{20,24},{24,20},{28,16},{1,13},{... | collective-permute-start | bytes 393224 | tf_op jit(solution)/shard_map/ppermute | solution.py:314
  5.6 27.7 %collective-permute-start.7 = (bf16[32,4736]{1,0:T(8,128)(2,1)S(1)}, bf16[32,4736]{1,0:T(8,128)(2,1)S(1)}, u32[]{:S(2)}, u32[]{:S(2)}) collective-permute-start(bf16[32,4736]{1,0:T(8,128)(2,1)S(1)} %get-tuple-element.26), channel_id=1, source_target_pairs={{0,2},{1,3},{2,0},{3,1},{4,6},{5,7},{6,4},{7,5},{8,10},{9,11},{10,... | collective-permute-start | bytes 909320 | tf_op jit(solution)/shard_map/ppermute | solution.py:314
  8.4 24.9 %collective-permute-start.8 = (bf16[32,4736]{1,0:T(8,128)(2,1)S(1)}, bf16[32,4736]{1,0:T(8,128)(2,1)S(1)}, u32[]{:S(2)}, u32[]{:S(2)}) collective-permute-start(bf16[32,4736]{1,0:T(8,128)(2,1)S(1)} %get-tuple-element.27), channel_id=1, source_target_pairs={{0,1},{1,0},{2,3},{3,2},{4,5},{5,4},{6,7},{7,6},{8,9},{9,8},{10,11... | collective-permute-start | bytes 909320 | tf_op jit(solution)/shard_map/ppermute | solution.py:314
  10.0 23.3 %collective-permute-start.9 = (bf16[32,4736]{1,0:T(8,128)(2,1)S(1)}, bf16[32,4736]{1,0:T(8,128)(2,1)S(1)}, u32[]{:S(2)}, u32[]{:S(2)}) collective-permute-start(bf16[32,4736]{1,0:T(8,128)(2,1)S(1)} %get-tuple-element.28), channel_id=1, source_target_pairs={{0,3},{1,2},{2,1},{3,0},{4,7},{5,6},{6,5},{7,4},{8,11},{9,10},{10,... | collective-permute-start | bytes 909320 | tf_op jit(solution)/shard_map/ppermute | solution.py:314
  10.0 5.3 %collective-permute-start.3 = (bf16[128,512]{1,0:T(8,128)(2,1)S(1)}, bf16[128,512]{1,0:T(8,128)(2,1)S(1)}, u32[]{:S(2)}, u32[]{:S(2)}) collective-permute-start(bf16[128,512]{1,0:T(8,128)(2,1)S(1)} %get-tuple-element.24.rest_0_.rest_4_), channel_id=1, source_target_pairs={{0,16},{4,20},{8,24},{12,28},{16,0},{20,4},{24,8},{28,12},{1,17},{... | collective-permute-start | bytes 393224 | tf_op jit(solution)/shard_map/ppermute | solution.py:314
  12.2 6.4 %collective-permute-start.4 = (bf16[128,512]{1,0:T(8,128)(2,1)S(1)}, bf16[128,512]{1,0:T(8,128)(2,1)S(1)}, u32[]{:S(2)}, u32[]{:S(2)}) collective-permute-start(bf16[128,512]{1,0:T(8,128)(2,1)S(1)} %get-tuple-element.24.rest_0_.rest_4_), channel_id=1, source_target_pairs={{0,20},{4,16},{8,28},{12,24},{16,4},{20,0},{24,12},{28,8},{1,21},{... | collective-permute-start | bytes 393224 | tf_op jit(solution)/shard_map/ppermute | solution.py:314
  15.3 6.4 %collective-permute-start.5 = (bf16[128,512]{1,0:T(8,128)(2,1)S(1)}, bf16[128,512]{1,0:T(8,128)(2,1)S(1)}, u32[]{:S(2)}, u32[]{:S(2)}) collective-permute-start(bf16[128,512]{1,0:T(8,128)(2,1)S(1)} %get-tuple-element.24.rest_0_.rest_4_), channel_id=1, source_target_pairs={{0,24},{4,28},{8,16},{12,20},{16,8},{20,12},{24,0},{28,4},{1,25},{... | collective-permute-start | bytes 393224 | tf_op jit(solution)/shard_map/ppermute | solution.py:314
  18.6 6.5 %collective-permute-start.6 = (bf16[128,512]{1,0:T(8,128)(2,1)S(1)}, bf16[128,512]{1,0:T(8,128)(2,1)S(1)}, u32[]{:S(2)}, u32[]{:S(2)}) collective-permute-start(bf16[128,512]{1,0:T(8,128)(2,1)S(1)} %get-tuple-element.24.rest_0_.rest_4_), channel_id=1, source_target_pairs={{0,28},{4,24},{8,20},{12,16},{16,12},{20,8},{24,4},{28,0},{1,29},{... | collective-permute-start | bytes 393224 | tf_op jit(solution)/shard_map/ppermute | solution.py:314
  38.6 6.6 %collective-permute-start.10 = (bf16[4,128,512]{2,1,0:T(8,128)(2,1)S(1)}, bf16[4,128,512]{2,1,0:T(8,128)(2,1)S(1)}, u32[]{:S(2)}, u32[]{:S(2)}) collective-permute-start(bf16[4,128,512]{2,1,0:T(8,128)(2,1)S(1)} %get-tuple-element.32), channel_id=1, source_target_pairs={{0,4},{4,0},{8,12},{12,8},{16,20},{20,16},{24,28},{28,24},{1,5},{5... | collective-permute-start | bytes 1572872 | tf_op jit(solution)/shard_map/ppermute | solution.py:314
  39.5 13.3 %collective-permute-start.14 = (bf16[32,2560]{1,0:T(8,128)(2,1)S(1)}, bf16[32,2560]{1,0:T(8,128)(2,1)S(1)}, u32[]{:S(2)}, u32[]{:S(2)}) collective-permute-start(bf16[32,2560]{1,0:T(8,128)(2,1)S(1)} %get-tuple-element.34), channel_id=1, source_target_pairs={{0,2},{1,3},{2,0},{3,1},{4,6},{5,7},{6,4},{7,5},{8,10},{9,11},{10,... | collective-permute-start | bytes 491528 | tf_op jit(solution)/shard_map/ppermute | solution.py:314
  43.7 13.0 %collective-permute-start.15 = (bf16[32,2560]{1,0:T(8,128)(2,1)S(1)}, bf16[32,2560]{1,0:T(8,128)(2,1)S(1)}, u32[]{:S(2)}, u32[]{:S(2)}) collective-permute-start(bf16[32,2560]{1,0:T(8,128)(2,1)S(1)} %get-tuple-element.35), channel_id=1, source_target_pairs={{0,1},{1,0},{2,3},{3,2},{4,5},{5,4},{6,7},{7,6},{8,9},{9,8},{10,11... | collective-permute-start | bytes 491528 | tf_op jit(solution)/shard_map/ppermute | solution.py:314
  43.7 13.0 %collective-permute-start.16 = (bf16[32,2560]{1,0:T(8,128)(2,1)S(1)}, bf16[32,2560]{1,0:T(8,128)(2,1)S(1)}, u32[]{:S(2)}, u32[]{:S(2)}) collective-permute-start(bf16[32,2560]{1,0:T(8,128)(2,1)S(1)} %get-tuple-element.36), channel_id=1, source_target_pairs={{0,3},{1,2},{2,1},{3,0},{4,7},{5,6},{6,5},{7,4},{8,11},{9,10},{10,... | collective-permute-start | bytes 491528 | tf_op jit(solution)/shard_map/ppermute | solution.py:314
  45.4 12.2 %collective-permute-start.13 = (bf16[128,512]{1,0:T(8,128)(2,1)S(1)}, bf16[128,512]{1,0:T(8,128)(2,1)S(1)}, u32[]{:S(2)}, u32[]{:S(2)}) collective-permute-start(bf16[128,512]{1,0:T(8,128)(2,1)S(1)} %get-tuple-element.41), channel_id=1, source_target_pairs={{0,24},{4,28},{8,16},{12,20},{16,8},{20,12},{24,0},{28,4},{1,25},{... | collective-permute-start | bytes 393224 | tf_op jit(solution)/shard_map/ppermute | solution.py:314
  47.9 9.7 %collective-permute-start.12 = (bf16[128,512]{1,0:T(8,128)(2,1)S(1)}, bf16[128,512]{1,0:T(8,128)(2,1)S(1)}, u32[]{:S(2)}, u32[]{:S(2)}) collective-permute-start(bf16[128,512]{1,0:T(8,128)(2,1)S(1)} %get-tuple-element.42), channel_id=1, source_target_pairs={{0,16},{4,20},{8,24},{12,28},{16,0},{20,4},{24,8},{28,12},{1,17},{... | collective-permute-start | bytes 393224 | tf_op jit(solution)/shard_map/ppermute | solution.py:314
  52.8 5.0 %collective-permute-start.11 = (bf16[128,512]{1,0:T(8,128)(2,1)S(1)}, bf16[128,512]{1,0:T(8,128)(2,1)S(1)}, u32[]{:S(2)}, u32[]{:S(2)}) collective-permute-start(bf16[128,512]{1,0:T(8,128)(2,1)S(1)} %get-tuple-element.40), channel_id=1, source_target_pairs={{0,8},{4,12},{8,0},{12,4},{16,24},{20,28},{24,16},{28,20},{1,9},{5... | collective-permute-start | bytes 393224 | tf_op jit(solution)/shard_map/ppermute | solution.py:314

commit v5 on v4

--- a/solution.py
+++ b/solution.py
@@ -12,7 +12,7 @@
 LOG2E = math.log2(math.e)
 SCALE = 1.0 / math.sqrt(HEAD)
 VMEM_LIMIT = 28 * 1024 * 1024
-KEY_CHUNK = 512
+KEY_CHUNK = 256
 
 BF = jnp.bfloat16
 F32 = jnp.float32
@@ -270,8 +270,14 @@
                 back[:, first : first + HEAD] = result[start : start + rows]
 
 
-def unpack_kernel(me_ref, *rest):
-    backs, (rq_ref, rk_ref, rv_ref) = by_partner(rest[:-3]), rest[-3:]
+def unpack_kernel(sums, me_ref, *rest):
+    (own_ref, *got), rest = rest[:sums], rest[sums:]
+    backs, (pk_ref, pv_ref, rq_ref, rk_ref, rv_ref) = by_partner(rest[:-5]), rest[-5:]
+    total = own_ref[...]
+    for ref in got:
+        total = total + ref[...].astype(F32)
+    pk_ref[...] = total[:, : pk_ref.shape[1]].astype(BF)
+    pv_ref[...] = total[:, pk_ref.shape[1] :].astype(BF)
     me = me_ref[0]
     width = rq_ref.shape[1] // len(backs)
     narrow = rk_ref.shape[1] // len(backs)
@@ -369,7 +375,11 @@
         ),
     )
     got = [swap(x, "roll", k) if k else x for k, x in enumerate(packs)]
-    blocks = [in_vmem(swap(kv, "ctx", s) if s else kv) for s in range(slots)]
+    blocks = [kv]
+    for s in range(1, slots):
+        double = s % 2 and bin(s).count("1") > 2
+        blocks.append(swap(blocks[s - 1], "ctx", 1) if double else swap(kv, "ctx", s))
+    blocks = [in_vmem(x) for x in blocks]
 
     prompt_dq, part, roll_own_dq = call(
         functools.partial(prompt_kernel, members),
@@ -394,19 +404,18 @@
     odd_got = swap(odd, "ctx", 1)
     backs = [in_vmem(swap(x, "roll", k) if k else x) for k, x in enumerate(backs)]
     pair = [even[t] + odd_got[t].astype(F32) for t in range(slots // 2)]
-    total = pair[0]
-    for t in range(1, slots // 2):
-        total = total + swap(pair[t].astype(BF), "ctx", 2 * t).astype(F32)
-    prompt_dk, prompt_dv = total[:, :narrow].astype(BF), total[:, narrow:].astype(BF)
-    roll_dq, roll_dk, roll_dv = call(
-        unpack_kernel,
+    sums = [pair[0]] + [swap(pair[t].astype(BF), "ctx", 2 * t) for t in range(slots // 2 - 1, 0, -1)]
+    prompt_dk, prompt_dv, roll_dq, roll_dk, roll_dv = call(
+        functools.partial(unpack_kernel, len(sums)),
         "unpack",
         [
+            shape((prompt_rows, narrow), BF),
+            shape((prompt_rows, narrow), BF),
             shape((rows, parts * width), BF),
             shape((rows, parts * narrow), BF),
             shape((rows, parts * narrow), BF),
         ],
-        (roll_id, *[backs[k] for k in send_order(parts)]),
+        (roll_id, *map(in_vmem, sums), *[backs[k] for k in send_order(parts)]),
     )
     return prompt_dq, prompt_dk, prompt_dv, roll_dq, roll_dk, roll_dv
 

time: 58.7 us -> 58.5 us (level)
  starting transfers between devices: 27.9 us -> 25.2 us
  waiting for transfers between devices: 12.8 us -> 15.2 us
  Pallas kernels: 16.2 us -> 17.1 us
  local copies, waits for them, and re-layouts: 0.66 us -> 0 us
    ppermute x17, starting transfers between devices: 27.9 us -> 25.2 us  [swap(): return lax.ppermute(x, axis, [(i, i ^ k) for i in range(n)])]
    ppermute x17, waiting for transfers between devices: 12.8 us -> 15.2 us  [swap(): return lax.ppermute(x, axis, [(i, i ^ k) for i in range(n)])]
    pallas_call x4, Pallas kernels: 16.2 us -> 17.1 us  [call(): pl.pallas_call(kernel, name=name, out_shape=outs, in_specs=[SMEM] * scala...]
    slice x1 -> x0, local copies, waits for them, and re-layouts: 0.66 us -> none  [on_device(): total[:, narrow:].astype(BF)]
where the time goes in v5:
time: 58.5 us; the launch traced here: 58.4 us
  starting transfers between devices  25.2 us (43%)
  Pallas kernels  17.1 us (29%)
  waiting for transfers between devices  15.2 us (26%)
  between operations  0.68 us (1%)
    ppermute x17, starting transfers between devices, swap(): return lax.ppermute(x, axis, [(i, i ^ k) for i in range(n)])  25.2 us
    pallas_call x4, Pallas kernels, call(): pl.pallas_call(kernel, name=name, out_shape=outs, in_specs=[SMEM] * scala...  17.1 us
    ppermute x17, waiting for transfers between devices, swap(): return lax.ppermute(x, axis, [(i, i ^ k) for i in range(n)])  15.2 us
  transfers between devices with their start and end apart: 17, of which 7 were waited for; matrix products, arithmetic and copies ran while one was open for 0% of the time, Pallas kernels for 16%

profile of v5, /device:TPU:0, one launch (start us, length us, event | category | flops | bytes accessed | tf_op | source)
XLA Modules:
  0.0 58.4 jit_solution(14699517153006895519)
XLA Ops:
  0.6 1.8 %pack.1 = (bf16[128,512]{1,0:T(8,128)(2,1)S(1)}, bf16[32,4736]{1,0:T(8,128)(2,1)S(1)}, bf16[32,4736]{1,0:T(8,128)(2,1)S(1)}, bf16[32,4736]{1,0:T(8,128)(2,1)S(1)}, bf16[32,4736]{1,0:T(8,128)(2,1)S(1)}) custom-call(s32[1]{0:T(128)} %bitcast.2.me_ref, bf16[32,8192]{1,0:T(8,128)(2,1)} %q_ref.2, bf16[32,8192]{1,0:T(8,128)(2,1)} %do_ref.2, ...), custom_call_target="tpu_custom_call" | custom-call | tf_op jit(solution)/shard_map/pack/pallas_call | solution.py:297
  2.5 0.5 collective-permute-start
  3.0 2.6 %collective-permute-start.1 = (bf16[128,512]{1,0:T(8,128)(2,1)S(1)}, bf16[128,512]{1,0:T(8,128)(2,1)S(1)}, u32[]{:S(2)}, u32[]{:S(2)}) collective-permute-start(bf16[128,512]{1,0:T(8,128)(2,1)S(1)} %get-tuple-element.26.rest_0_.rest_4_), channel_id=1, source_target_pairs={{0,8},{4,12},{8,0},{12,4},{16,24},{20,28},{24,16},{28,20},{1,9},{5... | collective-permute-start | bytes 393224 | tf_op jit(solution)/shard_map/ppermute | solution.py:320
  5.5 0.1 collective-permute-start.2
  5.6 2.8 %collective-permute-start.7 = (bf16[32,4736]{1,0:T(8,128)(2,1)S(1)}, bf16[32,4736]{1,0:T(8,128)(2,1)S(1)}, u32[]{:S(2)}, u32[]{:S(2)}) collective-permute-start(bf16[32,4736]{1,0:T(8,128)(2,1)S(1)} %get-tuple-element.28), channel_id=1, source_target_pairs={{0,2},{1,3},{2,0},{3,1},{4,6},{5,7},{6,4},{7,5},{8,10},{9,11},{10,... | collective-permute-start | bytes 909320 | tf_op jit(solution)/shard_map/ppermute | solution.py:320
  8.4 1.6 %collective-permute-start.8 = (bf16[32,4736]{1,0:T(8,128)(2,1)S(1)}, bf16[32,4736]{1,0:T(8,128)(2,1)S(1)}, u32[]{:S(2)}, u32[]{:S(2)}) collective-permute-start(bf16[32,4736]{1,0:T(8,128)(2,1)S(1)} %get-tuple-element.29), channel_id=1, source_target_pairs={{0,1},{1,0},{2,3},{3,2},{4,5},{5,4},{6,7},{7,6},{8,9},{9,8},{10,11... | collective-permute-start | bytes 909320 | tf_op jit(solution)/shard_map/ppermute | solution.py:320
  10.0 0.0 collective-permute-done.rest_1_.rest_5_
  10.0 0.0 collective-permute-start.9
  10.0 0.0 collective-permute-done.1.rest_2_.rest_6_
  10.0 1.8 %collective-permute-start.3 = (bf16[128,512]{1,0:T(8,128)(2,1)S(1)}, bf16[128,512]{1,0:T(8,128)(2,1)S(1)}, u32[]{:S(2)}, u32[]{:S(2)}) collective-permute-start(bf16[128,512]{1,0:T(8,128)(2,1)S(1)} %get-tuple-element.26.rest_0_.rest_4_), channel_id=1, source_target_pairs={{0,16},{4,20},{8,24},{12,28},{16,0},{20,4},{24,8},{28,12},{1,17},{... | collective-permute-start | bytes 393224 | tf_op jit(solution)/shard_map/ppermute | solution.py:320
  11.9 0.3 collective-permute-done.2.rest_3_.rest_7_
  12.2 2.5 %collective-permute-start.5 = (bf16[128,512]{1,0:T(8,128)(2,1)S(1)}, bf16[128,512]{1,0:T(8,128)(2,1)S(1)}, u32[]{:S(2)}, u32[]{:S(2)}) collective-permute-start(bf16[128,512]{1,0:T(8,128)(2,1)S(1)} %get-tuple-element.26.rest_0_.rest_4_), channel_id=1, source_target_pairs={{0,24},{4,28},{8,16},{12,20},{16,8},{20,12},{24,0},{28,4},{1,25},{... | collective-permute-start | bytes 393224 | tf_op jit(solution)/shard_map/ppermute | solution.py:320
  14.7 0.6 collective-permute-done.3.rest_4_.rest_8_
  15.3 0.0 collective-permute-start.4
  15.3 3.7 %collective-permute-done.5.rest_6_.rest_10_ = bf16[128,512]{1,0:T(8,128)(2,1)S(1)} collective-permute-done((bf16[128,512]{1,0:T(8,128)(2,1)S(1)}, bf16[128,512]{1,0:T(8,128)(2,1)S(1)}, u32[]{:S(2)}, u32[]{:S(2)}) %collective-permute-start.5) | collective-permute-done | bytes 131104 | tf_op jit(solution)/shard_map/ppermute | solution.py:320
  19.0 0.0 collective-permute-start.6
  19.0 2.7 %collective-permute-done.4.rest_5_.rest_9_ = bf16[128,512]{1,0:T(8,128)(2,1)S(1)} collective-permute-done((bf16[128,512]{1,0:T(8,128)(2,1)S(1)}, bf16[128,512]{1,0:T(8,128)(2,1)S(1)}, u32[]{:S(2)}, u32[]{:S(2)}) %collective-permute-start.4) | collective-permute-done | bytes 131104 | tf_op jit(solution)/shard_map/ppermute | solution.py:320
  21.7 0.0 collective-permute-done.6.rest_7_.rest_11_
  21.7 9.4 %prompt_grads.1 = (bf16[128,2048]{1,0:T(8,128)(2,1)}, f32[8,128,512]{2,1,0:T(8,128)S(1)}, f32[2,128,256]{2,1,0:T(8,128)S(1)}) custom-call(s32[1]{0:T(128)} %bitcast.me_ref, bf16[128,2048]{1,0:T(8,128)(2,1)} %q_ref.3, bf16[128,2048]{1,0:T(8,128)(2,1)} %do_ref.3, bf16[128,2048]{1,0:T(8,128)(2,1)} %o_ref.3, bf16[16,128]{1,0:T(8,128)(2,1)} %bitcast.11, ...), custom_call_target="tpu_custom_call" | custom-call | tf_op jit(solution)/shard_map/prompt_grads/pallas_call | solution.py:297
  31.1 0.0 collective-permute-done.7.rest_1_
  31.1 0.0 collective-permute-done.8.rest_2_
  31.1 0.0 collective-permute-done.9.rest_3_
  31.1 5.0 %roll_grads.1 = (f32[4,128,512]{2,1,0:T(8,128)S(1)}, bf16[4,128,512]{2,1,0:T(8,128)(2,1)S(1)}, bf16[32,2560]{1,0:T(8,128)(2,1)S(1)}, bf16[32,2560]{1,0:T(8,128)(...) custom-call(s32[1]{0:T(128)} %bitcast.2.me_ref, ...), custom_call_target="tpu_custom_call" | custom-call | tf_op jit(solution)/shard_map/roll_grads/pallas_call | solution.py:297
  36.1 0.2 collective-permute-start.10
  36.3 7.1 %collective-permute-start.14 = (bf16[32,2560]{1,0:T(8,128)(2,1)S(1)}, bf16[32,2560]{1,0:T(8,128)(2,1)S(1)}, u32[]{:S(2)}, u32[]{:S(2)}) collective-permute-start(bf16[32,2560]{1,0:T(8,128)(2,1)S(1)} %get-tuple-element.36), channel_id=1, source_target_pairs={{0,2},{1,3},{2,0},{3,1},{4,6},{5,7},{6,4},{7,5},{8,10},{9,11},{10,... | collective-permute-start | bytes 491528 | tf_op jit(solution)/shard_map/ppermute | solution.py:320
  43.4 0.0 collective-permute-start.15
  43.4 1.5 %collective-permute-start.16 = (bf16[32,2560]{1,0:T(8,128)(2,1)S(1)}, bf16[32,2560]{1,0:T(8,128)(2,1)S(1)}, u32[]{:S(2)}, u32[]{:S(2)}) collective-permute-start(bf16[32,2560]{1,0:T(8,128)(2,1)S(1)} %get-tuple-element.38), channel_id=1, source_target_pairs={{0,3},{1,2},{2,1},{3,0},{4,7},{5,6},{6,5},{7,4},{8,11},{9,10},{10,... | collective-permute-start | bytes 491528 | tf_op jit(solution)/shard_map/ppermute | solution.py:320
  45.0 0.0 collective-permute-done.10
  45.0 0.2 fusion.2
  45.1 2.5 %collective-permute-start.11 = (bf16[128,512]{1,0:T(8,128)(2,1)S(1)}, bf16[128,512]{1,0:T(8,128)(2,1)S(1)}, u32[]{:S(2)}, u32[]{:S(2)}) collective-permute-start(bf16[128,512]{1,0:T(8,128)(2,1)S(1)} %get-tuple-element.46), channel_id=1, source_target_pairs={{0,24},{4,28},{8,16},{12,20},{16,8},{20,12},{24,0},{28,4},{1,25},{... | collective-permute-start | bytes 393224 | tf_op jit(solution)/shard_map/ppermute | solution.py:320
  47.6 0.5 collective-permute-start.12
  48.1 4.3 %collective-permute-done.14.rest_5_ = bf16[32,2560]{1,0:T(8,128)(2,1)S(1)} collective-permute-done((bf16[32,2560]{1,0:T(8,128)(2,1)S(1)}, bf16[32,2560]{1,0:T(8,128)(2,1)S(1)}, u32[]{:S(2)}, u32[]{:S(2)}) %collective-permute-start.14) | collective-permute-done | bytes 163872 | tf_op jit(solution)/shard_map/ppermute | solution.py:320
  52.5 1.5 %collective-permute-start.13 = (bf16[128,512]{1,0:T(8,128)(2,1)S(1)}, bf16[128,512]{1,0:T(8,128)(2,1)S(1)}, u32[]{:S(2)}, u32[]{:S(2)}) collective-permute-start(bf16[128,512]{1,0:T(8,128)(2,1)S(1)} %get-tuple-element.44), channel_id=1, source_target_pairs={{0,8},{4,12},{8,0},{12,4},{16,24},{20,28},{24,16},{28,20},{1,9},{5... | collective-permute-start | bytes 393224 | tf_op jit(solution)/shard_map/ppermute | solution.py:320
  54.0 2.4 %collective-permute-done.15.rest_6_ = bf16[32,2560]{1,0:T(8,128)(2,1)S(1)} collective-permute-done((bf16[32,2560]{1,0:T(8,128)(2,1)S(1)}, bf16[32,2560]{1,0:T(8,128)(2,1)S(1)}, u32[]{:S(2)}, u32[]{:S(2)}) %collective-permute-start.15) | collective-permute-done | bytes 163872 | tf_op jit(solution)/shard_map/ppermute | solution.py:320
  56.4 0.0 collective-permute-done.16.rest_7_
  56.4 0.0 collective-permute-done.11.rest_1_
  56.4 0.0 collective-permute-done.12.rest_2_
  56.4 1.0 %collective-permute-done.13.rest_3_ = bf16[128,512]{1,0:T(8,128)(2,1)S(1)} collective-permute-done((bf16[128,512]{1,0:T(8,128)(2,1)S(1)}, bf16[128,512]{1,0:T(8,128)(2,1)S(1)}, u32[]{:S(2)}, u32[]{:S(2)}) %collective-permute-start.13) | collective-permute-done | bytes 131104 | tf_op jit(solution)/shard_map/ppermute | solution.py:320
  57.4 0.9 %unpack.1 = (bf16[128,256]{1,0:T(8,128)(2,1)}, bf16[128,256]{1,0:T(8,128)(2,1)}, bf16[32,8192]{1,0:T(8,128)(2,1)}, bf16[32,1024]{1,0:T(8,128)(2,1)}, bf16[32,1024]{1,0:T(8,128)(2,1)}) custom-call(s32[1]{0:T(128)} %bitcast.2.me_ref, f32[128,512]{1,0:T(8,128)S(1)} %get-tuple-element.47.rest_0_, bf16[128,512]{1,0:T(8,128)(2,1)S(1)} %collective-permute-done.11.rest_1_, ...), custom_call_target="tpu_custom_call" | custom-call | tf_op jit(solution)/shard_map/unpack/pallas_call | solution.py:297
Async XLA Ops:
  2.5 7.6 %collective-permute-start = (bf16[128,512]{1,0:T(8,128)(2,1)S(1)}, bf16[128,512]{1,0:T(8,128)(2,1)S(1)}, u32[]{:S(2)}, u32[]{:S(2)}) collective-permute-start(bf16[128,512]{1,0:T(8,128)(2,1)S(1)} %get-tuple-element.26.rest_0_.rest_4_), channel_id=1, source_target_pairs={{0,4},{4,0},{8,12},{12,8},{16,20},{20,16},{24,28},{28,24},{1,5},{5... | collective-permute-start | bytes 393224 | tf_op jit(solution)/shard_map/ppermute | solution.py:320
  3.0 7.0 %collective-permute-start.1 = (bf16[128,512]{1,0:T(8,128)(2,1)S(1)}, bf16[128,512]{1,0:T(8,128)(2,1)S(1)}, u32[]{:S(2)}, u32[]{:S(2)}) collective-permute-start(bf16[128,512]{1,0:T(8,128)(2,1)S(1)} %get-tuple-element.26.rest_0_.rest_4_), channel_id=1, source_target_pairs={{0,8},{4,12},{8,0},{12,4},{16,24},{20,28},{24,16},{28,20},{1,9},{5... | collective-permute-start | bytes 393224 | tf_op jit(solution)/shard_map/ppermute | solution.py:320
  5.5 6.6 %collective-permute-start.2 = (bf16[128,512]{1,0:T(8,128)(2,1)S(1)}, bf16[128,512]{1,0:T(8,128)(2,1)S(1)}, u32[]{:S(2)}, u32[]{:S(2)}) collective-permute-start(bf16[128,512]{1,0:T(8,128)(2,1)S(1)} %get-tuple-element.26.rest_0_.rest_4_), channel_id=1, source_target_pairs={{0,12},{4,8},{8,4},{12,0},{16,28},{20,24},{24,20},{28,16},{1,13},{... | collective-permute-start | bytes 393224 | tf_op jit(solution)/shard_map/ppermute | solution.py:320
  5.6 25.5 %collective-permute-start.7 = (bf16[32,4736]{1,0:T(8,128)(2,1)S(1)}, bf16[32,4736]{1,0:T(8,128)(2,1)S(1)}, u32[]{:S(2)}, u32[]{:S(2)}) collective-permute-start(bf16[32,4736]{1,0:T(8,128)(2,1)S(1)} %get-tuple-element.28), channel_id=1, source_target_pairs={{0,2},{1,3},{2,0},{3,1},{4,6},{5,7},{6,4},{7,5},{8,10},{9,11},{10,... | collective-permute-start | bytes 909320 | tf_op jit(solution)/shard_map/ppermute | solution.py:320
  8.4 22.7 %collective-permute-start.8 = (bf16[32,4736]{1,0:T(8,128)(2,1)S(1)}, bf16[32,4736]{1,0:T(8,128)(2,1)S(1)}, u32[]{:S(2)}, u32[]{:S(2)}) collective-permute-start(bf16[32,4736]{1,0:T(8,128)(2,1)S(1)} %get-tuple-element.29), channel_id=1, source_target_pairs={{0,1},{1,0},{2,3},{3,2},{4,5},{5,4},{6,7},{7,6},{8,9},{9,8},{10,11... | collective-permute-start | bytes 909320 | tf_op jit(solution)/shard_map/ppermute | solution.py:320
  10.0 21.1 %collective-permute-start.9 = (bf16[32,4736]{1,0:T(8,128)(2,1)S(1)}, bf16[32,4736]{1,0:T(8,128)(2,1)S(1)}, u32[]{:S(2)}, u32[]{:S(2)}) collective-permute-start(bf16[32,4736]{1,0:T(8,128)(2,1)S(1)} %get-tuple-element.30), channel_id=1, source_target_pairs={{0,3},{1,2},{2,1},{3,0},{4,7},{5,6},{6,5},{7,4},{8,11},{9,10},{10,... | collective-permute-start | bytes 909320 | tf_op jit(solution)/shard_map/ppermute | solution.py:320
  10.0 5.3 %collective-permute-start.3 = (bf16[128,512]{1,0:T(8,128)(2,1)S(1)}, bf16[128,512]{1,0:T(8,128)(2,1)S(1)}, u32[]{:S(2)}, u32[]{:S(2)}) collective-permute-start(bf16[128,512]{1,0:T(8,128)(2,1)S(1)} %get-tuple-element.26.rest_0_.rest_4_), channel_id=1, source_target_pairs={{0,16},{4,20},{8,24},{12,28},{16,0},{20,4},{24,8},{28,12},{1,17},{... | collective-permute-start | bytes 393224 | tf_op jit(solution)/shard_map/ppermute | solution.py:320
  12.2 6.8 %collective-permute-start.5 = (bf16[128,512]{1,0:T(8,128)(2,1)S(1)}, bf16[128,512]{1,0:T(8,128)(2,1)S(1)}, u32[]{:S(2)}, u32[]{:S(2)}) collective-permute-start(bf16[128,512]{1,0:T(8,128)(2,1)S(1)} %get-tuple-element.26.rest_0_.rest_4_), channel_id=1, source_target_pairs={{0,24},{4,28},{8,16},{12,20},{16,8},{20,12},{24,0},{28,4},{1,25},{... | collective-permute-start | bytes 393224 | tf_op jit(solution)/shard_map/ppermute | solution.py:320
  15.3 6.5 %collective-permute-start.4 = (bf16[128,512]{1,0:T(8,128)(2,1)S(1)}, bf16[128,512]{1,0:T(8,128)(2,1)S(1)}, u32[]{:S(2)}, u32[]{:S(2)}) collective-permute-start(bf16[128,512]{1,0:T(8,128)(2,1)S(1)} %get-tuple-element.26.rest_0_.rest_4_), channel_id=1, source_target_pairs={{0,20},{4,16},{8,28},{12,24},{16,4},{20,0},{24,12},{28,8},{1,21},{... | collective-permute-start | bytes 393224 | tf_op jit(solution)/shard_map/ppermute | solution.py:320
  19.0 2.7 %collective-permute-start.6 = (bf16[128,512]{1,0:T(8,128)(2,1)S(1)}, bf16[128,512]{1,0:T(8,128)(2,1)S(1)}, u32[]{:S(2)}, u32[]{:S(2)}) collective-permute-start(bf16[128,512]{1,0:T(8,128)(2,1)S(1)} %collective-permute-done.5.rest_6_.rest_10_), channel_id=1, source_target_pairs={{0,4},{4,0},{8,12},{12,8},{16,20},{20,16},{24,28},{28,24},{1,5},{5... | collective-permute-start | bytes 393224 | tf_op jit(solution)/shard_map/ppermute | solution.py:320
  36.1 8.8 %collective-permute-start.10 = (bf16[4,128,512]{2,1,0:T(8,128)(2,1)S(1)}, bf16[4,128,512]{2,1,0:T(8,128)(2,1)S(1)}, u32[]{:S(2)}, u32[]{:S(2)}) collective-permute-start(bf16[4,128,512]{2,1,0:T(8,128)(2,1)S(1)} %get-tuple-element.34), channel_id=1, source_target_pairs={{0,4},{4,0},{8,12},{12,8},{16,20},{20,16},{24,28},{28,24},{1,5},{5... | collective-permute-start | bytes 1572872 | tf_op jit(solution)/shard_map/ppermute | solution.py:320
  36.3 16.2 %collective-permute-start.14 = (bf16[32,2560]{1,0:T(8,128)(2,1)S(1)}, bf16[32,2560]{1,0:T(8,128)(2,1)S(1)}, u32[]{:S(2)}, u32[]{:S(2)}) collective-permute-start(bf16[32,2560]{1,0:T(8,128)(2,1)S(1)} %get-tuple-element.36), channel_id=1, source_target_pairs={{0,2},{1,3},{2,0},{3,1},{4,6},{5,7},{6,4},{7,5},{8,10},{9,11},{10,... | collective-permute-start | bytes 491528 | tf_op jit(solution)/shard_map/ppermute | solution.py:320
  43.4 13.0 %collective-permute-start.15 = (bf16[32,2560]{1,0:T(8,128)(2,1)S(1)}, bf16[32,2560]{1,0:T(8,128)(2,1)S(1)}, u32[]{:S(2)}, u32[]{:S(2)}) collective-permute-start(bf16[32,2560]{1,0:T(8,128)(2,1)S(1)} %get-tuple-element.37), channel_id=1, source_target_pairs={{0,1},{1,0},{2,3},{3,2},{4,5},{5,4},{6,7},{7,6},{8,9},{9,8},{10,11... | collective-permute-start | bytes 491528 | tf_op jit(solution)/shard_map/ppermute | solution.py:320
  43.4 13.0 %collective-permute-start.16 = (bf16[32,2560]{1,0:T(8,128)(2,1)S(1)}, bf16[32,2560]{1,0:T(8,128)(2,1)S(1)}, u32[]{:S(2)}, u32[]{:S(2)}) collective-permute-start(bf16[32,2560]{1,0:T(8,128)(2,1)S(1)} %get-tuple-element.38), channel_id=1, source_target_pairs={{0,3},{1,2},{2,1},{3,0},{4,7},{5,6},{6,5},{7,4},{8,11},{9,10},{10,... | collective-permute-start | bytes 491528 | tf_op jit(solution)/shard_map/ppermute | solution.py:320
  45.1 11.3 %collective-permute-start.11 = (bf16[128,512]{1,0:T(8,128)(2,1)S(1)}, bf16[128,512]{1,0:T(8,128)(2,1)S(1)}, u32[]{:S(2)}, u32[]{:S(2)}) collective-permute-start(bf16[128,512]{1,0:T(8,128)(2,1)S(1)} %get-tuple-element.46), channel_id=1, source_target_pairs={{0,24},{4,28},{8,16},{12,20},{16,8},{20,12},{24,0},{28,4},{1,25},{... | collective-permute-start | bytes 393224 | tf_op jit(solution)/shard_map/ppermute | solution.py:320
  47.6 8.8 %collective-permute-start.12 = (bf16[128,512]{1,0:T(8,128)(2,1)S(1)}, bf16[128,512]{1,0:T(8,128)(2,1)S(1)}, u32[]{:S(2)}, u32[]{:S(2)}) collective-permute-start(bf16[128,512]{1,0:T(8,128)(2,1)S(1)} %get-tuple-element.45), channel_id=1, source_target_pairs={{0,16},{4,20},{8,24},{12,28},{16,0},{20,4},{24,8},{28,12},{1,17},{... | collective-permute-start | bytes 393224 | tf_op jit(solution)/shard_map/ppermute | solution.py:320
  52.5 5.0 %collective-permute-start.13 = (bf16[128,512]{1,0:T(8,128)(2,1)S(1)}, bf16[128,512]{1,0:T(8,128)(2,1)S(1)}, u32[]{:S(2)}, u32[]{:S(2)}) collective-permute-start(bf16[128,512]{1,0:T(8,128)(2,1)S(1)} %get-tuple-element.44), channel_id=1, source_target_pairs={{0,8},{4,12},{8,0},{12,4},{16,24},{20,28},{24,16},{28,20},{1,9},{5... | collective-permute-start | bytes 393224 | tf_op jit(solution)/shard_map/ppermute | solution.py:320

commit v6 on v5

--- a/solution.py
+++ b/solution.py
@@ -60,8 +60,11 @@
     return sorted(range(parts), key=lambda k: (k % 2, k))
 
 
-def by_partner(refs):
-    order = send_order(len(refs))
+def return_order(parts):
+    return sorted(range(parts), key=lambda k: (k > 0, k % 2 == 0, -k))
+
+
+def by_partner(refs, order):
     return [refs[order.index(k)] for k in range(len(refs))]
 
 
@@ -204,7 +207,7 @@
 
 
 def roll_kernel(parts, slots, members, me_ref, *rest):
-    packs, rest = by_partner(rest[:parts]), rest[parts:]
+    packs, rest = by_partner(rest[:parts], send_order(parts)), rest[parts:]
     kv_refs, rest = rest[:slots], rest[slots:]
     part_ref, roll_dq_ref, even_ref, odd_ref = rest[:4]
     backs = rest[4:]
@@ -272,7 +275,7 @@
 
 def unpack_kernel(sums, me_ref, *rest):
     (own_ref, *got), rest = rest[:sums], rest[sums:]
-    backs, (pk_ref, pv_ref, rq_ref, rk_ref, rv_ref) = by_partner(rest[:-5]), rest[-5:]
+    backs, (pk_ref, pv_ref, rq_ref, rk_ref, rv_ref) = by_partner(rest[:-5], return_order(len(rest) - 5)), rest[-5:]
     total = own_ref[...]
     for ref in got:
         total = total + ref[...].astype(F32)
@@ -415,7 +418,7 @@
             shape((rows, parts * narrow), BF),
             shape((rows, parts * narrow), BF),
         ],
-        (roll_id, *map(in_vmem, sums), *[backs[k] for k in send_order(parts)]),
+        (roll_id, *map(in_vmem, sums), *[backs[k] for k in return_order(parts)]),
     )
     return prompt_dq, prompt_dk, prompt_dv, roll_dq, roll_dk, roll_dv
 

time: 58.5 us -> 56.5 us (0.966)
  starting transfers between devices: 25.2 us -> 23.3 us
    ppermute x17, starting transfers between devices: 25.2 us -> 23.3 us  [swap(): return lax.ppermute(x, axis, [(i, i ^ k) for i in range(n)])]
  transfers between devices with their start and end apart: 17 -> 17, of which waited for: 7 -> 6; matrix products, arithmetic and copies ran while one was open for 0% -> 0% of each run, Pallas kernels for 16% -> 17%
where the time goes in v6:
time: 56.5 us; the launch traced here: 56.4 us
  starting transfers between devices  23.3 us (41%)
  Pallas kernels  17.1 us (30%)
  waiting for transfers between devices  15.1 us (27%)
  between operations  0.68 us (1%)
    ppermute x17, starting transfers between devices, swap(): return lax.ppermute(x, axis, [(i, i ^ k) for i in range(n)])  23.3 us
    pallas_call x4, Pallas kernels, call(): pl.pallas_call(kernel, name=name, out_shape=outs, in_specs=[SMEM] * scala...  17.1 us
    ppermute x17, waiting for transfers between devices, swap(): return lax.ppermute(x, axis, [(i, i ^ k) for i in range(n)])  15.1 us
  transfers between devices with their start and end apart: 17, of which 6 were waited for; matrix products, arithmetic and copies ran while one was open for 0% of the time, Pallas kernels for 17%

profile of v6, /device:TPU:0, one launch (start us, length us, event | category | flops | bytes accessed | tf_op | source)
XLA Modules:
  0.0 56.4 jit_solution(998825726867722057)
XLA Ops:
  0.6 1.8 %pack.1 = (bf16[128,512]{1,0:T(8,128)(2,1)S(1)}, bf16[32,4736]{1,0:T(8,128)(2,1)S(1)}, bf16[32,4736]{1,0:T(8,128)(2,1)S(1)}, bf16[32,4736]{1,0:T(8,128)(2,1)S(1)}, bf16[32,4736]{1,0:T(8,128)(2,1)S(1)}) custom-call(s32[1]{0:T(128)} %bitcast.2.me_ref, bf16[32,8192]{1,0:T(8,128)(2,1)} %q_ref.2, bf16[32,8192]{1,0:T(8,128)(2,1)} %do_ref.2, ...), custom_call_target="tpu_custom_call" | custom-call | tf_op jit(solution)/shard_map/pack/pallas_call | solution.py:300
  2.5 0.5 collective-permute-start
  3.0 2.6 %collective-permute-start.1 = (bf16[128,512]{1,0:T(8,128)(2,1)S(1)}, bf16[128,512]{1,0:T(8,128)(2,1)S(1)}, u32[]{:S(2)}, u32[]{:S(2)}) collective-permute-start(bf16[128,512]{1,0:T(8,128)(2,1)S(1)} %get-tuple-element.26.rest_0_.rest_4_), channel_id=1, source_target_pairs={{0,8},{4,12},{8,0},{12,4},{16,24},{20,28},{24,16},{28,20},{1,9},{5... | collective-permute-start | bytes 393224 | tf_op jit(solution)/shard_map/ppermute | solution.py:323
  5.5 0.1 collective-permute-start.2
  5.6 2.8 %collective-permute-start.7 = (bf16[32,4736]{1,0:T(8,128)(2,1)S(1)}, bf16[32,4736]{1,0:T(8,128)(2,1)S(1)}, u32[]{:S(2)}, u32[]{:S(2)}) collective-permute-start(bf16[32,4736]{1,0:T(8,128)(2,1)S(1)} %get-tuple-element.28), channel_id=1, source_target_pairs={{0,2},{1,3},{2,0},{3,1},{4,6},{5,7},{6,4},{7,5},{8,10},{9,11},{10,... | collective-permute-start | bytes 909320 | tf_op jit(solution)/shard_map/ppermute | solution.py:323
  8.4 1.6 %collective-permute-start.8 = (bf16[32,4736]{1,0:T(8,128)(2,1)S(1)}, bf16[32,4736]{1,0:T(8,128)(2,1)S(1)}, u32[]{:S(2)}, u32[]{:S(2)}) collective-permute-start(bf16[32,4736]{1,0:T(8,128)(2,1)S(1)} %get-tuple-element.29), channel_id=1, source_target_pairs={{0,1},{1,0},{2,3},{3,2},{4,5},{5,4},{6,7},{7,6},{8,9},{9,8},{10,11... | collective-permute-start | bytes 909320 | tf_op jit(solution)/shard_map/ppermute | solution.py:323
  10.0 0.0 collective-permute-done.rest_1_.rest_5_
  10.0 0.0 collective-permute-start.9
  10.0 0.0 collective-permute-done.1.rest_2_.rest_6_
  10.0 1.8 %collective-permute-start.3 = (bf16[128,512]{1,0:T(8,128)(2,1)S(1)}, bf16[128,512]{1,0:T(8,128)(2,1)S(1)}, u32[]{:S(2)}, u32[]{:S(2)}) collective-permute-start(bf16[128,512]{1,0:T(8,128)(2,1)S(1)} %get-tuple-element.26.rest_0_.rest_4_), channel_id=1, source_target_pairs={{0,16},{4,20},{8,24},{12,28},{16,0},{20,4},{24,8},{28,12},{1,17},{... | collective-permute-start | bytes 393224 | tf_op jit(solution)/shard_map/ppermute | solution.py:323
  11.9 0.3 collective-permute-done.2.rest_3_.rest_7_
  12.2 2.5 %collective-permute-start.5 = (bf16[128,512]{1,0:T(8,128)(2,1)S(1)}, bf16[128,512]{1,0:T(8,128)(2,1)S(1)}, u32[]{:S(2)}, u32[]{:S(2)}) collective-permute-start(bf16[128,512]{1,0:T(8,128)(2,1)S(1)} %get-tuple-element.26.rest_0_.rest_4_), channel_id=1, source_target_pairs={{0,24},{4,28},{8,16},{12,20},{16,8},{20,12},{24,0},{28,4},{1,25},{... | collective-permute-start | bytes 393224 | tf_op jit(solution)/shard_map/ppermute | solution.py:323
  14.7 0.6 %collective-permute-done.3.rest_4_.rest_8_ = bf16[128,512]{1,0:T(8,128)(2,1)S(1)} collective-permute-done((bf16[128,512]{1,0:T(8,128)(2,1)S(1)}, bf16[128,512]{1,0:T(8,128)(2,1)S(1)}, u32[]{:S(2)}, u32[]{:S(2)}) %collective-permute-start.3) | collective-permute-done | bytes 131104 | tf_op jit(solution)/shard_map/ppermute | solution.py:323
  15.3 0.0 collective-permute-start.4
  15.3 3.7 %collective-permute-done.5.rest_6_.rest_10_ = bf16[128,512]{1,0:T(8,128)(2,1)S(1)} collective-permute-done((bf16[128,512]{1,0:T(8,128)(2,1)S(1)}, bf16[128,512]{1,0:T(8,128)(2,1)S(1)}, u32[]{:S(2)}, u32[]{:S(2)}) %collective-permute-start.5) | collective-permute-done | bytes 131104 | tf_op jit(solution)/shard_map/ppermute | solution.py:323
  19.0 0.0 collective-permute-start.6
  19.0 2.7 %collective-permute-done.4.rest_5_.rest_9_ = bf16[128,512]{1,0:T(8,128)(2,1)S(1)} collective-permute-done((bf16[128,512]{1,0:T(8,128)(2,1)S(1)}, bf16[128,512]{1,0:T(8,128)(2,1)S(1)}, u32[]{:S(2)}, u32[]{:S(2)}) %collective-permute-start.4) | collective-permute-done | bytes 131104 | tf_op jit(solution)/shard_map/ppermute | solution.py:323
  21.7 0.0 collective-permute-done.6.rest_7_.rest_11_
  21.7 9.4 %prompt_grads.1 = (bf16[128,2048]{1,0:T(8,128)(2,1)}, f32[8,128,512]{2,1,0:T(8,128)S(1)}, f32[2,128,256]{2,1,0:T(8,128)S(1)}) custom-call(s32[1]{0:T(128)} %bitcast.me_ref, bf16[128,2048]{1,0:T(8,128)(2,1)} %q_ref.3, bf16[128,2048]{1,0:T(8,128)(2,1)} %do_ref.3, bf16[128,2048]{1,0:T(8,128)(2,1)} %o_ref.3, bf16[16,128]{1,0:T(8,128)(2,1)} %bitcast.11, ...), custom_call_target="tpu_custom_call" | custom-call | tf_op jit(solution)/shard_map/prompt_grads/pallas_call | solution.py:300
  31.1 0.0 collective-permute-done.7.rest_1_
  31.1 0.0 collective-permute-done.8.rest_2_
  31.1 0.0 collective-permute-done.9.rest_3_
  31.1 5.0 %roll_grads.1 = (f32[4,128,512]{2,1,0:T(8,128)S(1)}, bf16[4,128,512]{2,1,0:T(8,128)(2,1)S(1)}, bf16[32,2560]{1,0:T(8,128)(2,1)S(1)}, bf16[32,2560]{1,0:T(8,128)(...) custom-call(s32[1]{0:T(128)} %bitcast.2.me_ref, ...), custom_call_target="tpu_custom_call" | custom-call | tf_op jit(solution)/shard_map/roll_grads/pallas_call | solution.py:300
  36.1 0.2 collective-permute-start.10
  36.3 3.8 %collective-permute-start.14 = (bf16[32,2560]{1,0:T(8,128)(2,1)S(1)}, bf16[32,2560]{1,0:T(8,128)(2,1)S(1)}, u32[]{:S(2)}, u32[]{:S(2)}) collective-permute-start(bf16[32,2560]{1,0:T(8,128)(2,1)S(1)} %get-tuple-element.36), channel_id=1, source_target_pairs={{0,3},{1,2},{2,1},{3,0},{4,7},{5,6},{6,5},{7,4},{8,11},{9,10},{10,... | collective-permute-start | bytes 491528 | tf_op jit(solution)/shard_map/ppermute | solution.py:323
  40.1 3.9 %collective-permute-start.15 = (bf16[32,2560]{1,0:T(8,128)(2,1)S(1)}, bf16[32,2560]{1,0:T(8,128)(2,1)S(1)}, u32[]{:S(2)}, u32[]{:S(2)}) collective-permute-start(bf16[32,2560]{1,0:T(8,128)(2,1)S(1)} %get-tuple-element.37), channel_id=1, source_target_pairs={{0,1},{1,0},{2,3},{3,2},{4,5},{5,4},{6,7},{7,6},{8,9},{9,8},{10,11... | collective-permute-start | bytes 491528 | tf_op jit(solution)/shard_map/ppermute | solution.py:323
  44.0 0.0 collective-permute-start.16
  44.0 0.0 collective-permute-done.10
  44.0 0.2 fusion.2
  44.1 2.5 %collective-permute-start.11 = (bf16[128,512]{1,0:T(8,128)(2,1)S(1)}, bf16[128,512]{1,0:T(8,128)(2,1)S(1)}, u32[]{:S(2)}, u32[]{:S(2)}) collective-permute-start(bf16[128,512]{1,0:T(8,128)(2,1)S(1)} %get-tuple-element.46), channel_id=1, source_target_pairs={{0,24},{4,28},{8,16},{12,20},{16,8},{20,12},{24,0},{28,4},{1,25},{... | collective-permute-start | bytes 393224 | tf_op jit(solution)/shard_map/ppermute | solution.py:323
  46.7 0.5 collective-permute-start.12
  47.2 0.0 collective-permute-done.14.rest_5_
  47.2 0.5 collective-permute-start.13
  47.7 1.4 %collective-permute-done.15.rest_6_ = bf16[32,2560]{1,0:T(8,128)(2,1)S(1)} collective-permute-done((bf16[32,2560]{1,0:T(8,128)(2,1)S(1)}, bf16[32,2560]{1,0:T(8,128)(2,1)S(1)}, u32[]{:S(2)}, u32[]{:S(2)}) %collective-permute-start.15) | collective-permute-done | bytes 163872 | tf_op jit(solution)/shard_map/ppermute | solution.py:323
  49.1 6.3 %collective-permute-done.16.rest_7_ = bf16[32,2560]{1,0:T(8,128)(2,1)S(1)} collective-permute-done((bf16[32,2560]{1,0:T(8,128)(2,1)S(1)}, bf16[32,2560]{1,0:T(8,128)(2,1)S(1)}, u32[]{:S(2)}, u32[]{:S(2)}) %collective-permute-start.16) | collective-permute-done | bytes 163872 | tf_op jit(solution)/shard_map/ppermute | solution.py:323
  55.4 0.0 collective-permute-done.11.rest_1_
  55.4 0.0 collective-permute-done.12.rest_2_
  55.4 0.0 collective-permute-done.13.rest_3_
  55.4 0.9 %unpack.1 = (bf16[128,256]{1,0:T(8,128)(2,1)}, bf16[128,256]{1,0:T(8,128)(2,1)}, bf16[32,8192]{1,0:T(8,128)(2,1)}, bf16[32,1024]{1,0:T(8,128)(2,1)}, bf16[32,1024]{1,0:T(8,128)(2,1)}) custom-call(s32[1]{0:T(128)} %bitcast.2.me_ref, f32[128,512]{1,0:T(8,128)S(1)} %get-tuple-element.47.rest_0_, bf16[128,512]{1,0:T(8,128)(2,1)S(1)} %collective-permute-done.11.rest_1_, ...), custom_call_target="tpu_custom_call" | custom-call | tf_op jit(solution)/shard_map/unpack/pallas_call | solution.py:300
Async XLA Ops:
  2.5 7.6 %collective-permute-start = (bf16[128,512]{1,0:T(8,128)(2,1)S(1)}, bf16[128,512]{1,0:T(8,128)(2,1)S(1)}, u32[]{:S(2)}, u32[]{:S(2)}) collective-permute-start(bf16[128,512]{1,0:T(8,128)(2,1)S(1)} %get-tuple-element.26.rest_0_.rest_4_), channel_id=1, source_target_pairs={{0,4},{4,0},{8,12},{12,8},{16,20},{20,16},{24,28},{28,24},{1,5},{5... | collective-permute-start | bytes 393224 | tf_op jit(solution)/shard_map/ppermute | solution.py:323
  3.0 7.0 %collective-permute-start.1 = (bf16[128,512]{1,0:T(8,128)(2,1)S(1)}, bf16[128,512]{1,0:T(8,128)(2,1)S(1)}, u32[]{:S(2)}, u32[]{:S(2)}) collective-permute-start(bf16[128,512]{1,0:T(8,128)(2,1)S(1)} %get-tuple-element.26.rest_0_.rest_4_), channel_id=1, source_target_pairs={{0,8},{4,12},{8,0},{12,4},{16,24},{20,28},{24,16},{28,20},{1,9},{5... | collective-permute-start | bytes 393224 | tf_op jit(solution)/shard_map/ppermute | solution.py:323
  5.5 6.6 %collective-permute-start.2 = (bf16[128,512]{1,0:T(8,128)(2,1)S(1)}, bf16[128,512]{1,0:T(8,128)(2,1)S(1)}, u32[]{:S(2)}, u32[]{:S(2)}) collective-permute-start(bf16[128,512]{1,0:T(8,128)(2,1)S(1)} %get-tuple-element.26.rest_0_.rest_4_), channel_id=1, source_target_pairs={{0,12},{4,8},{8,4},{12,0},{16,28},{20,24},{24,20},{28,16},{1,13},{... | collective-permute-start | bytes 393224 | tf_op jit(solution)/shard_map/ppermute | solution.py:323
  5.6 25.5 %collective-permute-start.7 = (bf16[32,4736]{1,0:T(8,128)(2,1)S(1)}, bf16[32,4736]{1,0:T(8,128)(2,1)S(1)}, u32[]{:S(2)}, u32[]{:S(2)}) collective-permute-start(bf16[32,4736]{1,0:T(8,128)(2,1)S(1)} %get-tuple-element.28), channel_id=1, source_target_pairs={{0,2},{1,3},{2,0},{3,1},{4,6},{5,7},{6,4},{7,5},{8,10},{9,11},{10,... | collective-permute-start | bytes 909320 | tf_op jit(solution)/shard_map/ppermute | solution.py:323
  8.4 22.7 %collective-permute-start.8 = (bf16[32,4736]{1,0:T(8,128)(2,1)S(1)}, bf16[32,4736]{1,0:T(8,128)(2,1)S(1)}, u32[]{:S(2)}, u32[]{:S(2)}) collective-permute-start(bf16[32,4736]{1,0:T(8,128)(2,1)S(1)} %get-tuple-element.29), channel_id=1, source_target_pairs={{0,1},{1,0},{2,3},{3,2},{4,5},{5,4},{6,7},{7,6},{8,9},{9,8},{10,11... | collective-permute-start | bytes 909320 | tf_op jit(solution)/shard_map/ppermute | solution.py:323
  10.0 21.1 %collective-permute-start.9 = (bf16[32,4736]{1,0:T(8,128)(2,1)S(1)}, bf16[32,4736]{1,0:T(8,128)(2,1)S(1)}, u32[]{:S(2)}, u32[]{:S(2)}) collective-permute-start(bf16[32,4736]{1,0:T(8,128)(2,1)S(1)} %get-tuple-element.30), channel_id=1, source_target_pairs={{0,3},{1,2},{2,1},{3,0},{4,7},{5,6},{6,5},{7,4},{8,11},{9,10},{10,... | collective-permute-start | bytes 909320 | tf_op jit(solution)/shard_map/ppermute | solution.py:323
  10.0 5.3 %collective-permute-start.3 = (bf16[128,512]{1,0:T(8,128)(2,1)S(1)}, bf16[128,512]{1,0:T(8,128)(2,1)S(1)}, u32[]{:S(2)}, u32[]{:S(2)}) collective-permute-start(bf16[128,512]{1,0:T(8,128)(2,1)S(1)} %get-tuple-element.26.rest_0_.rest_4_), channel_id=1, source_target_pairs={{0,16},{4,20},{8,24},{12,28},{16,0},{20,4},{24,8},{28,12},{1,17},{... | collective-permute-start | bytes 393224 | tf_op jit(solution)/shard_map/ppermute | solution.py:323
  12.2 6.8 %collective-permute-start.5 = (bf16[128,512]{1,0:T(8,128)(2,1)S(1)}, bf16[128,512]{1,0:T(8,128)(2,1)S(1)}, u32[]{:S(2)}, u32[]{:S(2)}) collective-permute-start(bf16[128,512]{1,0:T(8,128)(2,1)S(1)} %get-tuple-element.26.rest_0_.rest_4_), channel_id=1, source_target_pairs={{0,24},{4,28},{8,16},{12,20},{16,8},{20,12},{24,0},{28,4},{1,25},{... | collective-permute-start | bytes 393224 | tf_op jit(solution)/shard_map/ppermute | solution.py:323
  15.3 6.5 %collective-permute-start.4 = (bf16[128,512]{1,0:T(8,128)(2,1)S(1)}, bf16[128,512]{1,0:T(8,128)(2,1)S(1)}, u32[]{:S(2)}, u32[]{:S(2)}) collective-permute-start(bf16[128,512]{1,0:T(8,128)(2,1)S(1)} %get-tuple-element.26.rest_0_.rest_4_), channel_id=1, source_target_pairs={{0,20},{4,16},{8,28},{12,24},{16,4},{20,0},{24,12},{28,8},{1,21},{... | collective-permute-start | bytes 393224 | tf_op jit(solution)/shard_map/ppermute | solution.py:323
  19.0 2.7 %collective-permute-start.6 = (bf16[128,512]{1,0:T(8,128)(2,1)S(1)}, bf16[128,512]{1,0:T(8,128)(2,1)S(1)}, u32[]{:S(2)}, u32[]{:S(2)}) collective-permute-start(bf16[128,512]{1,0:T(8,128)(2,1)S(1)} %collective-permute-done.5.rest_6_.rest_10_), channel_id=1, source_target_pairs={{0,4},{4,0},{8,12},{12,8},{16,20},{20,16},{24,28},{28,24},{1,5},{5... | collective-permute-start | bytes 393224 | tf_op jit(solution)/shard_map/ppermute | solution.py:323
  36.1 7.8 %collective-permute-start.10 = (bf16[4,128,512]{2,1,0:T(8,128)(2,1)S(1)}, bf16[4,128,512]{2,1,0:T(8,128)(2,1)S(1)}, u32[]{:S(2)}, u32[]{:S(2)}) collective-permute-start(bf16[4,128,512]{2,1,0:T(8,128)(2,1)S(1)} %get-tuple-element.34), channel_id=1, source_target_pairs={{0,4},{4,0},{8,12},{12,8},{16,20},{20,16},{24,28},{28,24},{1,5},{5... | collective-permute-start | bytes 1572872 | tf_op jit(solution)/shard_map/ppermute | solution.py:323
  36.3 10.9 %collective-permute-start.14 = (bf16[32,2560]{1,0:T(8,128)(2,1)S(1)}, bf16[32,2560]{1,0:T(8,128)(2,1)S(1)}, u32[]{:S(2)}, u32[]{:S(2)}) collective-permute-start(bf16[32,2560]{1,0:T(8,128)(2,1)S(1)} %get-tuple-element.36), channel_id=1, source_target_pairs={{0,3},{1,2},{2,1},{3,0},{4,7},{5,6},{6,5},{7,4},{8,11},{9,10},{10,... | collective-permute-start | bytes 491528 | tf_op jit(solution)/shard_map/ppermute | solution.py:323
  40.1 9.0 %collective-permute-start.15 = (bf16[32,2560]{1,0:T(8,128)(2,1)S(1)}, bf16[32,2560]{1,0:T(8,128)(2,1)S(1)}, u32[]{:S(2)}, u32[]{:S(2)}) collective-permute-start(bf16[32,2560]{1,0:T(8,128)(2,1)S(1)} %get-tuple-element.37), channel_id=1, source_target_pairs={{0,1},{1,0},{2,3},{3,2},{4,5},{5,4},{6,7},{7,6},{8,9},{9,8},{10,11... | collective-permute-start | bytes 491528 | tf_op jit(solution)/shard_map/ppermute | solution.py:323
  44.0 11.4 %collective-permute-start.16 = (bf16[32,2560]{1,0:T(8,128)(2,1)S(1)}, bf16[32,2560]{1,0:T(8,128)(2,1)S(1)}, u32[]{:S(2)}, u32[]{:S(2)}) collective-permute-start(bf16[32,2560]{1,0:T(8,128)(2,1)S(1)} %get-tuple-element.38), channel_id=1, source_target_pairs={{0,2},{1,3},{2,0},{3,1},{4,6},{5,7},{6,4},{7,5},{8,10},{9,11},{10,... | collective-permute-start | bytes 491528 | tf_op jit(solution)/shard_map/ppermute | solution.py:323
  44.1 11.3 %collective-permute-start.11 = (bf16[128,512]{1,0:T(8,128)(2,1)S(1)}, bf16[128,512]{1,0:T(8,128)(2,1)S(1)}, u32[]{:S(2)}, u32[]{:S(2)}) collective-permute-start(bf16[128,512]{1,0:T(8,128)(2,1)S(1)} %get-tuple-element.46), channel_id=1, source_target_pairs={{0,24},{4,28},{8,16},{12,20},{16,8},{20,12},{24,0},{28,4},{1,25},{... | collective-permute-start | bytes 393224 | tf_op jit(solution)/shard_map/ppermute | solution.py:323
  46.7 8.8 %collective-permute-start.12 = (bf16[128,512]{1,0:T(8,128)(2,1)S(1)}, bf16[128,512]{1,0:T(8,128)(2,1)S(1)}, u32[]{:S(2)}, u32[]{:S(2)}) collective-permute-start(bf16[128,512]{1,0:T(8,128)(2,1)S(1)} %get-tuple-element.45), channel_id=1, source_target_pairs={{0,16},{4,20},{8,24},{12,28},{16,0},{20,4},{24,8},{28,12},{1,17},{... | collective-permute-start | bytes 393224 | tf_op jit(solution)/shard_map/ppermute | solution.py:323
  47.2 8.2 %collective-permute-start.13 = (bf16[128,512]{1,0:T(8,128)(2,1)S(1)}, bf16[128,512]{1,0:T(8,128)(2,1)S(1)}, u32[]{:S(2)}, u32[]{:S(2)}) collective-permute-start(bf16[128,512]{1,0:T(8,128)(2,1)S(1)} %get-tuple-element.44), channel_id=1, source_target_pairs={{0,8},{4,12},{8,0},{12,4},{16,24},{20,28},{24,16},{28,20},{1,9},{5... | collective-permute-start | bytes 393224 | tf_op jit(solution)/shard_map/ppermute | solution.py:323
